TPU v7x, 32 devices: a whole 2x2x4 slice. The times are simulated.
32 devices in a mesh: groups: 2 (over y), expert: 16 (over z, x, core).
Axes of the slice: x: 2, y: 2, z: 4, core: 2. Of those that a mesh axis runs over, the one named last changes fastest.
Arguments:
- tokens: bfloat16 [256, 3584], P(('groups', 'expert')), parts along dimension 0
- moe_gain: float32 [3584], replicated, may hold values from 0.1 to 1.9
- expert_ids: int32 [256, 2], P(('groups', 'expert')), parts along dimension 0, may hold values from 0 to 1, all different within a row; in each aligned block of 8 rows (0 to 7, 8 to 15, ...) at most 8 rows name the same one
- gate_scores: float32 [256, 2], P(('groups', 'expert')), parts along dimension 0, may hold values from 0.05 to 1
- w_gate: bfloat16 [16, 3584, 256], P('expert'), may hold values from -0.09375 to 0.09375
- w_up: bfloat16 [16, 3584, 256], P('expert'), may hold values from -0.09375 to 0.09375
- w_down: bfloat16 [16, 256, 3584], P('expert'), may hold values from -0.125 to 0.125
- final_gain: float32 [3584], replicated, may hold values from 0.1 to 1.9
- teacher_head: bfloat16 [3584, 4096], P(None, 'expert')
- vocab_map: int32 [4096], P('expert'), may hold values from 0 to 255, as said below
- student_logits: bfloat16 [256, 4096], P('groups', 'expert'), parts along dimension 0, may hold values from -16 to 160
- student_head: bfloat16 [2048, 4096], P(None, 'expert'), may hold values from -6 to 6
Outputs:
- divergence: float32 [256], P(('groups', 'expert')), parts along dimension 0
- grad_hidden: float32 [256, 2048], P(('groups', 'expert')), parts along dimension 0
There are 2 independent parts, one for each index of `groups`. A program takes and returns all parts, laid end to end along the dimension named above; an argument that names none is the same for every part. Nothing has to cross between parts.
Inputs may be any that keep to these rules, and one draw needn't show every extreme that they name: `expert_ids`: each row names 2 different experts; the rows of one device name any one expert at most 8 times, a bound that some block reaches. `vocab_map`: each aligned block of 256 entries holds every number of 0 to 255 once.
All inputs are finite; a program needn't handle non-finite values.
Results may differ from a plain program's by a relative error of at most 0.015.
Values may be sent and summed in bfloat16 or wider, within the bound.
No kernel may reach another device: no remote copies, remote signals or barrier semaphores. Data moves between devices by JAX's collectives and lax.ppermute only.
A program may use at most 128 MiB of HBM per device.

v0:
```python
import jax
import jax.numpy as jnp
from jax import lax
from jax.sharding import PartitionSpec as P

FF = 2048


EPSILON = 1e-06


def merged(part, axis, combine):
    gathered = jax.tree.map(lambda a: lax.all_gather(a, axis), part)

    def take(source):
        return jax.tree.map(lambda a: lax.dynamic_index_in_dim(a, source, 0, False), gathered)

    return lax.fori_loop(
        1, lax.axis_size(axis), lambda source, state: combine(state, take(source)), take(0)
    )


def rms_norm(values, gain):
    return values * lax.rsqrt(jnp.mean(values * values, axis=-1, keepdims=True) + EPSILON) * gain


def combine_parts(first_part, second_part):
    teach_max = jnp.maximum(first_part[0], second_part[0])
    first_teach = jnp.exp(first_part[0] - teach_max)
    second_teach = jnp.exp(second_part[0] - teach_max)
    teach_sum = first_part[1] * first_teach + second_part[1] * second_teach
    cross_sum = first_part[2] * first_teach + second_part[2] * second_teach
    stud_max = jnp.maximum(first_part[3], second_part[3])
    stud_sum = first_part[4] * jnp.exp(first_part[3] - stud_max) + second_part[4] * jnp.exp(
        second_part[3] - stud_max
    )
    return (teach_max, teach_sum, cross_sum, stud_max, stud_sum)


def per_device(
    tokens,
    moe_gain,
    expert_ids,
    gate_scores,
    w_gate,
    w_up,
    w_down,
    final_gain,
    teacher_head,
    vocab_map,
    student_logits,
    student_head,
):
    devices = lax.axis_size("expert")
    my_index = lax.axis_index("expert")
    tok_dev = tokens.shape[0]
    features = tokens.shape[1]
    route_count = expert_ids.shape[1]
    slices = FF // w_gate.shape[2]
    experts = devices // slices
    capacity = min(tok_dev, slices * max(1, 2 * tok_dev * route_count // (experts * slices)))
    routes = tok_dev * route_count
    floats = tokens.astype(jnp.float32)
    normed = rms_norm(floats, moe_gain).astype(jnp.bfloat16)
    weights = gate_scores / jnp.sum(gate_scores, axis=1, keepdims=True)
    flat_ids = expert_ids.reshape(-1)
    matches = (flat_ids[:, None] == jnp.arange(experts, dtype=jnp.int32)[None, :]).astype(jnp.int32)
    slot_rank = jnp.sum((jnp.cumsum(matches, axis=0) - 1) * matches, axis=1)
    places = flat_ids * capacity + slot_rank
    chosen = places[:, None] == jnp.arange(experts * capacity, dtype=jnp.int32)[None, :]
    owners = (
        jnp.arange(routes, dtype=jnp.int32)[:, None] // route_count
        == jnp.arange(tok_dev, dtype=jnp.int32)[None, :]
    )
    repeated = jnp.repeat(normed, route_count, axis=0)
    outgoing = jnp.dot(chosen.T.astype(jnp.bfloat16), repeated, preferred_element_type=jnp.float32)
    outgoing = outgoing.astype(jnp.bfloat16).reshape(experts, capacity, features)
    weighted_owner = owners.astype(jnp.float32) * weights.reshape(-1)[:, None]
    mixing = jnp.dot(weighted_owner.T, chosen.astype(jnp.float32), precision=lax.Precision.HIGHEST)
    copies = jnp.broadcast_to(outgoing[:, None], (experts, slices, capacity, features)).reshape(
        devices, capacity, features
    )
    arrived_rows = lax.all_to_all(copies, "expert", split_axis=0, concat_axis=0, tiled=True)
    count = arrived_rows.shape[1]
    flat_rows = arrived_rows.reshape(-1, features)
    gate_out = jnp.dot(flat_rows, w_gate[0], preferred_element_type=jnp.float32)
    up_out = jnp.dot(flat_rows, w_up[0], preferred_element_type=jnp.float32)
    activated = (jax.nn.silu(gate_out) * up_out).astype(jnp.bfloat16)
    partial_value = jnp.dot(activated, w_down[0], preferred_element_type=jnp.float32).astype(
        jnp.bfloat16
    )
    send_partial_value = partial_value.reshape(devices, count, features)
    returned = lax.all_to_all(send_partial_value, "expert", split_axis=0, concat_axis=0, tiled=True)
    summed = returned.reshape(experts, slices, capacity, features).astype(jnp.float32).sum(axis=1)
    summed = summed.reshape(experts * capacity, features)
    moe = jnp.dot(mixing, summed, precision=lax.Precision.HIGHEST)
    hidden = floats + moe
    final_norm = rms_norm(hidden, final_gain).astype(jnp.bfloat16)
    mapped_head = jnp.take(teacher_head, vocab_map, axis=1)
    teacher = jnp.dot(
        lax.all_gather(final_norm, "expert", axis=0, tiled=True),
        mapped_head,
        preferred_element_type=jnp.float32,
    )
    student = student_logits.astype(jnp.float32)
    local_teach = jnp.max(teacher, axis=1)
    local_exp = jnp.exp(teacher - local_teach[:, None])
    local_stud = jnp.max(student, axis=1)
    teach_max, teach_sum, cross_sum, stud_max, stud_sum = merged(
        (
            local_teach,
            jnp.sum(local_exp, axis=1),
            jnp.sum(local_exp * (teacher - student), axis=1),
            local_stud,
            jnp.sum(jnp.exp(student - local_stud[:, None]), axis=1),
        ),
        "expert",
        combine_parts,
    )
    teach_exp = jnp.exp(teacher - teach_max[:, None])
    divergence_all = (
        cross_sum / teach_sum - teach_max - jnp.log(teach_sum) + stud_max + jnp.log(stud_sum)
    )
    logit_grad = (
        jnp.exp(student - stud_max[:, None]) / stud_sum[:, None] - teach_exp / teach_sum[:, None]
    ).astype(jnp.bfloat16)
    divergence = lax.dynamic_slice_in_dim(divergence_all, my_index * tok_dev, tok_dev)
    grad_hidden = lax.psum_scatter(
        lax.dot_general(
            logit_grad, student_head, (((1,), (1,)), ((), ())), preferred_element_type=jnp.float32
        ),
        "expert",
        scatter_dimension=0,
        tiled=True,
    )
    return (divergence, grad_hidden)


def solution(mesh):
    placed = (
        P(("groups", "expert"), None),
        P(),
        P(("groups", "expert"), None),
        P(("groups", "expert"), None),
        P("expert", None, None),
        P("expert", None, None),
        P("expert", None, None),
        P(),
        P(None, "expert"),
        P("expert"),
        P("groups", "expert"),
        P(None, "expert"),
    )
    return jax.shard_map(
        per_device,
        mesh=mesh,
        in_specs=placed,
        out_specs=(P(("groups", "expert")), P(("groups", "expert"), None)),
        check_vma=False,
    )
```

profile of v0, /device:TPU:0, one launch (start us, length us, event | category | flops | bytes accessed | tf_op | source)
XLA Modules:
  0.0 242.4 jit_solution(3355588829982536830)
XLA Ops:
  7.2 0.0 copy-start
  7.2 0.9 copy.21
  8.1 0.1 reshape.114
  8.1 0.1 fusion.62
  8.3 0.2 select_reduce_fusion
  8.5 1.0 fusion.51
  9.4 0.9 fusion.53
  10.3 0.1 broadcast_in_dim.15
  10.5 0.0 copy-start.2
  10.5 0.3 fusion.14
  10.8 0.1 broadcast_in_dim.20
  10.8 29.8 %all_to_all.10 = bf16[16,8,3584]{2,1,0:T(8,128)(2,1)S(1)} all-to-all(bf16[16,8,3584]{2,1,0:T(8,128)(2,1)S(1)} %bitcast.98), channel_id=1, replica_groups=mesh['groups'=2,'expert'=16] {'expert'}, dimensions={0} | all-to-all | bytes 1835008 | tf_op jit(solution)/shard_map/all_to_all | solution.py:83
  40.7 0.0 copy-done.2
  40.7 0.4 fusion.18
  41.1 0.0 copy-done
  41.1 3.6 %fusion.13 = bf16[16,8,3584]{2,1,0:T(8,128)(2,1)} fusion(bf16[1,256,3584]{2,1,0:T(8,128)(2,1)S(1)} %copy-done, bf16[1,3584,256]{2,1,0:T(8,128)(2,1)} %param.19, bf16[16,8,3584]{2,1,0:T(8,128)(2,1)S(1)} %all_to_all.10, f32[128,256]{1,0:T(8,128)S(1)} %fusion.18), kind=kOutput, calls=%fused_computation.22 | convolution fusion | flops 470417408 | bytes 5636096 | tf_op jit(solution)/shard_map/dot_general | solution.py:89
  44.7 0.0 copy-start.7
  44.7 4.6 %all-to-all-start.1 = ((bf16[16,8,3584]{2,1,0:T(8,128)(2,1)}), bf16[16,8,3584]{2,1,0:T(8,128)(2,1)S(1)}, u32[]{:S(2)}, u32[]{:S(2)}) async-start(bf16[16,8,3584]{2,1,0:T(8,128)(2,1)} %fusion.13), calls=%async_computation.1 | async-start | bytes 1835008 | tf_op jit(solution)/shard_map/all_to_all | solution.py:93
  49.3 0.0 reduce-scatter.2.cloned.1.call-start
  49.4 0.0 copy-done.7
  49.4 0.1 copy.20
  49.5 0.1 mul.131
  49.6 0.0 copy-start.8
  49.6 3.9 %copy.22 = bf16[3584,256]{0,1:T(8,128)(2,1)} copy(bf16[3584,256]{1,0:T(8,128)(2,1)} %param.22) | data formatting | bytes 3670016 | tf_op args[8]
  53.5 0.0 copy-done.8
  53.5 0.0 copy-start.4
  53.6 0.0 copy-start.5
  53.6 6.6 %gather_fusion = bf16[256,3584]{1,0:T(8,128)(2,1)} fusion(bf16[3584,256]{0,1:T(8,128)(2,1)} %copy.22, s32[1024]{0:T(1024)S(1)} %pad_clamp_fusion), kind=kCustom, calls=%fused_computation | custom fusion | bytes 3671040 | tf_op jit(solution)/shard_map/jit(_take)/gather | solution.py:99
  60.1 0.0 copy-done.4
  60.1 0.0 copy-start.6
  60.1 0.1 reduce_max.28
  60.2 21.6 %all-gather.8 = f32[16,1,128]{2,1,0:T(1,128)S(1)} all-gather(f32[1,1,128]{2,1,0:T(1,128)S(1)} %get-tuple-element.305), channel_id=5, replica_groups=mesh['groups'=2,'expert'=16] {'expert'}, dimensions={0}, use_global_device_ids=true | all-gather | bytes 8704 | tf_op jit(solution)/shard_map/all_gather | solution.py:13
  81.9 0.3 fusion.61
  82.1 0.0 all-to-all-done.1
  82.1 0.0 copy-start.1
  82.1 0.1 convert_reduce_fusion
  82.3 0.0 copy-done.5
  82.3 0.4 multiply_reduce_fusion
  82.7 0.0 copy-done.6
  82.7 0.1 multiply_convert_fusion
  82.8 22.1 %all_gather.31 = bf16[128,3584]{1,0:T(8,128)(2,1)S(1)} all-gather(bf16[8,3584]{1,0:T(8,128)(2,1)S(1)} %multiply_convert_fusion), channel_id=1, replica_groups=mesh['groups'=2,'expert'=16] {'expert'}, dimensions={0}, use_global_device_ids=true | all-gather | bytes 974848 | tf_op jit(solution)/shard_map/all_gather | solution.py:101
  104.9 0.0 copy-done.1
  104.9 0.0 copy-start.3
  104.9 0.9 fusion.74
  105.8 0.2 fusion.38
  106.0 17.4 %all-gather.9 = f32[16,1,128]{2,1,0:T(1,128)S(1)} all-gather(f32[1,1,128]{2,1,0:T(1,128)S(1)} %bitcast.107), channel_id=6, replica_groups=mesh['groups'=2,'expert'=16] {'expert'}, dimensions={0}, use_global_device_ids=true | all-gather | bytes 8704 | tf_op jit(solution)/shard_map/all_gather | solution.py:13
  123.4 18.6 %all-gather.7 = f32[16,1,128]{2,1,0:T(1,128)S(1)} all-gather(f32[1,1,128]{2,1,0:T(1,128)S(1)} %bitcast.106), channel_id=4, replica_groups=mesh['groups'=2,'expert'=16] {'expert'}, dimensions={0}, use_global_device_ids=true | all-gather | bytes 8704 | tf_op jit(solution)/shard_map/all_gather | solution.py:13
  142.0 17.4 %all-gather.6 = f32[16,1,128]{2,1,0:T(1,128)S(1)} all-gather(f32[1,1,128]{2,1,0:T(1,128)S(1)} %bitcast.105), channel_id=3, replica_groups=mesh['groups'=2,'expert'=16] {'expert'}, dimensions={0}, use_global_device_ids=true | all-gather | bytes 8704 | tf_op jit(solution)/shard_map/all_gather | solution.py:13
  159.4 18.6 %all-gather.5 = f32[16,1,128]{2,1,0:T(1,128)S(1)} all-gather(f32[1,1,128]{2,1,0:T(1,128)S(1)} %bitcast.104), channel_id=2, replica_groups=mesh['groups'=2,'expert'=16] {'expert'}, dimensions={0}, use_global_device_ids=true | all-gather | bytes 8704 | tf_op jit(solution)/shard_map/all_gather | solution.py:13
  178.0 1.3 while.23
  179.3 0.0 copy-done.3
  179.3 1.5 fusion.54
  180.7 0.0 reduce-scatter.2.cloned.1.call-update
  180.8 0.6 dynamic_slice.74
  181.4 54.2 %reduce-scatter.2.cloned.1.call-done = f32[8,2048]{1,0:T(8,128)} async-done(((f32[128,2048]{1,0:T(8,128)}), f32[8,2048]{1,0:T(8,128)}) %reduce-scatter.2.cloned.1.call-update) | async-done | bytes 65552 | tf_op jit(solution)/shard_map/reduce_scatter | solution.py:128
  (63 shorter events, 1.0 us)
Async XLA Ops:
  7.2 33.9 %copy-start = (bf16[1,256,3584]{2,1,0:T(8,128)(2,1)S(1)}, bf16[1,256,3584]{2,1,0:T(8,128)(2,1)}, u32[]{:S(2)}) copy-start(bf16[1,256,3584]{2,1,0:T(8,128)(2,1)} %param.20) | copy-start | bytes 5505028
  10.5 30.2 %copy-start.2 = (bf16[1,3584,256]{2,1,0:T(8,128)(2,1)S(1)}, bf16[1,3584,256]{2,1,0:T(8,128)(2,1)}, u32[]{:S(2)}) copy-start(bf16[1,3584,256]{2,1,0:T(8,128)(2,1)} %param.18) | copy-start | bytes 5505028
  44.7 4.7 %copy-start.7 = (f32[8,2]{0,1:T(2,128)S(1)}, f32[8,2]{0,1:T(2,128)}, u32[]{:S(2)}) copy-start(f32[8,2]{0,1:T(2,128)} %param.17) | copy-start | bytes 196
  44.7 37.4 %all-to-all-start.1 = ((bf16[16,8,3584]{2,1,0:T(8,128)(2,1)}), bf16[16,8,3584]{2,1,0:T(8,128)(2,1)S(1)}, u32[]{:S(2)}, u32[]{:S(2)}) async-start(bf16[16,8,3584]{2,1,0:T(8,128)(2,1)} %fusion.13), calls=%async_computation.1 | async-start | bytes 1835008 | tf_op jit(solution)/shard_map/all_to_all | solution.py:93
  49.3 186.3 %reduce-scatter.2.cloned.1.call-start = ((), (), s32[]{:S(2)}) async-start(), calls=%async_computation.3 | async-start | bytes 1114112 | tf_op jit(solution)/shard_map/reduce_scatter | solution.py:128
  49.6 3.9 %copy-start.8 = (s32[256]{0:T(256)S(1)}, s32[256]{0:T(256)}, u32[]{:S(2)}) copy-start(s32[256]{0:T(256)} %param.23) | copy-start | bytes 3076
  53.5 6.6 %copy-start.4 = (bf16[128,256]{1,0:T(8,128)(2,1)S(1)}, bf16[128,256]{1,0:T(8,128)(2,1)}, u32[]{:S(2)}) copy-start(bf16[128,256]{1,0:T(8,128)(2,1)} %param.24) | copy-start | bytes 196612
  53.6 28.7 %copy-start.5 = (bf16[8,3584]{1,0:T(8,128)(2,1)S(1)}, bf16[8,3584]{1,0:T(8,128)(2,1)}, u32[]{:S(2)}) copy-start(bf16[8,3584]{1,0:T(8,128)(2,1)} %param.14) | copy-start | bytes 172036
  60.1 22.5 %copy-start.6 = (f32[3584]{0:T(1024)S(1)}, f32[3584]{0:T(1024)}, u32[]{:S(2)}) copy-start(f32[3584]{0:T(1024)} %param.21) | copy-start | bytes 43012
  82.1 22.8 %copy-start.1 = (bf16[256,3584]{1,0:T(8,128)(2,1)S(1)}, bf16[256,3584]{1,0:T(8,128)(2,1)}, u32[]{:S(2)}) copy-start(bf16[256,3584]{1,0:T(8,128)(2,1)} %gather_fusion) | copy-start | bytes 5505028
  104.9 74.4 %copy-start.3 = (bf16[2048,256]{1,0:T(8,128)(2,1)S(1)}, bf16[2048,256]{1,0:T(8,128)(2,1)}, u32[]{:S(2)}) copy-start(bf16[2048,256]{1,0:T(8,128)(2,1)} %param.25) | copy-start | bytes 3145732
Sparse Core Ops, SparseCore 0:
  180.9 54.6 reduce-scatter.1
where the time goes:
time: 243 us; the launch traced here: 242 us
  blocking collectives  146 us (60%)
  waiting for transfers between devices  54.2 us (22%)
  between operations  14.2 us (6%)
  local copies, waits for them, and re-layouts  12.5 us (5%)
  matrix products  7.27 us (3%)
  starting transfers between devices  4.65 us (2%)
  other arithmetic  3.65 us (2%)
    all_gather x5, blocking collectives, merged(): gathered = jax.tree.map(lambda a: lax.all_gather(a, axis), part)  93.6 us
    reduce_scatter x1, waiting for transfers between devices, per_device(): lax.psum_scatter(lax.dot_general(logit_grad, student_head, (((1,), (1,)),...  54.2 us
    all_to_all x1, blocking collectives, per_device(): lax.all_to_all(copies, 'expert', split_axis=0, concat_axis=0, tiled=True)  29.8 us
    all_gather x1, blocking collectives, per_device(): lax.all_gather(final_norm, 'expert', axis=0, tiled=True)  22.1 us
    gather x1, local copies, waits for them, and re-layouts, per_device(): mapped_head = jnp.take(teacher_head, vocab_map, axis=1)  6.55 us
  transfers between devices with their start and end apart: 2, of which 1 were waited for; matrix products, arithmetic and copies ran while one was open for 5% of the time, Pallas kernels for 0%

commit v1 on v0

v1 whole, which is shorter than its diff:
```python
import functools

import jax
import jax.numpy as jnp
from jax import lax
from jax.experimental import pallas as pl
from jax.experimental.pallas import tpu as pltpu
from jax.sharding import PartitionSpec as P

FF = 2048
EPSILON = 1e-06
F32 = jnp.float32
BF16 = jnp.bfloat16
BLOCK = 128


def radices(devices):
    bits = devices.bit_length() - 1
    x_bits = (bits - 1) // 3
    return 1 << (bits - 1 - x_bits), 1 << x_bits, 2


def dot(a, b):
    return jnp.dot(a, b, preferred_element_type=F32)


def dot_t(a, b):
    return lax.dot_general(a, b, (((1,), (1,)), ((), ())), preferred_element_type=F32)


def lanes(rows):
    return lax.broadcasted_iota(jnp.int32, (rows, BLOCK), 1)


def pack(columns):
    lane = lanes(columns[0].shape[0])
    block = jnp.zeros(lane.shape, F32)
    for j, column in enumerate(columns):
        block = jnp.where((lane % 32 == j) & (lane < 96), column, block)
    return block


def split(block):
    lane = lanes(block.shape[0])
    high = block.astype(BF16)
    rest = block - high.astype(F32)
    middle = rest.astype(BF16)
    low = (rest - middle.astype(F32)).astype(BF16).astype(F32)
    return jnp.where(lane < 32, high.astype(F32), jnp.where(lane < 64, middle.astype(F32), low)).astype(BF16)


def column(block, j, exact):
    lane = lanes(block.shape[0])
    keep = (lane == j) if exact else (lane % 32 == j)
    return jnp.sum(jnp.where(keep, block, 0.0), axis=1, keepdims=True)


def combine(parts, width):
    blocks = [(ref[:, width:].astype(F32), i == 0) for i, ref in enumerate(parts)]
    tops = [column(b, 0, own) for b, own in blocks]
    top = functools.reduce(jnp.maximum, tops)
    scales = [jnp.exp(t - top) for t in tops]
    totals = [sum(column(b, j, own) * s for (b, own), s in zip(blocks, scales)) for j in (1, 2)]
    values = sum(ref[:, :width].astype(F32) * s for ref, s in zip(parts, scales))
    return values, top, totals


def call(body, outs, *args, scratch=(), scalars=0):
    smem = pl.BlockSpec(memory_space=pltpu.SMEM)
    vmem = pl.BlockSpec(memory_space=pltpu.VMEM)
    return pl.pallas_call(
        body,
        out_shape=[jax.ShapeDtypeStruct(s, d) for s, d in outs],
        in_specs=[smem] * scalars + [vmem] * (len(args) - scalars),
        out_specs=[vmem] * len(outs),
        scratch_shapes=list(scratch),
        compiler_params=pltpu.CompilerParams(vmem_limit_bytes=56 * 2**20),
    )(*args)


def normed_rows(values, gain):
    return values * lax.rsqrt(jnp.mean(values * values, axis=-1, keepdims=True) + EPSILON) * gain


def enter_body(tokens, gain, ids, scores, out):
    rows, features = tokens.shape
    out[:, :features] = normed_rows(tokens[...].astype(F32), gain[...]).astype(BF16)
    diagonal = lax.broadcasted_iota(jnp.int32, (rows, rows), 0) == lax.broadcasted_iota(
        jnp.int32, (rows, rows), 1
    )
    lane = lanes(rows) % 64
    block = jnp.zeros(lane.shape, F32)
    total = jnp.zeros((rows, 1), F32)
    for k in range(ids.shape[0]):
        chosen = jnp.where(diagonal, ids[k : k + 1, :].astype(F32), 0.0)
        chosen = jnp.sum(chosen, axis=1, keepdims=True)
        score = jnp.where(diagonal, scores[k : k + 1, :], 0.0)
        score = jnp.sum(score, axis=1, keepdims=True)
        block = block + jnp.where(lane.astype(F32) == chosen, score, 0.0)
        total = total + score
    block = block / total
    high = block.astype(BF16).astype(F32)
    out[:, features:] = jnp.where(lanes(rows) < 64, high, block - high).astype(BF16)


def experts_body(slices, parts, me, *refs):
    inputs, (w_gate, w_up, w_down, send, keep, rows_ref) = refs[:parts], refs[parts:]
    count = inputs[0].shape[0]
    features = w_gate.shape[1]
    for i, ref in enumerate(inputs):
        rows_ref[i * count : (i + 1) * count, :] = ref[...]
    expert = me[0] // slices

    def block(start, size):
        rows = rows_ref[pl.ds(start, size), :features]
        gate = dot(rows, w_gate[0])
        up = dot(rows, w_up[0])
        lane = lanes(size) % 64
        table = rows_ref[pl.ds(start, size), features:].astype(F32)
        weight = jnp.sum(jnp.where(lane == expert, table, 0.0), axis=1, keepdims=True)
        activated = (gate / (1.0 + jnp.exp(-gate)) * up).astype(BF16)
        return activated, weight

    half = parts * count // 2
    if half < BLOCK:
        activated, weight = block(0, 2 * half)
        step = 512
        for at in range(0, features, step):
            out = dot(activated, w_down[0, :, at : at + step]) * weight
            keep[:, at : at + step] = out[:half]
            send[:, at : at + step] = out[half:].astype(BF16)
    else:
        for h, target in enumerate((keep, send)):

            @pl.loop(0, half // BLOCK)
            def _(i):
                start = pl.multiple_of(i * BLOCK, BLOCK)
                activated, weight = block(h * half + start, BLOCK)
                out = dot(activated, w_down[0]) * weight
                target[pl.ds(start, BLOCK), :] = out.astype(target.dtype)


def add_split_body(received, *refs):
    parts, (keep, *sends) = refs[: received + 1], refs[received + 1 :]
    total = sum((ref[...].astype(F32) for ref in parts[1:]), parts[0][...])
    rows = keep.shape[0]
    keep[...] = total[:rows]
    for i, send in enumerate(sends):
        send[...] = total[(i + 1) * rows : (i + 2) * rows].astype(BF16)


def hidden_body(received, *refs):
    parts, (tokens, gain, out) = refs[: received + 1], refs[received + 1 :]
    total = sum((ref[...].astype(F32) for ref in parts[1:]), parts[0][...])
    out[...] = normed_rows(tokens[...].astype(F32) + total, gain[...]).astype(BF16)


def student_body(me, devices, order, vocab_map, logits, head, moved, moved_head, send, keep, scratch):
    entries = logits.shape[1]
    tok_dev = logits.shape[0] // devices
    place = lax.broadcasted_iota(jnp.int32, (entries, entries), 0) == vocab_map[...]
    place = jnp.where(place, 1.0, 0.0).astype(BF16)
    scratch[...] = dot_t(logits[...], place)
    moved_head[...] = dot_t(head[...], place).astype(BF16)
    for slot, offset in enumerate(order):
        source = pl.multiple_of((me[0] ^ offset) * tok_dev, tok_dev)
        moved[slot * tok_dev : (slot + 1) * tok_dev, :] = scratch[pl.ds(source, tok_dev), :]
    half = keep.shape[0]
    width = moved_head.shape[0]
    step = min(half, BLOCK)
    for at in range(0, 2 * half, step):
        student = moved[at : at + step, :]
        top = jnp.max(student, axis=1, keepdims=True)
        exps = jnp.exp(student - top)
        total = jnp.sum(exps, axis=1, keepdims=True)
        emit(at, step, half, width, exps, moved_head, [top, total, jnp.zeros_like(top)], send, keep)


def emit(at, step, half, width, exps, head, columns, send, keep):
    stats = pack(columns)
    values = dot_t(exps.astype(BF16), head[...])
    for start, stop, target in ((0, half, keep), (half, 2 * half, send)):
        low, high = max(at, start), min(at + step, stop)
        if low < high:
            inner, outer = slice(low - at, high - at), slice(low - start, high - start)
            target[outer, :width] = values[inner].astype(target.dtype)
            block = stats[inner]
            target[outer, width:] = block if target is keep else split(block)


def teacher_body(parts, *refs):
    inputs, (head, moved, moved_head, send, keep, rows_ref) = refs[:parts], refs[parts:]
    count = inputs[0].shape[0]
    for i, ref in enumerate(inputs):
        rows_ref[i * count : (i + 1) * count, :] = ref[...]
    half = keep.shape[0]
    width = moved_head.shape[0]
    step = BLOCK
    for at in range(0, 2 * half, step):
        teacher = dot(rows_ref[at : at + step, :], head[...])
        student = moved[at : at + step, :]
        top = jnp.max(teacher, axis=1, keepdims=True)
        exps = jnp.exp(teacher - top)
        total = jnp.sum(exps, axis=1, keepdims=True)
        cross = jnp.sum(exps * (teacher - student), axis=1, keepdims=True)
        emit(at, step, half, width, exps, moved_head, [top, total, cross], send, keep)


def combine_split_body(received, *refs):
    parts, (keep, *sends) = refs[: received + 1], refs[received + 1 :]
    width = keep.shape[1] - BLOCK
    values, top, totals = combine(parts, width)
    stats = pack([top, *totals])
    coded = split(stats)
    rows = keep.shape[0]
    keep[:, :width] = values[:rows]
    keep[:, width:] = stats[:rows]
    for i, send in enumerate(sends):
        inner = slice((i + 1) * rows, (i + 2) * rows)
        send[:, :width] = values[inner].astype(BF16)
        send[:, width:] = coded[inner]


def leave_body(received, *refs):
    teacher, refs = refs[: received + 1], refs[received + 1 :]
    student, (divergence, grad) = refs[: received + 1], refs[received + 1 :]
    width = grad.shape[1]
    teach_values, teach_max, (teach_sum, cross_sum) = combine(teacher, width)
    stud_values, stud_max, (stud_sum, _) = combine(student, width)
    grad[...] = stud_values / stud_sum - teach_values / teach_sum
    value = cross_sum / teach_sum - teach_max - jnp.log(teach_sum) + stud_max + jnp.log(stud_sum)
    rows = grad.shape[0]
    diagonal = lax.broadcasted_iota(jnp.int32, (rows, rows), 0) == lax.broadcasted_iota(
        jnp.int32, (rows, rows), 1
    )
    divergence[...] = jnp.sum(jnp.where(diagonal, value, 0.0), axis=0, keepdims=True)


def per_device(
    tokens,
    moe_gain,
    expert_ids,
    gate_scores,
    w_gate,
    w_up,
    w_down,
    final_gain,
    teacher_head,
    vocab_map,
    student_logits,
    student_head,
):
    devices = lax.axis_size("expert")
    size_z, size_x, _ = radices(devices)
    me = lax.axis_index("expert").astype(jnp.int32).reshape(1)
    tok_dev, features = tokens.shape
    slices = FF // w_gate.shape[2]
    width = student_head.shape[0]
    all_rows = devices * tok_dev
    half, quarter = all_rows // 2, all_rows // (2 * size_x)
    entries = student_head.shape[1]
    order = [
        kz * 2 * size_x + kx * 2 + kc
        for kc in range(2)
        for kx in range(size_x)
        for kz in range(size_z)
    ]

    def swap(values, offset):
        return lax.ppermute(values, "expert", [(i, i ^ offset) for i in range(devices)])

    def gather(rows):
        along_z = [rows] + [swap(rows, kz * 2 * size_x) for kz in range(1, size_z)]
        column = jnp.concatenate(along_z)
        plane = [column] + [swap(column, kx * 2) for kx in range(1, size_x)]
        return plane + [swap(part, 1) for part in plane]

    def scatter(send, keep, body, last):
        cols = keep.shape[1]
        keep, *sends = call(
            functools.partial(body, 1),
            [((quarter, cols), F32)] + [((quarter, cols), BF16)] * (size_x - 1),
            keep,
            swap(send, 1),
        )
        received = [swap(s, 2 * (i + 1)) for i, s in enumerate(sends)]
        keep, *sends = call(
            functools.partial(body, size_x - 1),
            [((tok_dev, cols), F32)] + [((tok_dev, cols), BF16)] * (size_z - 1),
            keep,
            *received,
        )
        received = [swap(s, 2 * size_x * (i + 1)) for i, s in enumerate(sends)]
        return [keep, *received]

    (message,) = call(
        enter_body,
        [((tok_dev, features + BLOCK), BF16)],
        tokens,
        moe_gain.reshape(1, -1),
        expert_ids.T,
        gate_scores.T,
    )

    def student_kernel(me_ref, *refs):
        student_body(me_ref, devices, order, *refs)

    moved, moved_head, stud_send, stud_keep = call(
        student_kernel,
        [
            ((all_rows, entries), F32),
            ((width, entries), BF16),
            ((half, width + BLOCK), BF16),
            ((half, width + BLOCK), F32),
        ],
        me,
        vocab_map.reshape(1, -1),
        student_logits,
        student_head,
        scratch=[pltpu.VMEM((all_rows, entries), F32)],
        scalars=1,
    )
    student = scatter(stud_send, stud_keep, combine_split_body, None)
    arrived = gather(message)
    send, keep = call(
        functools.partial(experts_body, slices, len(arrived)),
        [((half, features), BF16), ((half, features), F32)],
        me,
        *arrived,
        w_gate,
        w_up,
        w_down,
        scratch=[pltpu.VMEM((all_rows, features + BLOCK), BF16)],
        scalars=1,
    )
    summed = scatter(send, keep, add_split_body, None)
    (final_norm,) = call(
        functools.partial(hidden_body, len(summed) - 1),
        [((tok_dev, features), BF16)],
        *summed,
        tokens,
        final_gain.reshape(1, -1),
    )
    arrived = gather(final_norm)
    send, keep = call(
        functools.partial(teacher_body, len(arrived)),
        [((half, width + BLOCK), BF16), ((half, width + BLOCK), F32)],
        *arrived,
        teacher_head,
        moved,
        moved_head,
        scratch=[pltpu.VMEM((all_rows, features), BF16)],
    )
    teacher = scatter(send, keep, combine_split_body, None)
    divergence, grad = call(
        functools.partial(leave_body, len(teacher) - 1),
        [((1, tok_dev), F32), ((tok_dev, width), F32)],
        *teacher,
        *student,
    )
    return divergence.reshape(tok_dev), grad


def solution(mesh):
    placed = (
        P(("groups", "expert"), None),
        P(),
        P(("groups", "expert"), None),
        P(("groups", "expert"), None),
        P("expert", None, None),
        P("expert", None, None),
        P("expert", None, None),
        P(),
        P(None, "expert"),
        P("expert"),
        P("groups", "expert"),
        P(None, "expert"),
    )
    return jax.shard_map(
        per_device,
        mesh=mesh,
        in_specs=placed,
        out_specs=(P(("groups", "expert")), P(("groups", "expert"), None)),
        check_vma=False,
    )
```

time: 243 us -> 108 us (0.44)
  blocking collectives: 146 us -> 0 us
  Pallas kernels: 0 us -> 29.6 us
  starting transfers between devices: 4.65 us -> 30.6 us
  waiting for transfers between devices: 54.2 us -> 36.4 us
  between operations: 14.2 us -> 0.79 us
  matrix products: 7.27 us -> 0 us
  local copies, waits for them, and re-layouts: 12.5 us -> 8.8 us
    all_gather x6 -> x0, blocking collectives: 116 us -> none  [the longest x5 93.6 us: merged(): gathered = jax.tree.map(lambda a: lax.all_gather(a, axis), part)]
    reduce_scatter x1 -> x0, waiting for transfers between devices: 54.2 us -> none  [per_device(): lax.psum_scatter(lax.dot_general(logit_grad, student_head, (((1,), (1,)),...]
    ppermute x0 -> x27, waiting for transfers between devices: none -> 36.4 us  [swap(): lax.ppermute(values, 'expert', [(i, i ^ offset) for i in range(devices)])]
    ppermute x0 -> x27, starting transfers between devices: none -> 30.6 us  [swap(): lax.ppermute(values, 'expert', [(i, i ^ offset) for i in range(devices)])]
    all_to_all x1 -> x0, blocking collectives: 29.8 us -> none  [per_device(): lax.all_to_all(copies, 'expert', split_axis=0, concat_axis=0, tiled=True)]
    pallas_call x0 -> x12, Pallas kernels: none -> 29.6 us  [call(): pl.pallas_call(body, out_shape=[jax.ShapeDtypeStruct(s, d) for s, d in ou...]
    dot_general x7 -> x0, matrix products: 7.27 us -> none  [the longest x1 3.61 us: per_device(): jnp.dot(activated, w_down[0], preferred_element_type=jnp.float32)]
    gather x1 -> x0, local copies, waits for them, and re-layouts: 6.55 us -> none  [per_device(): mapped_head = jnp.take(teacher_head, vocab_map, axis=1)]
  transfers between devices with their start and end apart: 2 -> 27, of which waited for: 1 -> 14; matrix products, arithmetic and copies ran while one was open for 5% -> 1% of each run, Pallas kernels for 0% -> 14%
where the time goes in v1:
time: 108 us
  waiting for transfers between devices  36.4 us (34%)
  starting transfers between devices  30.6 us (28%)
  Pallas kernels  29.6 us (27%)
  local copies, waits for them, and re-layouts  8.8 us (8%)
  other arithmetic  1.68 us (2%)
    ppermute x27, waiting for transfers between devices, swap(): lax.ppermute(values, 'expert', [(i, i ^ offset) for i in range(devices)])  36.4 us
    ppermute x27, starting transfers between devices, swap(): lax.ppermute(values, 'expert', [(i, i ^ offset) for i in range(devices)])  30.6 us
    pallas_call x12, Pallas kernels, call(): pl.pallas_call(body, out_shape=[jax.ShapeDtypeStruct(s, d) for s, d in ou...  29.6 us
    unnamed x48, local copies, waits for them, and re-layouts  6.87 us
  transfers between devices with their start and end apart: 27, of which 14 were waited for; matrix products, arithmetic and copies ran while one was open for 1% of the time, Pallas kernels for 14%

profile of v1, /device:TPU:0, one launch (start us, length us, event | category | flops | bytes accessed | tf_op | source)
XLA Modules:
  0.0 107.9 jit_solution(428708553796854391)
XLA Ops:
  0.6 1.3 %reshape.20.gain = f32[1,3584]{1,0:T(1,128)} reshape(f32[3584]{0:T(1024)} %param.13) | data formatting | bytes 28672 | tf_op jit(solution)/shard_map/reshape | solution.py:300
  2.0 1.6 %shard_map.131 = bf16[8,3712]{1,0:T(8,128)(2,1)} custom-call(bf16[8,3584]{1,0:T(8,128)(2,1)} %refs_4_.4, f32[1,3584]{1,0:T(1,128)} %reshape.20.gain, s32[2,8]{1,0:T(2,128)} %bitcast.5, f32[2,8]{1,0:T(2,128)} %bitcast.6), custom_call_target="tpu_custom_call" | custom-call | tf_op jit(solution)/shard_map/pallas_call | solution.py:71
  3.5 5.0 %collective-permute-start.2 = (bf16[8,3712]{1,0:T(8,128)(2,1)}, bf16[8,3712]{1,0:T(8,128)(2,1)S(1)}, u32[]{:S(2)}, u32[]{:S(2)}) collective-permute-start(bf16[8,3712]{1,0:T(8,128)(2,1)} %shard_map.131), channel_id=1, source_target_pairs={{0,12},{1,13},{2,14},{3,15},{4,8},{5,9},{6,10},{7,11},{8,4},{9,5},... | collective-permute-start | bytes 178184 | tf_op jit(solution)/shard_map/ppermute | solution.py:270
  8.6 0.6 collective-permute-start
  9.2 2.1 %collective-permute-done.2 = bf16[8,3712]{1,0:T(8,128)(2,1)S(1)} collective-permute-done((bf16[8,3712]{1,0:T(8,128)(2,1)}, bf16[8,3712]{1,0:T(8,128)(2,1)S(1)}, u32[]{:S(2)}, u32[]{:S(2)}) %collective-permute-start.2) | collective-permute-done | bytes 59424 | tf_op jit(solution)/shard_map/ppermute | solution.py:270
  11.3 2.7 %collective-permute-done.1 = bf16[8,3712]{1,0:T(8,128)(2,1)S(1)} collective-permute-done((bf16[8,3712]{1,0:T(8,128)(2,1)}, bf16[8,3712]{1,0:T(8,128)(2,1)S(1)}, u32[]{:S(2)}, u32[]{:S(2)}) %collective-permute-start.1) | collective-permute-done | bytes 59424 | tf_op jit(solution)/shard_map/ppermute | solution.py:270
  14.0 0.8 pad_maximum_fusion.refs_0_
  14.8 1.7 %collective-permute-start.3 = (bf16[32,3712]{1,0:T(8,128)(2,1)S(1)}, bf16[32,3712]{1,0:T(8,128)(2,1)S(1)}, u32[]{:S(2)}, u32[]{:S(2)}) collective-permute-start(bf16[32,3712]{1,0:T(8,128)(2,1)S(1)} %pad_maximum_fusion.refs_0_), channel_id=1, source_target_pairs={{0,2},{1,3},{2,0},{3,1},{4,6},{5,7},{6,4},{7,5},{8,10},{9,11},{10,... | collective-permute-start | bytes 712712 | tf_op jit(solution)/shard_map/ppermute | solution.py:270
  16.5 5.3 %collective-permute-done.3.refs_1_ = bf16[32,3712]{1,0:T(8,128)(2,1)S(1)} collective-permute-done((bf16[32,3712]{1,0:T(8,128)(2,1)S(1)}, bf16[32,3712]{1,0:T(8,128)(2,1)S(1)}, u32[]{:S(2)}, u32[]{:S(2)}) %collective-permute-start.3) | collective-permute-done | bytes 237600 | tf_op jit(solution)/shard_map/ppermute | solution.py:270
  21.8 1.5 %collective-permute-done.5.refs_3_ = bf16[32,3712]{1,0:T(8,128)(2,1)S(1)} collective-permute-done((bf16[32,3712]{1,0:T(8,128)(2,1)S(1)}, bf16[32,3712]{1,0:T(8,128)(2,1)S(1)}, u32[]{:S(2)}, u32[]{:S(2)}) %collective-permute-start.5) | collective-permute-done | bytes 237600 | tf_op jit(solution)/shard_map/ppermute | solution.py:270
  23.3 0.7 copy-done.7
  24.0 5.1 %shard_map.132 = (bf16[64,3584]{1,0:T(8,128)(2,1)}, f32[64,3584]{1,0:T(8,128)}) custom-call(s32[1]{0:T(128)} %bitcast.me.me_ref, bf16[32,3712]{1,0:T(8,128)(2,1)} %copy-done, bf16[32,3712]{1,0:T(8,128)(2,1)} %copy-done.5, bf16[32,3712]{1,0:T(8,128)(2,1)} %copy-done.6, bf16[32,3712]{1,0:T(8,128)(2,1)} %copy-done.7, bf16[1,3584,256]{2,1,0:T(8,128)(2,1)} %refs_4_.3, ...), custom_call_target="tpu_custom_call" | custom-call | tf_op jit(solution)/shard_map/pallas_call | solution.py:71
  29.1 0.1 collective-permute-start.6
  29.2 1.9 %collective-permute-done.6.refs_1_ = bf16[64,3584]{1,0:T(8,128)(2,1)S(1)} collective-permute-done((bf16[64,3584]{1,0:T(8,128)(2,1)}, bf16[64,3584]{1,0:T(8,128)(2,1)S(1)}, u32[]{:S(2)}, u32[]{:S(2)}) %collective-permute-start.6) | collective-permute-done | bytes 458784 | tf_op jit(solution)/shard_map/ppermute | solution.py:270
  31.1 0.8 copy-done.2
  31.9 2.2 %shard_map.133 = (f32[32,3584]{1,0:T(8,128)}, bf16[32,3584]{1,0:T(8,128)(2,1)}) custom-call(f32[64,3584]{1,0:T(8,128)} %get-tuple-element.30.refs_0_, bf16[64,3584]{1,0:T(8,128)(2,1)} %copy-done.2), custom_call_target="tpu_custom_call" | custom-call | tf_op jit(solution)/shard_map/pallas_call | solution.py:71
  34.1 1.6 %collective-permute-start.7 = (bf16[32,3584]{1,0:T(8,128)(2,1)}, bf16[32,3584]{1,0:T(8,128)(2,1)S(1)}, u32[]{:S(2)}, u32[]{:S(2)}) collective-permute-start(bf16[32,3584]{1,0:T(8,128)(2,1)} %get-tuple-element.33), channel_id=1, source_target_pairs={{0,2},{1,3},{2,0},{3,1},{4,6},{5,7},{6,4},{7,5},{8,10},{9,11},{10,... | collective-permute-start | bytes 688136 | tf_op jit(solution)/shard_map/ppermute | solution.py:270
  35.7 6.3 %collective-permute-done.7.refs_1_ = bf16[32,3584]{1,0:T(8,128)(2,1)S(1)} collective-permute-done((bf16[32,3584]{1,0:T(8,128)(2,1)}, bf16[32,3584]{1,0:T(8,128)(2,1)S(1)}, u32[]{:S(2)}, u32[]{:S(2)}) %collective-permute-start.7) | collective-permute-done | bytes 229408 | tf_op jit(solution)/shard_map/ppermute | solution.py:270
  41.9 0.7 copy-done.8
  42.6 1.8 %shard_map.134 = (f32[8,3584]{1,0:T(8,128)}, bf16[8,3584]{1,0:T(8,128)(2,1)}, bf16[8,3584]{1,0:T(8,128)(2,1)}, bf16[8,3584]{1,0:T(8,128)(2,1)}) custom-call(f32[32,3584]{1,0:T(8,128)} %get-tuple-element.32.refs_0_, bf16[32,3584]{1,0:T(8,128)(2,1)} %copy-done.8), custom_call_target="tpu_custom_call" | custom-call | tf_op jit(solution)/shard_map/pallas_call | solution.py:71
  44.4 0.7 collective-permute-start.8
  45.1 1.8 %collective-permute-start.9 = (bf16[8,3584]{1,0:T(8,128)(2,1)}, bf16[8,3584]{1,0:T(8,128)(2,1)S(1)}, u32[]{:S(2)}, u32[]{:S(2)}) collective-permute-start(bf16[8,3584]{1,0:T(8,128)(2,1)} %get-tuple-element.36), channel_id=1, source_target_pairs={{0,8},{1,9},{2,10},{3,11},{4,12},{5,13},{6,14},{7,15},{8,0},{9,1},... | collective-permute-start | bytes 172040 | tf_op jit(solution)/shard_map/ppermute | solution.py:270
  46.9 1.9 %collective-permute-start.10 = (bf16[8,3584]{1,0:T(8,128)(2,1)}, bf16[8,3584]{1,0:T(8,128)(2,1)S(1)}, u32[]{:S(2)}, u32[]{:S(2)}) collective-permute-start(bf16[8,3584]{1,0:T(8,128)(2,1)} %get-tuple-element.37), channel_id=1, source_target_pairs={{0,12},{1,13},{2,14},{3,15},{4,8},{5,9},{6,10},{7,11},{8,4},{9,5},... | collective-permute-start | bytes 172040 | tf_op jit(solution)/shard_map/ppermute | solution.py:270
  48.8 0.6 reshape.21.refs_5_
  49.4 2.3 %collective-permute-done.9.refs_2_ = bf16[8,3584]{1,0:T(8,128)(2,1)S(1)} collective-permute-done((bf16[8,3584]{1,0:T(8,128)(2,1)}, bf16[8,3584]{1,0:T(8,128)(2,1)S(1)}, u32[]{:S(2)}, u32[]{:S(2)}) %collective-permute-start.9) | collective-permute-done | bytes 57376 | tf_op jit(solution)/shard_map/ppermute | solution.py:270
  51.7 1.4 %collective-permute-done.10.refs_3_ = bf16[8,3584]{1,0:T(8,128)(2,1)S(1)} collective-permute-done((bf16[8,3584]{1,0:T(8,128)(2,1)}, bf16[8,3584]{1,0:T(8,128)(2,1)S(1)}, u32[]{:S(2)}, u32[]{:S(2)}) %collective-permute-start.10) | collective-permute-done | bytes 57376 | tf_op jit(solution)/shard_map/ppermute | solution.py:270
  53.1 0.6 copy-done.16
  53.7 1.7 %shard_map.135 = bf16[8,3584]{1,0:T(8,128)(2,1)} custom-call(f32[8,3584]{1,0:T(8,128)} %get-tuple-element.34.refs_0_, bf16[8,3584]{1,0:T(8,128)(2,1)} %copy-done.14, bf16[8,3584]{1,0:T(8,128)(2,1)} %copy-done.15, bf16[8,3584]{1,0:T(8,128)(2,1)} %copy-done.16, bf16[8,3584]{1,0:T(8,128)(2,1)} %refs_4_.4, f32[1,3584]{1,0:T(1,128)} %reshape.21.refs_5_), custom_call_target="tpu_custom_call" | custom-call | tf_op jit(solution)/shard_map/pallas_call | solution.py:71
  55.4 1.9 %collective-permute-start.13 = (bf16[8,3584]{1,0:T(8,128)(2,1)}, bf16[8,3584]{1,0:T(8,128)(2,1)S(1)}, u32[]{:S(2)}, u32[]{:S(2)}) collective-permute-start(bf16[8,3584]{1,0:T(8,128)(2,1)} %shard_map.135), channel_id=1, source_target_pairs={{0,12},{1,13},{2,14},{3,15},{4,8},{5,9},{6,10},{7,11},{8,4},{9,5},... | collective-permute-start | bytes 172040 | tf_op jit(solution)/shard_map/ppermute | solution.py:270
  57.3 0.0 collective-permute-start.12
  57.3 2.5 %collective-permute-start.11 = (bf16[8,3584]{1,0:T(8,128)(2,1)}, bf16[8,3584]{1,0:T(8,128)(2,1)S(1)}, u32[]{:S(2)}, u32[]{:S(2)}) collective-permute-start(bf16[8,3584]{1,0:T(8,128)(2,1)} %shard_map.135), channel_id=1, source_target_pairs={{0,4},{1,5},{2,6},{3,7},{4,0},{5,1},{6,2},{7,3},{8,12},{9,13},{10,... | collective-permute-start | bytes 172040 | tf_op jit(solution)/shard_map/ppermute | solution.py:270
  59.8 1.8 %collective-permute-done.13 = bf16[8,3584]{1,0:T(8,128)(2,1)S(1)} collective-permute-done((bf16[8,3584]{1,0:T(8,128)(2,1)}, bf16[8,3584]{1,0:T(8,128)(2,1)S(1)}, u32[]{:S(2)}, u32[]{:S(2)}) %collective-permute-start.13) | collective-permute-done | bytes 57376 | tf_op jit(solution)/shard_map/ppermute | solution.py:270
  61.6 1.2 %collective-permute-done.12 = bf16[8,3584]{1,0:T(8,128)(2,1)S(1)} collective-permute-done((bf16[8,3584]{1,0:T(8,128)(2,1)}, bf16[8,3584]{1,0:T(8,128)(2,1)S(1)}, u32[]{:S(2)}, u32[]{:S(2)}) %collective-permute-start.12) | collective-permute-done | bytes 57376 | tf_op jit(solution)/shard_map/ppermute | solution.py:270
  62.8 0.0 collective-permute-done.11
  62.8 0.8 pad_maximum_fusion.1.refs_0_
  63.7 1.6 %collective-permute-start.14 = (bf16[32,3584]{1,0:T(8,128)(2,1)S(1)}, bf16[32,3584]{1,0:T(8,128)(2,1)S(1)}, u32[]{:S(2)}, u32[]{:S(2)}) collective-permute-start(bf16[32,3584]{1,0:T(8,128)(2,1)S(1)} %pad_maximum_fusion.1.refs_0_), channel_id=1, source_target_pairs={{0,2},{1,3},{2,0},{3,1},{4,6},{5,7},{6,4},{7,5},{8,10},{9,11},{10,... | collective-permute-start | bytes 688136 | tf_op jit(solution)/shard_map/ppermute | solution.py:270
  65.2 4.5 %collective-permute-done.14.refs_1_ = bf16[32,3584]{1,0:T(8,128)(2,1)S(1)} collective-permute-done((bf16[32,3584]{1,0:T(8,128)(2,1)S(1)}, bf16[32,3584]{1,0:T(8,128)(2,1)S(1)}, u32[]{:S(2)}, u32[]{:S(2)}) %collective-permute-start.14) | collective-permute-done | bytes 229408 | tf_op jit(solution)/shard_map/ppermute | solution.py:270
  69.8 3.4 %shard_map.136 = (f32[128,256]{1,0:T(8,128)}, bf16[2048,256]{1,0:T(8,128)(2,1)}, bf16[64,2176]{1,0:T(8,128)(2,1)}, f32[64,2176]{1,0:T(8,128)}) custom-call(s32[1]{0:T(128)} %bitcast.me.me_ref, s32[1,256]{1,0:T(1,128)} %bitcast.7, bf16[128,256]{1,0:T(8,128)(2,1)} %refs_1_.1, bf16[2048,256]{1,0:T(8,128)(2,1)} %refs_2_.1), custom_call_target="tpu_custom_call" | custom-call | tf_op jit(solution)/shard_map/pallas_call | solution.py:71
  73.2 0.4 collective-permute-start.22
  73.6 0.6 copy-done.10
  74.3 0.1 copy-done.11
  74.4 4.4 %shard_map.137 = (bf16[64,2176]{1,0:T(8,128)(2,1)}, f32[64,2176]{1,0:T(8,128)}) custom-call(bf16[32,3584]{1,0:T(8,128)(2,1)} %copy-done.1, bf16[32,3584]{1,0:T(8,128)(2,1)} %copy-done.9, bf16[32,3584]{1,0:T(8,128)(2,1)} %copy-done.10, bf16[32,3584]{1,0:T(8,128)(2,1)} %copy-done.11, bf16[3584,256]{1,0:T(8,128)(2,1)} %refs_4_.5, ...), custom_call_target="tpu_custom_call" | custom-call | tf_op jit(solution)/shard_map/pallas_call | solution.py:71
  78.7 0.1 collective-permute-start.17
  78.8 0.7 copy-done.3
  79.5 2.0 %shard_map.140 = (f32[32,2176]{1,0:T(8,128)}, bf16[32,2176]{1,0:T(8,128)(2,1)}) custom-call(f32[64,2176]{1,0:T(8,128)} %get-tuple-element.48.refs_0_, bf16[64,2176]{1,0:T(8,128)(2,1)} %copy-done.3), custom_call_target="tpu_custom_call" | custom-call | tf_op jit(solution)/shard_map/pallas_call | solution.py:71
  81.6 1.5 %collective-permute-start.23 = (bf16[32,2176]{1,0:T(8,128)(2,1)}, bf16[32,2176]{1,0:T(8,128)(2,1)S(1)}, u32[]{:S(2)}, u32[]{:S(2)}) collective-permute-start(bf16[32,2176]{1,0:T(8,128)(2,1)} %get-tuple-element.51), channel_id=1, source_target_pairs={{0,2},{1,3},{2,0},{3,1},{4,6},{5,7},{6,4},{7,5},{8,10},{9,11},{10,... | collective-permute-start | bytes 417800 | tf_op jit(solution)/shard_map/ppermute | solution.py:270
  83.1 0.7 copy-done.4
  83.8 2.0 %shard_map.138 = (f32[32,2176]{1,0:T(8,128)}, bf16[32,2176]{1,0:T(8,128)(2,1)}) custom-call(f32[64,2176]{1,0:T(8,128)} %get-tuple-element.40.refs_0_, bf16[64,2176]{1,0:T(8,128)(2,1)} %copy-done.4), custom_call_target="tpu_custom_call" | custom-call | tf_op jit(solution)/shard_map/pallas_call | solution.py:71
  85.8 0.5 collective-permute-start.18
  86.3 1.5 %collective-permute-done.23.refs_1_ = bf16[32,2176]{1,0:T(8,128)(2,1)S(1)} collective-permute-done((bf16[32,2176]{1,0:T(8,128)(2,1)}, bf16[32,2176]{1,0:T(8,128)(2,1)S(1)}, u32[]{:S(2)}, u32[]{:S(2)}) %collective-permute-start.23) | collective-permute-done | bytes 139296 | tf_op jit(solution)/shard_map/ppermute | solution.py:270
  87.8 0.6 copy-done.13
  88.4 1.8 %shard_map.141 = (f32[8,2176]{1,0:T(8,128)}, bf16[8,2176]{1,0:T(8,128)(2,1)}, bf16[8,2176]{1,0:T(8,128)(2,1)}, bf16[8,2176]{1,0:T(8,128)(2,1)}) custom-call(f32[32,2176]{1,0:T(8,128)} %get-tuple-element.50.refs_0_, bf16[32,2176]{1,0:T(8,128)(2,1)} %copy-done.13), custom_call_target="tpu_custom_call" | custom-call | tf_op jit(solution)/shard_map/pallas_call | solution.py:71
  90.2 1.4 %collective-permute-start.24 = (bf16[8,2176]{1,0:T(8,128)(2,1)}, bf16[8,2176]{1,0:T(8,128)(2,1)S(1)}, u32[]{:S(2)}, u32[]{:S(2)}) collective-permute-start(bf16[8,2176]{1,0:T(8,128)(2,1)} %get-tuple-element.53), channel_id=1, source_target_pairs={{0,4},{1,5},{2,6},{3,7},{4,0},{5,1},{6,2},{7,3},{8,12},{9,13},{10,... | collective-permute-start | bytes 104456 | tf_op jit(solution)/shard_map/ppermute | solution.py:270
  91.6 1.1 %collective-permute-start.25 = (bf16[8,2176]{1,0:T(8,128)(2,1)}, bf16[8,2176]{1,0:T(8,128)(2,1)S(1)}, u32[]{:S(2)}, u32[]{:S(2)}) collective-permute-start(bf16[8,2176]{1,0:T(8,128)(2,1)} %get-tuple-element.54), channel_id=1, source_target_pairs={{0,8},{1,9},{2,10},{3,11},{4,12},{5,13},{6,14},{7,15},{8,0},{9,1},... | collective-permute-start | bytes 104456 | tf_op jit(solution)/shard_map/ppermute | solution.py:270
  92.7 1.9 %collective-permute-start.26 = (bf16[8,2176]{1,0:T(8,128)(2,1)}, bf16[8,2176]{1,0:T(8,128)(2,1)S(1)}, u32[]{:S(2)}, u32[]{:S(2)}) collective-permute-start(bf16[8,2176]{1,0:T(8,128)(2,1)} %get-tuple-element.55), channel_id=1, source_target_pairs={{0,12},{1,13},{2,14},{3,15},{4,8},{5,9},{6,10},{7,11},{8,4},{9,5},... | collective-permute-start | bytes 104456 | tf_op jit(solution)/shard_map/ppermute | solution.py:270
  94.6 0.7 copy-done.12
  95.3 1.8 %shard_map.139 = (f32[8,2176]{1,0:T(8,128)}, bf16[8,2176]{1,0:T(8,128)(2,1)}, bf16[8,2176]{1,0:T(8,128)(2,1)}, bf16[8,2176]{1,0:T(8,128)(2,1)}) custom-call(f32[32,2176]{1,0:T(8,128)} %get-tuple-element.42.refs_0_, bf16[32,2176]{1,0:T(8,128)(2,1)} %copy-done.12), custom_call_target="tpu_custom_call" | custom-call | tf_op jit(solution)/shard_map/pallas_call | solution.py:71
  97.1 0.5 collective-permute-start.19
  97.5 2.0 %collective-permute-start.20 = (bf16[8,2176]{1,0:T(8,128)(2,1)}, bf16[8,2176]{1,0:T(8,128)(2,1)S(1)}, u32[]{:S(2)}, u32[]{:S(2)}) collective-permute-start(bf16[8,2176]{1,0:T(8,128)(2,1)} %get-tuple-element.46), channel_id=1, source_target_pairs={{0,8},{1,9},{2,10},{3,11},{4,12},{5,13},{6,14},{7,15},{8,0},{9,1},... | collective-permute-start | bytes 104456 | tf_op jit(solution)/shard_map/ppermute | solution.py:270
  99.5 1.9 %collective-permute-start.21 = (bf16[8,2176]{1,0:T(8,128)(2,1)}, bf16[8,2176]{1,0:T(8,128)(2,1)S(1)}, u32[]{:S(2)}, u32[]{:S(2)}) collective-permute-start(bf16[8,2176]{1,0:T(8,128)(2,1)} %get-tuple-element.47), channel_id=1, source_target_pairs={{0,12},{1,13},{2,14},{3,15},{4,8},{5,9},{6,10},{7,11},{8,4},{9,5},... | collective-permute-start | bytes 104456 | tf_op jit(solution)/shard_map/ppermute | solution.py:270
  101.5 1.4 %collective-permute-done.20.refs_2_ = bf16[8,2176]{1,0:T(8,128)(2,1)S(1)} collective-permute-done((bf16[8,2176]{1,0:T(8,128)(2,1)}, bf16[8,2176]{1,0:T(8,128)(2,1)S(1)}, u32[]{:S(2)}, u32[]{:S(2)}) %collective-permute-start.20) | collective-permute-done | bytes 34848 | tf_op jit(solution)/shard_map/ppermute | solution.py:270
  102.9 2.6 %collective-permute-done.21.refs_3_ = bf16[8,2176]{1,0:T(8,128)(2,1)S(1)} collective-permute-done((bf16[8,2176]{1,0:T(8,128)(2,1)}, bf16[8,2176]{1,0:T(8,128)(2,1)S(1)}, u32[]{:S(2)}, u32[]{:S(2)}) %collective-permute-start.21) | collective-permute-done | bytes 34848 | tf_op jit(solution)/shard_map/ppermute | solution.py:270
  105.5 0.6 copy-done.22
  106.1 1.8 %shard_map.142 = (f32[1,8]{1,0:T(1,128)}, f32[8,2048]{1,0:T(8,128)}) custom-call(f32[8,2176]{1,0:T(8,128)} %get-tuple-element.44.refs_0_, bf16[8,2176]{1,0:T(8,128)(2,1)} %copy-done.20, bf16[8,2176]{1,0:T(8,128)(2,1)} %copy-done.21, bf16[8,2176]{1,0:T(8,128)(2,1)} %copy-done.22, f32[8,2176]{1,0:T(8,128)} %get-tuple-element.52.refs_4_, ...), custom_call_target="tpu_custom_call" | custom-call | tf_op jit(solution)/shard_map/pallas_call | solution.py:71
  (54 shorter events, 0.1 us)
Async XLA Ops:
  3.5 7.7 %collective-permute-start.2 = (bf16[8,3712]{1,0:T(8,128)(2,1)}, bf16[8,3712]{1,0:T(8,128)(2,1)S(1)}, u32[]{:S(2)}, u32[]{:S(2)}) collective-permute-start(bf16[8,3712]{1,0:T(8,128)(2,1)} %shard_map.131), channel_id=1, source_target_pairs={{0,12},{1,13},{2,14},{3,15},{4,8},{5,9},{6,10},{7,11},{8,4},{9,5},... | collective-permute-start | bytes 178184 | tf_op jit(solution)/shard_map/ppermute | solution.py:270
  8.6 5.4 %collective-permute-start.1 = (bf16[8,3712]{1,0:T(8,128)(2,1)}, bf16[8,3712]{1,0:T(8,128)(2,1)S(1)}, u32[]{:S(2)}, u32[]{:S(2)}) collective-permute-start(bf16[8,3712]{1,0:T(8,128)(2,1)} %shard_map.131), channel_id=1, source_target_pairs={{0,8},{1,9},{2,10},{3,11},{4,12},{5,13},{6,14},{7,15},{8,0},{9,1},... | collective-permute-start | bytes 178184 | tf_op jit(solution)/shard_map/ppermute | solution.py:270
  8.6 5.4 %collective-permute-start = (bf16[8,3712]{1,0:T(8,128)(2,1)}, bf16[8,3712]{1,0:T(8,128)(2,1)S(1)}, u32[]{:S(2)}, u32[]{:S(2)}) collective-permute-start(bf16[8,3712]{1,0:T(8,128)(2,1)} %shard_map.131), channel_id=1, source_target_pairs={{0,4},{1,5},{2,6},{3,7},{4,0},{5,1},{6,2},{7,3},{8,12},{9,13},{10,... | collective-permute-start | bytes 178184 | tf_op jit(solution)/shard_map/ppermute | solution.py:270
  14.8 8.5 %copy-start = (bf16[32,3712]{1,0:T(8,128)(2,1)}, bf16[32,3712]{1,0:T(8,128)(2,1)S(1)}, u32[]{:S(2)}) copy-start(bf16[32,3712]{1,0:T(8,128)(2,1)S(1)} %pad_maximum_fusion.refs_0_) | copy-start | bytes 712708
  14.8 6.9 %collective-permute-start.3 = (bf16[32,3712]{1,0:T(8,128)(2,1)S(1)}, bf16[32,3712]{1,0:T(8,128)(2,1)S(1)}, u32[]{:S(2)}, u32[]{:S(2)}) collective-permute-start(bf16[32,3712]{1,0:T(8,128)(2,1)S(1)} %pad_maximum_fusion.refs_0_), channel_id=1, source_target_pairs={{0,2},{1,3},{2,0},{3,1},{4,6},{5,7},{6,4},{7,5},{8,10},{9,11},{10,... | collective-permute-start | bytes 712712 | tf_op jit(solution)/shard_map/ppermute | solution.py:270
  16.5 5.3 %collective-permute-start.4 = (bf16[32,3712]{1,0:T(8,128)(2,1)S(1)}, bf16[32,3712]{1,0:T(8,128)(2,1)S(1)}, u32[]{:S(2)}, u32[]{:S(2)}) collective-permute-start(bf16[32,3712]{1,0:T(8,128)(2,1)S(1)} %pad_maximum_fusion.refs_0_), channel_id=1, source_target_pairs={{0,1},{1,0},{2,3},{3,2},{4,5},{5,4},{6,7},{7,6},{8,9},{9,8},{10,11... | collective-permute-start | bytes 712712 | tf_op jit(solution)/shard_map/ppermute | solution.py:270
  21.8 1.5 %copy-start.5 = (bf16[32,3712]{1,0:T(8,128)(2,1)}, bf16[32,3712]{1,0:T(8,128)(2,1)S(1)}, u32[]{:S(2)}) copy-start(bf16[32,3712]{1,0:T(8,128)(2,1)S(1)} %collective-permute-done.3.refs_1_) | copy-start | bytes 712708
  21.8 1.5 %collective-permute-start.5 = (bf16[32,3712]{1,0:T(8,128)(2,1)S(1)}, bf16[32,3712]{1,0:T(8,128)(2,1)S(1)}, u32[]{:S(2)}, u32[]{:S(2)}) collective-permute-start(bf16[32,3712]{1,0:T(8,128)(2,1)S(1)} %collective-permute-done.3.refs_1_), channel_id=1, source_target_pairs={{0,1},{1,0},{2,3},{3,2},{4,5},{5,4},{6,7},{7,6},{8,9},{9,8},{10,11... | collective-permute-start | bytes 712712 | tf_op jit(solution)/shard_map/ppermute | solution.py:270
  21.8 1.5 %copy-start.6 = (bf16[32,3712]{1,0:T(8,128)(2,1)}, bf16[32,3712]{1,0:T(8,128)(2,1)S(1)}, u32[]{:S(2)}) copy-start(bf16[32,3712]{1,0:T(8,128)(2,1)S(1)} %collective-permute-done.4.refs_2_) | copy-start | bytes 712708
  23.3 0.7 copy-start.7
  29.1 19.7 %copy-start.23 = (f32[3584]{0:T(1024)S(1)}, f32[3584]{0:T(1024)}, u32[]{:S(2)}) copy-start(f32[3584]{0:T(1024)} %param.19) | copy-start | bytes 43012
  29.1 2.0 %collective-permute-start.6 = (bf16[64,3584]{1,0:T(8,128)(2,1)}, bf16[64,3584]{1,0:T(8,128)(2,1)S(1)}, u32[]{:S(2)}, u32[]{:S(2)}) collective-permute-start(bf16[64,3584]{1,0:T(8,128)(2,1)} %get-tuple-element.31), channel_id=1, source_target_pairs={{0,1},{1,0},{2,3},{3,2},{4,5},{5,4},{6,7},{7,6},{8,9},{9,8},{10,11... | collective-permute-start | bytes 1376264 | tf_op jit(solution)/shard_map/ppermute | solution.py:270
  31.1 0.8 copy-start.2
  34.1 7.9 %collective-permute-start.7 = (bf16[32,3584]{1,0:T(8,128)(2,1)}, bf16[32,3584]{1,0:T(8,128)(2,1)S(1)}, u32[]{:S(2)}, u32[]{:S(2)}) collective-permute-start(bf16[32,3584]{1,0:T(8,128)(2,1)} %get-tuple-element.33), channel_id=1, source_target_pairs={{0,2},{1,3},{2,0},{3,1},{4,6},{5,7},{6,4},{7,5},{8,10},{9,11},{10,... | collective-permute-start | bytes 688136 | tf_op jit(solution)/shard_map/ppermute | solution.py:270
  41.9 0.7 copy-start.8
  44.4 5.0 %collective-permute-start.8 = (bf16[8,3584]{1,0:T(8,128)(2,1)}, bf16[8,3584]{1,0:T(8,128)(2,1)S(1)}, u32[]{:S(2)}, u32[]{:S(2)}) collective-permute-start(bf16[8,3584]{1,0:T(8,128)(2,1)} %get-tuple-element.35), channel_id=1, source_target_pairs={{0,4},{1,5},{2,6},{3,7},{4,0},{5,1},{6,2},{7,3},{8,12},{9,13},{10,... | collective-permute-start | bytes 172040 | tf_op jit(solution)/shard_map/ppermute | solution.py:270
  45.1 6.6 %collective-permute-start.9 = (bf16[8,3584]{1,0:T(8,128)(2,1)}, bf16[8,3584]{1,0:T(8,128)(2,1)S(1)}, u32[]{:S(2)}, u32[]{:S(2)}) collective-permute-start(bf16[8,3584]{1,0:T(8,128)(2,1)} %get-tuple-element.36), channel_id=1, source_target_pairs={{0,8},{1,9},{2,10},{3,11},{4,12},{5,13},{6,14},{7,15},{8,0},{9,1},... | collective-permute-start | bytes 172040 | tf_op jit(solution)/shard_map/ppermute | solution.py:270
  46.9 6.2 %collective-permute-start.10 = (bf16[8,3584]{1,0:T(8,128)(2,1)}, bf16[8,3584]{1,0:T(8,128)(2,1)S(1)}, u32[]{:S(2)}, u32[]{:S(2)}) collective-permute-start(bf16[8,3584]{1,0:T(8,128)(2,1)} %get-tuple-element.37), channel_id=1, source_target_pairs={{0,12},{1,13},{2,14},{3,15},{4,8},{5,9},{6,10},{7,11},{8,4},{9,5},... | collective-permute-start | bytes 172040 | tf_op jit(solution)/shard_map/ppermute | solution.py:270
  49.4 3.7 %copy-start.14 = (bf16[8,3584]{1,0:T(8,128)(2,1)}, bf16[8,3584]{1,0:T(8,128)(2,1)S(1)}, u32[]{:S(2)}) copy-start(bf16[8,3584]{1,0:T(8,128)(2,1)S(1)} %collective-permute-done.8.refs_1_) | copy-start | bytes 172036
  51.7 1.4 %copy-start.15 = (bf16[8,3584]{1,0:T(8,128)(2,1)}, bf16[8,3584]{1,0:T(8,128)(2,1)S(1)}, u32[]{:S(2)}) copy-start(bf16[8,3584]{1,0:T(8,128)(2,1)S(1)} %collective-permute-done.9.refs_2_) | copy-start | bytes 172036
  53.1 0.6 copy-start.16
  55.4 6.2 %collective-permute-start.13 = (bf16[8,3584]{1,0:T(8,128)(2,1)}, bf16[8,3584]{1,0:T(8,128)(2,1)S(1)}, u32[]{:S(2)}, u32[]{:S(2)}) collective-permute-start(bf16[8,3584]{1,0:T(8,128)(2,1)} %shard_map.135), channel_id=1, source_target_pairs={{0,12},{1,13},{2,14},{3,15},{4,8},{5,9},{6,10},{7,11},{8,4},{9,5},... | collective-permute-start | bytes 172040 | tf_op jit(solution)/shard_map/ppermute | solution.py:270
  57.3 5.5 %collective-permute-start.12 = (bf16[8,3584]{1,0:T(8,128)(2,1)}, bf16[8,3584]{1,0:T(8,128)(2,1)S(1)}, u32[]{:S(2)}, u32[]{:S(2)}) collective-permute-start(bf16[8,3584]{1,0:T(8,128)(2,1)} %shard_map.135), channel_id=1, source_target_pairs={{0,8},{1,9},{2,10},{3,11},{4,12},{5,13},{6,14},{7,15},{8,0},{9,1},... | collective-permute-start | bytes 172040 | tf_op jit(solution)/shard_map/ppermute | solution.py:270
  57.3 5.5 %collective-permute-start.11 = (bf16[8,3584]{1,0:T(8,128)(2,1)}, bf16[8,3584]{1,0:T(8,128)(2,1)S(1)}, u32[]{:S(2)}, u32[]{:S(2)}) collective-permute-start(bf16[8,3584]{1,0:T(8,128)(2,1)} %shard_map.135), channel_id=1, source_target_pairs={{0,4},{1,5},{2,6},{3,7},{4,0},{5,1},{6,2},{7,3},{8,12},{9,13},{10,... | collective-permute-start | bytes 172040 | tf_op jit(solution)/shard_map/ppermute | solution.py:270
  63.7 9.9 %copy-start.1 = (bf16[32,3584]{1,0:T(8,128)(2,1)}, bf16[32,3584]{1,0:T(8,128)(2,1)S(1)}, u32[]{:S(2)}) copy-start(bf16[32,3584]{1,0:T(8,128)(2,1)S(1)} %pad_maximum_fusion.1.refs_0_) | copy-start | bytes 688132
  63.7 6.1 %collective-permute-start.14 = (bf16[32,3584]{1,0:T(8,128)(2,1)S(1)}, bf16[32,3584]{1,0:T(8,128)(2,1)S(1)}, u32[]{:S(2)}, u32[]{:S(2)}) collective-permute-start(bf16[32,3584]{1,0:T(8,128)(2,1)S(1)} %pad_maximum_fusion.1.refs_0_), channel_id=1, source_target_pairs={{0,2},{1,3},{2,0},{3,1},{4,6},{5,7},{6,4},{7,5},{8,10},{9,11},{10,... | collective-permute-start | bytes 688136 | tf_op jit(solution)/shard_map/ppermute | solution.py:270
  65.2 8.4 %collective-permute-start.15 = (bf16[32,3584]{1,0:T(8,128)(2,1)S(1)}, bf16[32,3584]{1,0:T(8,128)(2,1)S(1)}, u32[]{:S(2)}, u32[]{:S(2)}) collective-permute-start(bf16[32,3584]{1,0:T(8,128)(2,1)S(1)} %pad_maximum_fusion.1.refs_0_), channel_id=1, source_target_pairs={{0,1},{1,0},{2,3},{3,2},{4,5},{5,4},{6,7},{7,6},{8,9},{9,8},{10,11... | collective-permute-start | bytes 688136 | tf_op jit(solution)/shard_map/ppermute | solution.py:270
  69.8 3.9 %copy-start.9 = (bf16[32,3584]{1,0:T(8,128)(2,1)}, bf16[32,3584]{1,0:T(8,128)(2,1)S(1)}, u32[]{:S(2)}) copy-start(bf16[32,3584]{1,0:T(8,128)(2,1)S(1)} %collective-permute-done.14.refs_1_) | copy-start | bytes 688132
  69.8 3.8 %collective-permute-start.16 = (bf16[32,3584]{1,0:T(8,128)(2,1)S(1)}, bf16[32,3584]{1,0:T(8,128)(2,1)S(1)}, u32[]{:S(2)}, u32[]{:S(2)}) collective-permute-start(bf16[32,3584]{1,0:T(8,128)(2,1)S(1)} %collective-permute-done.14.refs_1_), channel_id=1, source_target_pairs={{0,1},{1,0},{2,3},{3,2},{4,5},{5,4},{6,7},{7,6},{8,9},{9,8},{10,11... | collective-permute-start | bytes 688136 | tf_op jit(solution)/shard_map/ppermute | solution.py:270
  73.2 5.6 %collective-permute-start.22 = (bf16[64,2176]{1,0:T(8,128)(2,1)}, bf16[64,2176]{1,0:T(8,128)(2,1)S(1)}, u32[]{:S(2)}, u32[]{:S(2)}) collective-permute-start(bf16[64,2176]{1,0:T(8,128)(2,1)} %get-tuple-element.49), channel_id=1, source_target_pairs={{0,1},{1,0},{2,3},{3,2},{4,5},{5,4},{6,7},{7,6},{8,9},{9,8},{10,11... | collective-permute-start | bytes 835592 | tf_op jit(solution)/shard_map/ppermute | solution.py:270
  73.6 0.7 copy-start.10
  73.6 0.7 copy-start.11
  78.7 4.3 %collective-permute-start.17 = (bf16[64,2176]{1,0:T(8,128)(2,1)}, bf16[64,2176]{1,0:T(8,128)(2,1)S(1)}, u32[]{:S(2)}, u32[]{:S(2)}) collective-permute-start(bf16[64,2176]{1,0:T(8,128)(2,1)} %get-tuple-element.41), channel_id=1, source_target_pairs={{0,1},{1,0},{2,3},{3,2},{4,5},{5,4},{6,7},{7,6},{8,9},{9,8},{10,11... | collective-permute-start | bytes 835592 | tf_op jit(solution)/shard_map/ppermute | solution.py:270
  78.8 0.7 copy-start.3
  81.6 6.2 %collective-permute-start.23 = (bf16[32,2176]{1,0:T(8,128)(2,1)}, bf16[32,2176]{1,0:T(8,128)(2,1)S(1)}, u32[]{:S(2)}, u32[]{:S(2)}) collective-permute-start(bf16[32,2176]{1,0:T(8,128)(2,1)} %get-tuple-element.51), channel_id=1, source_target_pairs={{0,2},{1,3},{2,0},{3,1},{4,6},{5,7},{6,4},{7,5},{8,10},{9,11},{10,... | collective-permute-start | bytes 417800 | tf_op jit(solution)/shard_map/ppermute | solution.py:270
  83.1 0.7 copy-start.4
  85.8 8.8 %collective-permute-start.18 = (bf16[32,2176]{1,0:T(8,128)(2,1)}, bf16[32,2176]{1,0:T(8,128)(2,1)S(1)}, u32[]{:S(2)}, u32[]{:S(2)}) collective-permute-start(bf16[32,2176]{1,0:T(8,128)(2,1)} %get-tuple-element.43), channel_id=1, source_target_pairs={{0,2},{1,3},{2,0},{3,1},{4,6},{5,7},{6,4},{7,5},{8,10},{9,11},{10,... | collective-permute-start | bytes 417800 | tf_op jit(solution)/shard_map/ppermute | solution.py:270
  87.8 0.7 copy-start.13
  90.2 9.3 %collective-permute-start.24 = (bf16[8,2176]{1,0:T(8,128)(2,1)}, bf16[8,2176]{1,0:T(8,128)(2,1)S(1)}, u32[]{:S(2)}, u32[]{:S(2)}) collective-permute-start(bf16[8,2176]{1,0:T(8,128)(2,1)} %get-tuple-element.53), channel_id=1, source_target_pairs={{0,4},{1,5},{2,6},{3,7},{4,0},{5,1},{6,2},{7,3},{8,12},{9,13},{10,... | collective-permute-start | bytes 104456 | tf_op jit(solution)/shard_map/ppermute | solution.py:270
  91.6 9.9 %collective-permute-start.25 = (bf16[8,2176]{1,0:T(8,128)(2,1)}, bf16[8,2176]{1,0:T(8,128)(2,1)S(1)}, u32[]{:S(2)}, u32[]{:S(2)}) collective-permute-start(bf16[8,2176]{1,0:T(8,128)(2,1)} %get-tuple-element.54), channel_id=1, source_target_pairs={{0,8},{1,9},{2,10},{3,11},{4,12},{5,13},{6,14},{7,15},{8,0},{9,1},... | collective-permute-start | bytes 104456 | tf_op jit(solution)/shard_map/ppermute | solution.py:270
  92.7 8.7 %collective-permute-start.26 = (bf16[8,2176]{1,0:T(8,128)(2,1)}, bf16[8,2176]{1,0:T(8,128)(2,1)S(1)}, u32[]{:S(2)}, u32[]{:S(2)}) collective-permute-start(bf16[8,2176]{1,0:T(8,128)(2,1)} %get-tuple-element.55), channel_id=1, source_target_pairs={{0,12},{1,13},{2,14},{3,15},{4,8},{5,9},{6,10},{7,11},{8,4},{9,5},... | collective-permute-start | bytes 104456 | tf_op jit(solution)/shard_map/ppermute | solution.py:270
  94.6 0.7 copy-start.12
  97.1 4.4 %collective-permute-start.19 = (bf16[8,2176]{1,0:T(8,128)(2,1)}, bf16[8,2176]{1,0:T(8,128)(2,1)S(1)}, u32[]{:S(2)}, u32[]{:S(2)}) collective-permute-start(bf16[8,2176]{1,0:T(8,128)(2,1)} %get-tuple-element.45), channel_id=1, source_target_pairs={{0,4},{1,5},{2,6},{3,7},{4,0},{5,1},{6,2},{7,3},{8,12},{9,13},{10,... | collective-permute-start | bytes 104456 | tf_op jit(solution)/shard_map/ppermute | solution.py:270
  97.5 5.4 %collective-permute-start.20 = (bf16[8,2176]{1,0:T(8,128)(2,1)}, bf16[8,2176]{1,0:T(8,128)(2,1)S(1)}, u32[]{:S(2)}, u32[]{:S(2)}) collective-permute-start(bf16[8,2176]{1,0:T(8,128)(2,1)} %get-tuple-element.46), channel_id=1, source_target_pairs={{0,8},{1,9},{2,10},{3,11},{4,12},{5,13},{6,14},{7,15},{8,0},{9,1},... | collective-permute-start | bytes 104456 | tf_op jit(solution)/shard_map/ppermute | solution.py:270
  99.5 6.0 %copy-start.17 = (bf16[8,2176]{1,0:T(8,128)(2,1)}, bf16[8,2176]{1,0:T(8,128)(2,1)S(1)}, u32[]{:S(2)}) copy-start(bf16[8,2176]{1,0:T(8,128)(2,1)S(1)} %collective-permute-done.24.refs_5_) | copy-start | bytes 104452
  99.5 5.9 %collective-permute-start.21 = (bf16[8,2176]{1,0:T(8,128)(2,1)}, bf16[8,2176]{1,0:T(8,128)(2,1)S(1)}, u32[]{:S(2)}, u32[]{:S(2)}) collective-permute-start(bf16[8,2176]{1,0:T(8,128)(2,1)} %get-tuple-element.47), channel_id=1, source_target_pairs={{0,12},{1,13},{2,14},{3,15},{4,8},{5,9},{6,10},{7,11},{8,4},{9,5},... | collective-permute-start | bytes 104456 | tf_op jit(solution)/shard_map/ppermute | solution.py:270
  101.5 4.0 %copy-start.18 = (bf16[8,2176]{1,0:T(8,128)(2,1)}, bf16[8,2176]{1,0:T(8,128)(2,1)S(1)}, u32[]{:S(2)}) copy-start(bf16[8,2176]{1,0:T(8,128)(2,1)S(1)} %collective-permute-done.25.refs_6_) | copy-start | bytes 104452
  101.5 4.0 %copy-start.19 = (bf16[8,2176]{1,0:T(8,128)(2,1)}, bf16[8,2176]{1,0:T(8,128)(2,1)S(1)}, u32[]{:S(2)}) copy-start(bf16[8,2176]{1,0:T(8,128)(2,1)S(1)} %collective-permute-done.26.refs_7_) | copy-start | bytes 104452
  101.5 4.0 %copy-start.20 = (bf16[8,2176]{1,0:T(8,128)(2,1)}, bf16[8,2176]{1,0:T(8,128)(2,1)S(1)}, u32[]{:S(2)}) copy-start(bf16[8,2176]{1,0:T(8,128)(2,1)S(1)} %collective-permute-done.19.refs_1_) | copy-start | bytes 104452
  102.9 2.6 %copy-start.21 = (bf16[8,2176]{1,0:T(8,128)(2,1)}, bf16[8,2176]{1,0:T(8,128)(2,1)S(1)}, u32[]{:S(2)}) copy-start(bf16[8,2176]{1,0:T(8,128)(2,1)S(1)} %collective-permute-done.20.refs_2_) | copy-start | bytes 104452
  105.5 0.6 copy-start.22

commit v2 on v1

--- a/solution.py
+++ b/solution.py
@@ -65,26 +65,53 @@
     return values, top, totals
 
 
-def call(body, outs, *args, scratch=(), scalars=0):
+def call(body, outs, *args, scratch=(), scalars=0, after=(), far=0, near=True, near_out=True, limit=16, cost=None):
     smem = pl.BlockSpec(memory_space=pltpu.SMEM)
     vmem = pl.BlockSpec(memory_space=pltpu.VMEM)
+    hbm = pl.BlockSpec(memory_space=pltpu.HBM)
+    unread = pl.BlockSpec(memory_space=pl.ANY)
+    count = len(args)
+    middle = count - scalars - far
+
+    def run(*refs):
+        body(*refs[:count], *refs[count + len(after) :])
+
+    if near:
+        kinds = [None] * scalars + [pltpu.VMEM] * middle + [pltpu.HBM] * far
+        args = [a if k is None else pltpu.with_memory_space_constraint(a, k) for a, k in zip(args, kinds)]
+    kind = pltpu.VMEM if near and near_out else jax.ShapeDtypeStruct
     return pl.pallas_call(
-        body,
-        out_shape=[jax.ShapeDtypeStruct(s, d) for s, d in outs],
-        in_specs=[smem] * scalars + [vmem] * (len(args) - scalars),
+        run,
+        out_shape=[kind(s, d) for s, d in outs],
+        in_specs=[smem] * scalars + [vmem] * middle + [hbm] * far + [unread] * len(after),
         out_specs=[vmem] * len(outs),
         scratch_shapes=list(scratch),
-        compiler_params=pltpu.CompilerParams(vmem_limit_bytes=56 * 2**20),
-    )(*args)
+        compiler_params=pltpu.CompilerParams(vmem_limit_bytes=(limit if near else 56) * 2**20),
+        cost_estimate=cost and pl.CostEstimate(flops=cost[0], bytes_accessed=cost[1], transcendentals=0),
+    )(*args, *after)
+
+
+def fetch(sources, targets, semaphores):
+    copies = [
+        pltpu.make_async_copy(source, target, semaphores.at[i])
+        for i, (source, target) in enumerate(zip(sources, targets))
+    ]
+    for copy in copies:
+        copy.start()
+    return copies
 
 
 def normed_rows(values, gain):
-    return values * lax.rsqrt(jnp.mean(values * values, axis=-1, keepdims=True) + EPSILON) * gain
-
-
-def enter_body(tokens, gain, ids, scores, out):
+    return values * lax.rsqrt(jnp.mean(values * values, axis=-1, keepdims=True) + EPSILON) * gain[None, :]
+
+
+def enter_body(tokens_far, gain_far, ids_far, scores_far, out, tokens, gain, ids, scores, semaphores):
+    copies = fetch(
+        (ids_far, scores_far, tokens_far, gain_far), (ids, scores, tokens, gain), semaphores
+    )
+    for copy in copies[:2]:
+        copy.wait()
     rows, features = tokens.shape
-    out[:, :features] = normed_rows(tokens[...].astype(F32), gain[...]).astype(BF16)
     diagonal = lax.broadcasted_iota(jnp.int32, (rows, rows), 0) == lax.broadcasted_iota(
         jnp.int32, (rows, rows), 1
     )
@@ -101,14 +128,27 @@
     block = block / total
     high = block.astype(BF16).astype(F32)
     out[:, features:] = jnp.where(lanes(rows) < 64, high, block - high).astype(BF16)
+    for copy in copies[2:]:
+        copy.wait()
+    out[:, :features] = normed_rows(tokens[...].astype(F32), gain[...]).astype(BF16)
+
+
+def paired(out):
+    return [slice(at, at + 16) for at in range(0, out.shape[0], 16)]
+
+
+def join_body(*refs):
+    *parts, out = refs
+    for rows, pair in zip(paired(out), zip(*[iter(parts)] * 2)):
+        out[rows, :] = jnp.concatenate([p[...].astype(F32) for p in pair]).astype(BF16)
 
 
 def experts_body(slices, parts, me, *refs):
-    inputs, (w_gate, w_up, w_down, send, keep, rows_ref) = refs[:parts], refs[parts:]
+    inputs, (w_gate, w_up, w_down, keep, send, rows_ref) = refs[:parts], refs[parts:]
     count = inputs[0].shape[0]
     features = w_gate.shape[1]
     for i, ref in enumerate(inputs):
-        rows_ref[i * count : (i + 1) * count, :] = ref[...]
+        rows_ref[i * count : (i + 1) * count, :] = ref[:, : rows_ref.shape[1]]
     expert = me[0] // slices
 
     def block(start, size):
@@ -146,7 +186,8 @@
     rows = keep.shape[0]
     keep[...] = total[:rows]
     for i, send in enumerate(sends):
-        send[...] = total[(i + 1) * rows : (i + 2) * rows].astype(BF16)
+        at = (len(sends) - i) * rows
+        send[...] = total[at : at + rows].astype(BF16)
 
 
 def hidden_body(received, *refs):
@@ -155,10 +196,17 @@
     out[...] = normed_rows(tokens[...].astype(F32) + total, gain[...]).astype(BF16)
 
 
-def student_body(me, devices, order, vocab_map, logits, head, moved, moved_head, send, keep, scratch):
+def student_body(devices, order, prefetched, me, vocab_far, logits_far, head_far, *refs):
+    sources, (moved, moved_head, keep, send, *refs) = refs[:prefetched], refs[prefetched:]
+    targets, (vocab_map, logits, head, scratch, semaphores) = refs[:prefetched], refs[prefetched:]
+    copies = fetch(
+        (vocab_far, logits_far, head_far, *sources), (vocab_map, logits, head, *targets), semaphores
+    )
+    for copy in copies[:3]:
+        copy.wait()
     entries = logits.shape[1]
     tok_dev = logits.shape[0] // devices
-    place = lax.broadcasted_iota(jnp.int32, (entries, entries), 0) == vocab_map[...]
+    place = lax.broadcasted_iota(jnp.int32, (entries, entries), 0) == vocab_map[...][None, :]
     place = jnp.where(place, 1.0, 0.0).astype(BF16)
     scratch[...] = dot_t(logits[...], place)
     moved_head[...] = dot_t(head[...], place).astype(BF16)
@@ -174,6 +222,8 @@
         exps = jnp.exp(student - top)
         total = jnp.sum(exps, axis=1, keepdims=True)
         emit(at, step, half, width, exps, moved_head, [top, total, jnp.zeros_like(top)], send, keep)
+    for copy in copies[3:]:
+        copy.wait()
 
 
 def emit(at, step, half, width, exps, head, columns, send, keep):
@@ -189,7 +239,7 @@
 
 
 def teacher_body(parts, *refs):
-    inputs, (head, moved, moved_head, send, keep, rows_ref) = refs[:parts], refs[parts:]
+    inputs, (head, moved, moved_head, keep, send, rows_ref) = refs[:parts], refs[parts:]
     count = inputs[0].shape[0]
     for i, ref in enumerate(inputs):
         rows_ref[i * count : (i + 1) * count, :] = ref[...]
@@ -216,9 +266,29 @@
     keep[:, :width] = values[:rows]
     keep[:, width:] = stats[:rows]
     for i, send in enumerate(sends):
-        inner = slice((i + 1) * rows, (i + 2) * rows)
+        at = (len(sends) - i) * rows
+        inner = slice(at, at + rows)
         send[:, :width] = values[inner].astype(BF16)
         send[:, width:] = coded[inner]
+
+
+def add_both_body(size_x, size_z, *refs):
+    moe, refs = refs[:size_x], refs[size_x:]
+    student, refs = refs[:2], refs[2:]
+    add_split_body(size_x - 1, *moe, *refs[:size_z])
+    combine_split_body(1, *student, *refs[size_z:])
+
+
+def pass_body(*refs):
+    for source, target in zip(refs[: len(refs) // 2], refs[len(refs) // 2 :]):
+        target[...] = source[...]
+
+
+def join_both_body(size_z, size_x, *refs):
+    parts, refs = refs[:size_z], refs[size_z:]
+    student, (out, *outs) = refs[:size_x], refs[size_x:]
+    join_body(*parts, out)
+    combine_split_body(size_x - 1, *student, *outs)
 
 
 def leave_body(received, *refs):
@@ -234,6 +304,10 @@
         jnp.int32, (rows, rows), 1
     )
     divergence[...] = jnp.sum(jnp.where(diagonal, value, 0.0), axis=0, keepdims=True)
+
+
+def take(outs):
+    return outs[0], outs[1:]
 
 
 def per_device(
@@ -266,65 +340,89 @@
         for kz in range(size_z)
     ]
 
+    near = all_rows <= BLOCK
+    run = functools.partial(call, near=near)
+
     def swap(values, offset):
         return lax.ppermute(values, "expert", [(i, i ^ offset) for i in range(devices)])
 
-    def gather(rows):
-        along_z = [rows] + [swap(rows, kz * 2 * size_x) for kz in range(1, size_z)]
-        column = jnp.concatenate(along_z)
-        plane = [column] + [swap(column, kx * 2) for kx in range(1, size_x)]
+    def along_z(rows):
+        return [rows] + [swap(rows, kz * 2 * size_x) for kz in range(1, size_z)]
+
+    def along_x(column):
+        return [column] + [swap(column, kx * 2) for kx in range(1, size_x)]
+
+    def over_cores(plane):
         return plane + [swap(part, 1) for part in plane]
 
-    def scatter(send, keep, body, last):
-        cols = keep.shape[1]
-        keep, *sends = call(
-            functools.partial(body, 1),
-            [((quarter, cols), F32)] + [((quarter, cols), BF16)] * (size_x - 1),
-            keep,
-            swap(send, 1),
-        )
-        received = [swap(s, 2 * (i + 1)) for i, s in enumerate(sends)]
-        keep, *sends = call(
-            functools.partial(body, size_x - 1),
-            [((tok_dev, cols), F32)] + [((tok_dev, cols), BF16)] * (size_z - 1),
-            keep,
-            *received,
-        )
-        received = [swap(s, 2 * size_x * (i + 1)) for i, s in enumerate(sends)]
-        return [keep, *received]
-
-    (message,) = call(
+    def add_cores(keep, send, body, after=()):
+        outs = [((quarter, keep.shape[1]), d) for d in [F32] + [BF16] * (size_x - 1)]
+        return run(functools.partial(body, 1), outs, keep, swap(send, 1), after=after)
+
+    def add_x(keep, sends, body, after=()):
+        outs = [((tok_dev, keep.shape[1]), d) for d in [F32] + [BF16] * (size_z - 1)]
+        return run(functools.partial(body, size_x - 1), outs, keep, *sends, after=after)
+
+    def along(sends):
+        return [swap(s, 2 * (size_x - 1 - i)) for i, s in enumerate(sends)]
+
+    def from_z(keep, sends):
+        return [keep] + [swap(s, 2 * size_x * (size_z - 1 - i)) for i, s in enumerate(sends)]
+
+    (message,) = run(
         enter_body,
         [((tok_dev, features + BLOCK), BF16)],
         tokens,
-        moe_gain.reshape(1, -1),
+        moe_gain,
         expert_ids.T,
         gate_scores.T,
-    )
-
-    def student_kernel(me_ref, *refs):
-        student_body(me_ref, devices, order, *refs)
-
-    moved, moved_head, stud_send, stud_keep = call(
-        student_kernel,
+        scratch=[
+            pltpu.VMEM((tok_dev, features), BF16),
+            pltpu.VMEM((features,), F32),
+            pltpu.VMEM(expert_ids.T.shape, jnp.int32),
+            pltpu.VMEM(expert_ids.T.shape, F32),
+            pltpu.SemaphoreType.DMA((4,)),
+        ],
+        far=4,
+    )
+    (column_rows,) = run(join_body, [((quarter, features + BLOCK), BF16)], *along_z(message))
+    plane = along_x(column_rows)
+    prefetched = [w_gate, w_up, w_down, teacher_head, tokens, final_gain]
+    fetched = prefetched if near else []
+    moved, moved_head, stud_keep, stud_send, *ready = run(
+        functools.partial(student_body, devices, order, len(fetched)),
         [
             ((all_rows, entries), F32),
             ((width, entries), BF16),
+            ((half, width + BLOCK), F32),
             ((half, width + BLOCK), BF16),
-            ((half, width + BLOCK), F32),
+            *[(a.shape, a.dtype) for a in fetched],
         ],
         me,
-        vocab_map.reshape(1, -1),
+        vocab_map,
         student_logits,
         student_head,
-        scratch=[pltpu.VMEM((all_rows, entries), F32)],
+        *fetched,
+        scratch=[
+            pltpu.VMEM((entries,), jnp.int32),
+            pltpu.VMEM((all_rows, entries), BF16),
+            pltpu.VMEM((width, entries), BF16),
+            pltpu.VMEM((all_rows, entries), F32),
+            pltpu.SemaphoreType.DMA((3 + len(fetched),)),
+        ],
         scalars=1,
-    )
-    student = scatter(stud_send, stud_keep, combine_split_body, None)
-    arrived = gather(message)
-    send, keep = call(
+        far=3 + len(fetched),
+        cost=(2 * entries * width * (all_rows + entries), 2 * sum(a.size for a in prefetched)),
+        after=[column_rows],
+    )
+    w_gate, w_up, w_down, teacher_head, tokens, final_gain = ready if near else prefetched
+    crossed = run(
+        pass_body, [(p.shape, p.dtype) for p in plane[1:]], *plane[1:], after=[stud_keep]
+    )
+    arrived = over_cores([column_rows, *crossed])
+    keep, send = run(
         functools.partial(experts_body, slices, len(arrived)),
-        [((half, features), BF16), ((half, features), F32)],
+        [((half, features), F32), ((half, features), BF16)],
         me,
         *arrived,
         w_gate,
@@ -333,43 +431,65 @@
         scratch=[pltpu.VMEM((all_rows, features + BLOCK), BF16)],
         scalars=1,
     )
-    summed = scatter(send, keep, add_split_body, None)
-    (final_norm,) = call(
+    keep, *sends = add_cores(keep, send, add_split_body)
+    outs = run(
+        functools.partial(add_both_body, size_x, size_z),
+        [((tok_dev, features), d) for d in [F32] + [BF16] * (size_z - 1)]
+        + [((quarter, width + BLOCK), d) for d in [F32] + [BF16] * (size_x - 1)],
+        keep,
+        *along(sends),
+        stud_keep,
+        swap(stud_send, 1),
+    )
+    summed = from_z(*take(outs[:size_z]))
+    stud_keep, *stud_sends = outs[size_z:]
+    (final_norm,) = run(
         functools.partial(hidden_body, len(summed) - 1),
         [((tok_dev, features), BF16)],
         *summed,
         tokens,
-        final_gain.reshape(1, -1),
-    )
-    arrived = gather(final_norm)
-    send, keep = call(
+        final_gain,
+    )
+    column_rows, *outs = run(
+        functools.partial(join_both_body, size_z, size_x),
+        [((quarter, features), BF16)]
+        + [((tok_dev, width + BLOCK), d) for d in [F32] + [BF16] * (size_z - 1)],
+        *along_z(final_norm),
+        stud_keep,
+        *along(stud_sends),
+    )
+    student = from_z(*take(outs))
+    arrived = over_cores(along_x(column_rows))
+    keep, send = run(
         functools.partial(teacher_body, len(arrived)),
-        [((half, width + BLOCK), BF16), ((half, width + BLOCK), F32)],
+        [((half, width + BLOCK), F32), ((half, width + BLOCK), BF16)],
         *arrived,
         teacher_head,
         moved,
         moved_head,
         scratch=[pltpu.VMEM((all_rows, features), BF16)],
     )
-    teacher = scatter(send, keep, combine_split_body, None)
-    divergence, grad = call(
+    keep, *sends = add_cores(keep, send, combine_split_body)
+    teacher = from_z(*take(add_x(keep, along(sends), combine_split_body)))
+    divergence, grad = run(
         functools.partial(leave_body, len(teacher) - 1),
         [((1, tok_dev), F32), ((tok_dev, width), F32)],
         *teacher,
         *student,
+        near_out=False,
     )
     return divergence.reshape(tok_dev), grad
 
 
 def solution(mesh):
     placed = (
-        P(("groups", "expert"), None),
+        P(("groups", "expert")),
         P(),
-        P(("groups", "expert"), None),
-        P(("groups", "expert"), None),
-        P("expert", None, None),
-        P("expert", None, None),
-        P("expert", None, None),
+        P(("groups", "expert")),
+        P(("groups", "expert")),
+        P("expert", None),
+        P("expert", None),
+        P("expert", None),
         P(),
         P(None, "expert"),
         P("expert"),
@@ -380,6 +500,6 @@
         per_device,
         mesh=mesh,
         in_specs=placed,
-        out_specs=(P(("groups", "expert")), P(("groups", "expert"), None)),
+        out_specs=(P(("groups", "expert")), P(("groups", "expert"))),
         check_vma=False,
     )

time: 108 us -> 74.4 us (0.69)
  Pallas kernels: 29.6 us -> 8.66 us
  local copies, waits for them, and re-layouts: 8.8 us -> 0 us
  waiting for transfers between devices: 36.4 us -> 34.5 us
  other arithmetic: 1.68 us -> 0 us
    pallas_call x12 -> x13, Pallas kernels: 29.6 us -> 8.66 us  [call(): pl.pallas_call(run, out_shape=[kind(s, d) for s, d in outs], in_specs=[sm...]
    unnamed x48 -> x0, local copies, waits for them, and re-layouts: 6.87 us -> none
    reshape x2 -> x0, local copies, waits for them, and re-layouts: 1.93 us -> none  [the longest x1 1.32 us: per_device(): moe_gain.reshape(1, -1)]
    ppermute x27, waiting for transfers between devices: 36.4 us -> 34.5 us  [swap(): lax.ppermute(values, 'expert', [(i, i ^ offset) for i in range(devices)])]
    concatenate x2 -> x0, other arithmetic: 1.68 us -> none  [gather(): column = jnp.concatenate(along_z)]
  transfers between devices with their start and end apart: 27 -> 27, of which waited for: 14 -> 16; matrix products, arithmetic and copies ran while one was open for 1% -> 0% of each run, Pallas kernels for 14% -> 5%
where the time goes in v2:
time: 74.4 us; the launch traced here: 74.2 us
  waiting for transfers between devices  34.5 us (46%)
  starting transfers between devices  30.2 us (41%)
  Pallas kernels  8.66 us (12%)
  between operations  0.75 us (1%)
    ppermute x27, waiting for transfers between devices, swap(): lax.ppermute(values, 'expert', [(i, i ^ offset) for i in range(devices)])  34.5 us
    ppermute x27, starting transfers between devices, swap(): lax.ppermute(values, 'expert', [(i, i ^ offset) for i in range(devices)])  30.2 us
    pallas_call x13, Pallas kernels, call(): pl.pallas_call(run, out_shape=[kind(s, d) for s, d in outs], in_specs=[sm...  8.66 us
  transfers between devices with their start and end apart: 27, of which 16 were waited for; matrix products, arithmetic and copies ran while one was open for 0% of the time, Pallas kernels for 5%

profile of v2, /device:TPU:0, one launch (start us, length us, event | category | flops | bytes accessed | tf_op | source)
XLA Modules:
  0.0 74.2 jit_solution(14170299844248000012)
XLA Ops:
  0.6 1.0 %shard_map.131.refs_0_ = bf16[8,3712]{1,0:T(8,128)(2,1)S(1)} custom-call(bf16[8,3584]{1,0:T(8,128)(2,1)} %refs_8_.1, f32[3584]{0:T(1024)} %refs_1_.2, s32[2,8]{1,0:T(2,128)} %bitcast.4, f32[2,8]{1,0:T(2,128)} %bitcast.5), custom_call_target="tpu_custom_call" | custom-call | tf_op jit(solution)/shard_map/pallas_call | solution.py:83
  1.7 5.1 %collective-permute-start.2 = (bf16[8,3712]{1,0:T(8,128)(2,1)S(1)}, bf16[8,3712]{1,0:T(8,128)(2,1)S(1)}, u32[]{:S(2)}, u32[]{:S(2)}) collective-permute-start(bf16[8,3712]{1,0:T(8,128)(2,1)S(1)} %shard_map.131.refs_0_), channel_id=1, source_target_pairs={{0,12},{1,13},{2,14},{3,15},{4,8},{5,9},{6,10},{7,11},{8,4},{9,5},... | collective-permute-start | bytes 178184 | tf_op jit(solution)/shard_map/ppermute | solution.py:347
  6.8 0.0 collective-permute-start.1
  6.8 0.6 collective-permute-start
  7.4 1.8 %collective-permute-done.2.refs_3_ = bf16[8,3712]{1,0:T(8,128)(2,1)S(1)} collective-permute-done((bf16[8,3712]{1,0:T(8,128)(2,1)S(1)}, bf16[8,3712]{1,0:T(8,128)(2,1)S(1)}, u32[]{:S(2)}, u32[]{:S(2)}) %collective-permute-start.2) | collective-permute-done | bytes 59424 | tf_op jit(solution)/shard_map/ppermute | solution.py:347
  9.2 2.7 %collective-permute-done.1.refs_2_ = bf16[8,3712]{1,0:T(8,128)(2,1)S(1)} collective-permute-done((bf16[8,3712]{1,0:T(8,128)(2,1)S(1)}, bf16[8,3712]{1,0:T(8,128)(2,1)S(1)}, u32[]{:S(2)}, u32[]{:S(2)}) %collective-permute-start.1) | collective-permute-done | bytes 59424 | tf_op jit(solution)/shard_map/ppermute | solution.py:347
  11.9 0.0 collective-permute-done.refs_1_
  11.9 1.7 %collective-permute-start.3 = (bf16[32,3712]{1,0:T(8,128)(2,1)S(1)}, bf16[32,3712]{1,0:T(8,128)(2,1)S(1)}, u32[]{:S(2)}, u32[]{:S(2)}) collective-permute-start(bf16[32,3712]{1,0:T(8,128)(2,1)S(1)} %shard_map.132.refs_10_.refs_1_), channel_id=1, source_target_pairs={{0,2},{1,3},{2,0},{3,1},{4,6},{5,7},{6,4},{7,5},{8,10},{9,11},{10,... | collective-permute-start | bytes 712712 | tf_op jit(solution)/shard_map/ppermute | solution.py:347
  13.6 0.0 collective-permute-start.4
  13.6 3.6 %shard_map.133 = (f32[128,256]{1,0:T(8,128)S(1)}, bf16[2048,256]{1,0:T(8,128)(2,1)S(1)}, f32[64,2176]{1,0:T(8,128)S(1)}, bf16[64,2176]{1,0:T(8,128)(2,1)S(1)}, b...) custom-call(s32[1]{0:T(128)} %bitcast.refs_0_, ...), custom_call_target="tpu_custom_call" | custom-call | flops 402653184 | bytes 7404544 | tf_op jit(solution)/shard_map/pallas_call | solution.py:83
  17.2 1.7 %collective-permute-done.3.refs_0_ = bf16[32,3712]{1,0:T(8,128)(2,1)S(1)} collective-permute-done((bf16[32,3712]{1,0:T(8,128)(2,1)S(1)}, bf16[32,3712]{1,0:T(8,128)(2,1)S(1)}, u32[]{:S(2)}, u32[]{:S(2)}) %collective-permute-start.3) | collective-permute-done | bytes 237600 | tf_op jit(solution)/shard_map/ppermute | solution.py:347
  18.9 0.1 collective-permute-start.5
  19.0 0.0 collective-permute-done.4.refs_3_
  19.0 1.5 %collective-permute-done.5.refs_4_ = bf16[32,3712]{1,0:T(8,128)(2,1)S(1)} collective-permute-done((bf16[32,3712]{1,0:T(8,128)(2,1)S(1)}, bf16[32,3712]{1,0:T(8,128)(2,1)S(1)}, u32[]{:S(2)}, u32[]{:S(2)}) %collective-permute-start.5) | collective-permute-done | bytes 237600 | tf_op jit(solution)/shard_map/ppermute | solution.py:347
  20.5 1.0 %shard_map.135 = (f32[64,3584]{1,0:T(8,128)S(1)}, bf16[64,3584]{1,0:T(8,128)(2,1)S(1)}) custom-call(s32[1]{0:T(128)} %bitcast.refs_0_, bf16[32,3712]{1,0:T(8,128)(2,1)S(1)} %shard_map.132.refs_10_.refs_1_, bf16[32,3712]{1,0:T(8,128)(2,1)S(1)} %shard_map.134.refs_2_, bf16[32,3712]{1,0:T(8,128)(2,1)S(1)} %collective-permute-done.4.refs_3_, ...), custom_call_target="tpu_custom_call" | custom-call | tf_op jit(solution)/shard_map/pallas_call | solution.py:83
  21.5 0.2 collective-permute-start.6
  21.7 0.4 collective-permute-start.8
  22.1 1.3 %collective-permute-done.6.refs_1_ = bf16[64,3584]{1,0:T(8,128)(2,1)S(1)} collective-permute-done((bf16[64,3584]{1,0:T(8,128)(2,1)S(1)}, bf16[64,3584]{1,0:T(8,128)(2,1)S(1)}, u32[]{:S(2)}, u32[]{:S(2)}) %collective-permute-start.6) | collective-permute-done | bytes 458784 | tf_op jit(solution)/shard_map/ppermute | solution.py:347
  23.4 0.1 shard_map.136
  23.5 1.6 %collective-permute-start.7 = (bf16[32,3584]{1,0:T(8,128)(2,1)S(1)}, bf16[32,3584]{1,0:T(8,128)(2,1)S(1)}, u32[]{:S(2)}, u32[]{:S(2)}) collective-permute-start(bf16[32,3584]{1,0:T(8,128)(2,1)S(1)} %get-tuple-element.44), channel_id=1, source_target_pairs={{0,2},{1,3},{2,0},{3,1},{4,6},{5,7},{6,4},{7,5},{8,10},{9,11},{10,... | collective-permute-start | bytes 688136 | tf_op jit(solution)/shard_map/ppermute | solution.py:347
  25.1 0.0 collective-permute-done.8.refs_3_
  25.1 6.1 %collective-permute-done.7.refs_1_ = bf16[32,3584]{1,0:T(8,128)(2,1)S(1)} collective-permute-done((bf16[32,3584]{1,0:T(8,128)(2,1)S(1)}, bf16[32,3584]{1,0:T(8,128)(2,1)S(1)}, u32[]{:S(2)}, u32[]{:S(2)}) %collective-permute-start.7) | collective-permute-done | bytes 229408 | tf_op jit(solution)/shard_map/ppermute | solution.py:347
  31.2 0.3 shard_map.137
  31.5 1.6 %collective-permute-start.15 = (bf16[32,2176]{1,0:T(8,128)(2,1)S(1)}, bf16[32,2176]{1,0:T(8,128)(2,1)S(1)}, u32[]{:S(2)}, u32[]{:S(2)}) collective-permute-start(bf16[32,2176]{1,0:T(8,128)(2,1)S(1)} %get-tuple-element.53), channel_id=1, source_target_pairs={{0,2},{1,3},{2,0},{3,1},{4,6},{5,7},{6,4},{7,5},{8,10},{9,11},{10,... | collective-permute-start | bytes 417800 | tf_op jit(solution)/shard_map/ppermute | solution.py:347
  33.1 2.1 %collective-permute-start.9 = (bf16[8,3584]{1,0:T(8,128)(2,1)S(1)}, bf16[8,3584]{1,0:T(8,128)(2,1)S(1)}, u32[]{:S(2)}, u32[]{:S(2)}) collective-permute-start(bf16[8,3584]{1,0:T(8,128)(2,1)S(1)} %get-tuple-element.47), channel_id=1, source_target_pairs={{0,12},{1,13},{2,14},{3,15},{4,8},{5,9},{6,10},{7,11},{8,4},{9,5},... | collective-permute-start | bytes 172040 | tf_op jit(solution)/shard_map/ppermute | solution.py:347
  35.2 0.0 collective-permute-start.10
  35.2 2.3 %collective-permute-start.11 = (bf16[8,3584]{1,0:T(8,128)(2,1)S(1)}, bf16[8,3584]{1,0:T(8,128)(2,1)S(1)}, u32[]{:S(2)}, u32[]{:S(2)}) collective-permute-start(bf16[8,3584]{1,0:T(8,128)(2,1)S(1)} %get-tuple-element.49), channel_id=1, source_target_pairs={{0,4},{1,5},{2,6},{3,7},{4,0},{5,1},{6,2},{7,3},{8,12},{9,13},{10,... | collective-permute-start | bytes 172040 | tf_op jit(solution)/shard_map/ppermute | solution.py:347
  37.5 2.0 %collective-permute-done.9.refs_1_ = bf16[8,3584]{1,0:T(8,128)(2,1)S(1)} collective-permute-done((bf16[8,3584]{1,0:T(8,128)(2,1)S(1)}, bf16[8,3584]{1,0:T(8,128)(2,1)S(1)}, u32[]{:S(2)}, u32[]{:S(2)}) %collective-permute-start.9) | collective-permute-done | bytes 57376 | tf_op jit(solution)/shard_map/ppermute | solution.py:347
  39.5 1.3 %collective-permute-done.10.refs_2_ = bf16[8,3584]{1,0:T(8,128)(2,1)S(1)} collective-permute-done((bf16[8,3584]{1,0:T(8,128)(2,1)S(1)}, bf16[8,3584]{1,0:T(8,128)(2,1)S(1)}, u32[]{:S(2)}, u32[]{:S(2)}) %collective-permute-start.10) | collective-permute-done | bytes 57376 | tf_op jit(solution)/shard_map/ppermute | solution.py:347
  40.8 0.0 collective-permute-done.11.refs_3_
  40.8 0.1 shard_map.138.refs_0_
  41.0 2.2 %collective-permute-start.14 = (bf16[8,3584]{1,0:T(8,128)(2,1)S(1)}, bf16[8,3584]{1,0:T(8,128)(2,1)S(1)}, u32[]{:S(2)}, u32[]{:S(2)}) collective-permute-start(bf16[8,3584]{1,0:T(8,128)(2,1)S(1)} %shard_map.138.refs_0_), channel_id=1, source_target_pairs={{0,12},{1,13},{2,14},{3,15},{4,8},{5,9},{6,10},{7,11},{8,4},{9,5},... | collective-permute-start | bytes 172040 | tf_op jit(solution)/shard_map/ppermute | solution.py:347
  43.2 0.2 collective-permute-start.13
  43.4 2.1 %collective-permute-start.12 = (bf16[8,3584]{1,0:T(8,128)(2,1)S(1)}, bf16[8,3584]{1,0:T(8,128)(2,1)S(1)}, u32[]{:S(2)}, u32[]{:S(2)}) collective-permute-start(bf16[8,3584]{1,0:T(8,128)(2,1)S(1)} %shard_map.138.refs_0_), channel_id=1, source_target_pairs={{0,4},{1,5},{2,6},{3,7},{4,0},{5,1},{6,2},{7,3},{8,12},{9,13},{10,... | collective-permute-start | bytes 172040 | tf_op jit(solution)/shard_map/ppermute | solution.py:347
  45.4 1.7 %collective-permute-done.14.refs_3_ = bf16[8,3584]{1,0:T(8,128)(2,1)S(1)} collective-permute-done((bf16[8,3584]{1,0:T(8,128)(2,1)S(1)}, bf16[8,3584]{1,0:T(8,128)(2,1)S(1)}, u32[]{:S(2)}, u32[]{:S(2)}) %collective-permute-start.14) | collective-permute-done | bytes 57376 | tf_op jit(solution)/shard_map/ppermute | solution.py:347
  47.1 1.4 %collective-permute-done.13.refs_2_ = bf16[8,3584]{1,0:T(8,128)(2,1)S(1)} collective-permute-done((bf16[8,3584]{1,0:T(8,128)(2,1)S(1)}, bf16[8,3584]{1,0:T(8,128)(2,1)S(1)}, u32[]{:S(2)}, u32[]{:S(2)}) %collective-permute-start.13) | collective-permute-done | bytes 57376 | tf_op jit(solution)/shard_map/ppermute | solution.py:347
  48.6 0.0 collective-permute-done.12.refs_1_
  48.6 0.0 collective-permute-done.15.refs_5_
  48.6 0.1 shard_map.139
  48.7 0.6 collective-permute-start.16
  49.3 0.0 collective-permute-start.17
  49.3 5.9 %collective-permute-done.16.refs_1_ = bf16[32,3584]{1,0:T(8,128)(2,1)S(1)} collective-permute-done((bf16[32,3584]{1,0:T(8,128)(2,1)S(1)}, bf16[32,3584]{1,0:T(8,128)(2,1)S(1)}, u32[]{:S(2)}, u32[]{:S(2)}) %collective-permute-start.16) | collective-permute-done | bytes 229408 | tf_op jit(solution)/shard_map/ppermute | solution.py:347
  55.2 0.0 collective-permute-start.18
  55.2 0.0 collective-permute-done.17.refs_2_
  55.2 1.5 %collective-permute-done.18.refs_3_ = bf16[32,3584]{1,0:T(8,128)(2,1)S(1)} collective-permute-done((bf16[32,3584]{1,0:T(8,128)(2,1)S(1)}, bf16[32,3584]{1,0:T(8,128)(2,1)S(1)}, u32[]{:S(2)}, u32[]{:S(2)}) %collective-permute-start.18) | collective-permute-done | bytes 229408 | tf_op jit(solution)/shard_map/ppermute | solution.py:347
  56.7 1.2 %shard_map.140 = (f32[64,2176]{1,0:T(8,128)S(1)}, bf16[64,2176]{1,0:T(8,128)(2,1)S(1)}) custom-call(bf16[32,3584]{1,0:T(8,128)(2,1)S(1)} %get-tuple-element.54.refs_0_, bf16[32,3584]{1,0:T(8,128)(2,1)S(1)} %collective-permute-done.16.refs_1_, bf16[32,3584]{1,0:T(8,128)(2,1)S(1)} %collective-permute-done.17.refs_2_, ...), custom_call_target="tpu_custom_call" | custom-call | tf_op jit(solution)/shard_map/pallas_call | solution.py:83
  57.9 0.2 collective-permute-start.19
  58.1 1.4 %collective-permute-done.19.refs_1_ = bf16[64,2176]{1,0:T(8,128)(2,1)S(1)} collective-permute-done((bf16[64,2176]{1,0:T(8,128)(2,1)S(1)}, bf16[64,2176]{1,0:T(8,128)(2,1)S(1)}, u32[]{:S(2)}, u32[]{:S(2)}) %collective-permute-start.19) | collective-permute-done | bytes 278560 | tf_op jit(solution)/shard_map/ppermute | solution.py:347
  59.5 0.2 shard_map.141
  59.7 0.4 collective-permute-start.20
  60.2 2.7 %collective-permute-start.24 = (bf16[8,2176]{1,0:T(8,128)(2,1)S(1)}, bf16[8,2176]{1,0:T(8,128)(2,1)S(1)}, u32[]{:S(2)}, u32[]{:S(2)}) collective-permute-start(bf16[8,2176]{1,0:T(8,128)(2,1)S(1)} %get-tuple-element.67), channel_id=1, source_target_pairs={{0,12},{1,13},{2,14},{3,15},{4,8},{5,9},{6,10},{7,11},{8,4},{9,5},... | collective-permute-start | bytes 104456 | tf_op jit(solution)/shard_map/ppermute | solution.py:347
  62.9 0.0 collective-permute-start.25
  62.9 1.6 %collective-permute-start.26 = (bf16[8,2176]{1,0:T(8,128)(2,1)S(1)}, bf16[8,2176]{1,0:T(8,128)(2,1)S(1)}, u32[]{:S(2)}, u32[]{:S(2)}) collective-permute-start(bf16[8,2176]{1,0:T(8,128)(2,1)S(1)} %get-tuple-element.69), channel_id=1, source_target_pairs={{0,4},{1,5},{2,6},{3,7},{4,0},{5,1},{6,2},{7,3},{8,12},{9,13},{10,... | collective-permute-start | bytes 104456 | tf_op jit(solution)/shard_map/ppermute | solution.py:347
  64.6 1.0 %collective-permute-done.20.refs_1_ = bf16[32,2176]{1,0:T(8,128)(2,1)S(1)} collective-permute-done((bf16[32,2176]{1,0:T(8,128)(2,1)S(1)}, bf16[32,2176]{1,0:T(8,128)(2,1)S(1)}, u32[]{:S(2)}, u32[]{:S(2)}) %collective-permute-start.20) | collective-permute-done | bytes 139296 | tf_op jit(solution)/shard_map/ppermute | solution.py:347
  65.5 0.1 shard_map.142
  65.7 2.9 %collective-permute-start.21 = (bf16[8,2176]{1,0:T(8,128)(2,1)S(1)}, bf16[8,2176]{1,0:T(8,128)(2,1)S(1)}, u32[]{:S(2)}, u32[]{:S(2)}) collective-permute-start(bf16[8,2176]{1,0:T(8,128)(2,1)S(1)} %get-tuple-element.63), channel_id=1, source_target_pairs={{0,12},{1,13},{2,14},{3,15},{4,8},{5,9},{6,10},{7,11},{8,4},{9,5},... | collective-permute-start | bytes 104456 | tf_op jit(solution)/shard_map/ppermute | solution.py:347
  68.5 0.0 collective-permute-start.22
  68.5 0.0 collective-permute-done.24.refs_5_
  68.6 1.6 %collective-permute-start.23 = (bf16[8,2176]{1,0:T(8,128)(2,1)S(1)}, bf16[8,2176]{1,0:T(8,128)(2,1)S(1)}, u32[]{:S(2)}, u32[]{:S(2)}) collective-permute-start(bf16[8,2176]{1,0:T(8,128)(2,1)S(1)} %get-tuple-element.65), channel_id=1, source_target_pairs={{0,4},{1,5},{2,6},{3,7},{4,0},{5,1},{6,2},{7,3},{8,12},{9,13},{10,... | collective-permute-start | bytes 104456 | tf_op jit(solution)/shard_map/ppermute | solution.py:347
  70.1 0.0 collective-permute-done.25.refs_6_
  70.1 0.0 collective-permute-done.26.refs_7_
  70.1 1.4 %collective-permute-done.21.refs_1_ = bf16[8,2176]{1,0:T(8,128)(2,1)S(1)} collective-permute-done((bf16[8,2176]{1,0:T(8,128)(2,1)S(1)}, bf16[8,2176]{1,0:T(8,128)(2,1)S(1)}, u32[]{:S(2)}, u32[]{:S(2)}) %collective-permute-start.21) | collective-permute-done | bytes 34848 | tf_op jit(solution)/shard_map/ppermute | solution.py:347
  71.6 1.8 %collective-permute-done.22.refs_2_ = bf16[8,2176]{1,0:T(8,128)(2,1)S(1)} collective-permute-done((bf16[8,2176]{1,0:T(8,128)(2,1)S(1)}, bf16[8,2176]{1,0:T(8,128)(2,1)S(1)}, u32[]{:S(2)}, u32[]{:S(2)}) %collective-permute-start.22) | collective-permute-done | bytes 34848 | tf_op jit(solution)/shard_map/ppermute | solution.py:347
  73.4 0.8 %shard_map.143 = (f32[1,8]{1,0:T(1,128)}, f32[8,2048]{1,0:T(8,128)}) custom-call(f32[8,2176]{1,0:T(8,128)S(1)} %get-tuple-element.62.refs_0_, bf16[8,2176]{1,0:T(8,128)(2,1)S(1)} %collective-permute-done.21.refs_1_, bf16[8,2176]{1,0:T(8,128)(2,1)S(1)} %collective-permute-done.22.refs_2_, bf16[8,2176]{1,0:T(8,128)(2,1)S(1)} %collective-permute-done.23.refs_3_, ...), custom_call_target="tpu_custom_call" | custom-call | tf_op jit(solution)/shard_map/pallas_call | solution.py:83
  (3 shorter events, 0.0 us)
Async XLA Ops:
  1.7 7.6 %collective-permute-start.2 = (bf16[8,3712]{1,0:T(8,128)(2,1)S(1)}, bf16[8,3712]{1,0:T(8,128)(2,1)S(1)}, u32[]{:S(2)}, u32[]{:S(2)}) collective-permute-start(bf16[8,3712]{1,0:T(8,128)(2,1)S(1)} %shard_map.131.refs_0_), channel_id=1, source_target_pairs={{0,12},{1,13},{2,14},{3,15},{4,8},{5,9},{6,10},{7,11},{8,4},{9,5},... | collective-permute-start | bytes 178184 | tf_op jit(solution)/shard_map/ppermute | solution.py:347
  6.8 5.2 %collective-permute-start.1 = (bf16[8,3712]{1,0:T(8,128)(2,1)S(1)}, bf16[8,3712]{1,0:T(8,128)(2,1)S(1)}, u32[]{:S(2)}, u32[]{:S(2)}) collective-permute-start(bf16[8,3712]{1,0:T(8,128)(2,1)S(1)} %shard_map.131.refs_0_), channel_id=1, source_target_pairs={{0,8},{1,9},{2,10},{3,11},{4,12},{5,13},{6,14},{7,15},{8,0},{9,1},... | collective-permute-start | bytes 178184 | tf_op jit(solution)/shard_map/ppermute | solution.py:347
  6.8 5.2 %collective-permute-start = (bf16[8,3712]{1,0:T(8,128)(2,1)S(1)}, bf16[8,3712]{1,0:T(8,128)(2,1)S(1)}, u32[]{:S(2)}, u32[]{:S(2)}) collective-permute-start(bf16[8,3712]{1,0:T(8,128)(2,1)S(1)} %shard_map.131.refs_0_), channel_id=1, source_target_pairs={{0,4},{1,5},{2,6},{3,7},{4,0},{5,1},{6,2},{7,3},{8,12},{9,13},{10,... | collective-permute-start | bytes 178184 | tf_op jit(solution)/shard_map/ppermute | solution.py:347
  11.9 6.9 %collective-permute-start.3 = (bf16[32,3712]{1,0:T(8,128)(2,1)S(1)}, bf16[32,3712]{1,0:T(8,128)(2,1)S(1)}, u32[]{:S(2)}, u32[]{:S(2)}) collective-permute-start(bf16[32,3712]{1,0:T(8,128)(2,1)S(1)} %shard_map.132.refs_10_.refs_1_), channel_id=1, source_target_pairs={{0,2},{1,3},{2,0},{3,1},{4,6},{5,7},{6,4},{7,5},{8,10},{9,11},{10,... | collective-permute-start | bytes 712712 | tf_op jit(solution)/shard_map/ppermute | solution.py:347
  13.6 5.4 %collective-permute-start.4 = (bf16[32,3712]{1,0:T(8,128)(2,1)S(1)}, bf16[32,3712]{1,0:T(8,128)(2,1)S(1)}, u32[]{:S(2)}, u32[]{:S(2)}) collective-permute-start(bf16[32,3712]{1,0:T(8,128)(2,1)S(1)} %shard_map.132.refs_10_.refs_1_), channel_id=1, source_target_pairs={{0,1},{1,0},{2,3},{3,2},{4,5},{5,4},{6,7},{7,6},{8,9},{9,8},{10,11... | collective-permute-start | bytes 712712 | tf_op jit(solution)/shard_map/ppermute | solution.py:347
  18.9 1.6 %collective-permute-start.5 = (bf16[32,3712]{1,0:T(8,128)(2,1)S(1)}, bf16[32,3712]{1,0:T(8,128)(2,1)S(1)}, u32[]{:S(2)}, u32[]{:S(2)}) collective-permute-start(bf16[32,3712]{1,0:T(8,128)(2,1)S(1)} %shard_map.134.refs_2_), channel_id=1, source_target_pairs={{0,1},{1,0},{2,3},{3,2},{4,5},{5,4},{6,7},{7,6},{8,9},{9,8},{10,11... | collective-permute-start | bytes 712712 | tf_op jit(solution)/shard_map/ppermute | solution.py:347
  21.5 1.9 %collective-permute-start.6 = (bf16[64,3584]{1,0:T(8,128)(2,1)S(1)}, bf16[64,3584]{1,0:T(8,128)(2,1)S(1)}, u32[]{:S(2)}, u32[]{:S(2)}) collective-permute-start(bf16[64,3584]{1,0:T(8,128)(2,1)S(1)} %get-tuple-element.42), channel_id=1, source_target_pairs={{0,1},{1,0},{2,3},{3,2},{4,5},{5,4},{6,7},{7,6},{8,9},{9,8},{10,11... | collective-permute-start | bytes 1376264 | tf_op jit(solution)/shard_map/ppermute | solution.py:347
  21.7 3.4 %collective-permute-start.8 = (bf16[64,2176]{1,0:T(8,128)(2,1)S(1)}, bf16[64,2176]{1,0:T(8,128)(2,1)S(1)}, u32[]{:S(2)}, u32[]{:S(2)}) collective-permute-start(bf16[64,2176]{1,0:T(8,128)(2,1)S(1)} %get-tuple-element.45), channel_id=1, source_target_pairs={{0,1},{1,0},{2,3},{3,2},{4,5},{5,4},{6,7},{7,6},{8,9},{9,8},{10,11... | collective-permute-start | bytes 835592 | tf_op jit(solution)/shard_map/ppermute | solution.py:347
  23.5 7.7 %collective-permute-start.7 = (bf16[32,3584]{1,0:T(8,128)(2,1)S(1)}, bf16[32,3584]{1,0:T(8,128)(2,1)S(1)}, u32[]{:S(2)}, u32[]{:S(2)}) collective-permute-start(bf16[32,3584]{1,0:T(8,128)(2,1)S(1)} %get-tuple-element.44), channel_id=1, source_target_pairs={{0,2},{1,3},{2,0},{3,1},{4,6},{5,7},{6,4},{7,5},{8,10},{9,11},{10,... | collective-permute-start | bytes 688136 | tf_op jit(solution)/shard_map/ppermute | solution.py:347
  31.5 17.1 %collective-permute-start.15 = (bf16[32,2176]{1,0:T(8,128)(2,1)S(1)}, bf16[32,2176]{1,0:T(8,128)(2,1)S(1)}, u32[]{:S(2)}, u32[]{:S(2)}) collective-permute-start(bf16[32,2176]{1,0:T(8,128)(2,1)S(1)} %get-tuple-element.53), channel_id=1, source_target_pairs={{0,2},{1,3},{2,0},{3,1},{4,6},{5,7},{6,4},{7,5},{8,10},{9,11},{10,... | collective-permute-start | bytes 417800 | tf_op jit(solution)/shard_map/ppermute | solution.py:347
  33.1 6.4 %collective-permute-start.9 = (bf16[8,3584]{1,0:T(8,128)(2,1)S(1)}, bf16[8,3584]{1,0:T(8,128)(2,1)S(1)}, u32[]{:S(2)}, u32[]{:S(2)}) collective-permute-start(bf16[8,3584]{1,0:T(8,128)(2,1)S(1)} %get-tuple-element.47), channel_id=1, source_target_pairs={{0,12},{1,13},{2,14},{3,15},{4,8},{5,9},{6,10},{7,11},{8,4},{9,5},... | collective-permute-start | bytes 172040 | tf_op jit(solution)/shard_map/ppermute | solution.py:347
  35.2 5.6 %collective-permute-start.10 = (bf16[8,3584]{1,0:T(8,128)(2,1)S(1)}, bf16[8,3584]{1,0:T(8,128)(2,1)S(1)}, u32[]{:S(2)}, u32[]{:S(2)}) collective-permute-start(bf16[8,3584]{1,0:T(8,128)(2,1)S(1)} %get-tuple-element.48), channel_id=1, source_target_pairs={{0,8},{1,9},{2,10},{3,11},{4,12},{5,13},{6,14},{7,15},{8,0},{9,1},... | collective-permute-start | bytes 172040 | tf_op jit(solution)/shard_map/ppermute | solution.py:347
  35.2 5.6 %collective-permute-start.11 = (bf16[8,3584]{1,0:T(8,128)(2,1)S(1)}, bf16[8,3584]{1,0:T(8,128)(2,1)S(1)}, u32[]{:S(2)}, u32[]{:S(2)}) collective-permute-start(bf16[8,3584]{1,0:T(8,128)(2,1)S(1)} %get-tuple-element.49), channel_id=1, source_target_pairs={{0,4},{1,5},{2,6},{3,7},{4,0},{5,1},{6,2},{7,3},{8,12},{9,13},{10,... | collective-permute-start | bytes 172040 | tf_op jit(solution)/shard_map/ppermute | solution.py:347
  41.0 6.2 %collective-permute-start.14 = (bf16[8,3584]{1,0:T(8,128)(2,1)S(1)}, bf16[8,3584]{1,0:T(8,128)(2,1)S(1)}, u32[]{:S(2)}, u32[]{:S(2)}) collective-permute-start(bf16[8,3584]{1,0:T(8,128)(2,1)S(1)} %shard_map.138.refs_0_), channel_id=1, source_target_pairs={{0,12},{1,13},{2,14},{3,15},{4,8},{5,9},{6,10},{7,11},{8,4},{9,5},... | collective-permute-start | bytes 172040 | tf_op jit(solution)/shard_map/ppermute | solution.py:347
  43.2 5.4 %collective-permute-start.13 = (bf16[8,3584]{1,0:T(8,128)(2,1)S(1)}, bf16[8,3584]{1,0:T(8,128)(2,1)S(1)}, u32[]{:S(2)}, u32[]{:S(2)}) collective-permute-start(bf16[8,3584]{1,0:T(8,128)(2,1)S(1)} %shard_map.138.refs_0_), channel_id=1, source_target_pairs={{0,8},{1,9},{2,10},{3,11},{4,12},{5,13},{6,14},{7,15},{8,0},{9,1},... | collective-permute-start | bytes 172040 | tf_op jit(solution)/shard_map/ppermute | solution.py:347
  43.4 5.2 %collective-permute-start.12 = (bf16[8,3584]{1,0:T(8,128)(2,1)S(1)}, bf16[8,3584]{1,0:T(8,128)(2,1)S(1)}, u32[]{:S(2)}, u32[]{:S(2)}) collective-permute-start(bf16[8,3584]{1,0:T(8,128)(2,1)S(1)} %shard_map.138.refs_0_), channel_id=1, source_target_pairs={{0,4},{1,5},{2,6},{3,7},{4,0},{5,1},{6,2},{7,3},{8,12},{9,13},{10,... | collective-permute-start | bytes 172040 | tf_op jit(solution)/shard_map/ppermute | solution.py:347
  48.7 6.5 %collective-permute-start.16 = (bf16[32,3584]{1,0:T(8,128)(2,1)S(1)}, bf16[32,3584]{1,0:T(8,128)(2,1)S(1)}, u32[]{:S(2)}, u32[]{:S(2)}) collective-permute-start(bf16[32,3584]{1,0:T(8,128)(2,1)S(1)} %get-tuple-element.54.refs_0_), channel_id=1, source_target_pairs={{0,2},{1,3},{2,0},{3,1},{4,6},{5,7},{6,4},{7,5},{8,10},{9,11},{10,... | collective-permute-start | bytes 688136 | tf_op jit(solution)/shard_map/ppermute | solution.py:347
  49.3 5.9 %collective-permute-start.17 = (bf16[32,3584]{1,0:T(8,128)(2,1)S(1)}, bf16[32,3584]{1,0:T(8,128)(2,1)S(1)}, u32[]{:S(2)}, u32[]{:S(2)}) collective-permute-start(bf16[32,3584]{1,0:T(8,128)(2,1)S(1)} %get-tuple-element.54.refs_0_), channel_id=1, source_target_pairs={{0,1},{1,0},{2,3},{3,2},{4,5},{5,4},{6,7},{7,6},{8,9},{9,8},{10,11... | collective-permute-start | bytes 688136 | tf_op jit(solution)/shard_map/ppermute | solution.py:347
  55.2 1.5 %collective-permute-start.18 = (bf16[32,3584]{1,0:T(8,128)(2,1)S(1)}, bf16[32,3584]{1,0:T(8,128)(2,1)S(1)}, u32[]{:S(2)}, u32[]{:S(2)}) collective-permute-start(bf16[32,3584]{1,0:T(8,128)(2,1)S(1)} %collective-permute-done.16.refs_1_), channel_id=1, source_target_pairs={{0,1},{1,0},{2,3},{3,2},{4,5},{5,4},{6,7},{7,6},{8,9},{9,8},{10,11... | collective-permute-start | bytes 688136 | tf_op jit(solution)/shard_map/ppermute | solution.py:347
  57.9 1.6 %collective-permute-start.19 = (bf16[64,2176]{1,0:T(8,128)(2,1)S(1)}, bf16[64,2176]{1,0:T(8,128)(2,1)S(1)}, u32[]{:S(2)}, u32[]{:S(2)}) collective-permute-start(bf16[64,2176]{1,0:T(8,128)(2,1)S(1)} %get-tuple-element.59), channel_id=1, source_target_pairs={{0,1},{1,0},{2,3},{3,2},{4,5},{5,4},{6,7},{7,6},{8,9},{9,8},{10,11... | collective-permute-start | bytes 835592 | tf_op jit(solution)/shard_map/ppermute | solution.py:347
  59.7 5.8 %collective-permute-start.20 = (bf16[32,2176]{1,0:T(8,128)(2,1)S(1)}, bf16[32,2176]{1,0:T(8,128)(2,1)S(1)}, u32[]{:S(2)}, u32[]{:S(2)}) collective-permute-start(bf16[32,2176]{1,0:T(8,128)(2,1)S(1)} %get-tuple-element.61), channel_id=1, source_target_pairs={{0,2},{1,3},{2,0},{3,1},{4,6},{5,7},{6,4},{7,5},{8,10},{9,11},{10,... | collective-permute-start | bytes 417800 | tf_op jit(solution)/shard_map/ppermute | solution.py:347
  60.2 8.4 %collective-permute-start.24 = (bf16[8,2176]{1,0:T(8,128)(2,1)S(1)}, bf16[8,2176]{1,0:T(8,128)(2,1)S(1)}, u32[]{:S(2)}, u32[]{:S(2)}) collective-permute-start(bf16[8,2176]{1,0:T(8,128)(2,1)S(1)} %get-tuple-element.67), channel_id=1, source_target_pairs={{0,12},{1,13},{2,14},{3,15},{4,8},{5,9},{6,10},{7,11},{8,4},{9,5},... | collective-permute-start | bytes 104456 | tf_op jit(solution)/shard_map/ppermute | solution.py:347
  62.9 7.2 %collective-permute-start.25 = (bf16[8,2176]{1,0:T(8,128)(2,1)S(1)}, bf16[8,2176]{1,0:T(8,128)(2,1)S(1)}, u32[]{:S(2)}, u32[]{:S(2)}) collective-permute-start(bf16[8,2176]{1,0:T(8,128)(2,1)S(1)} %get-tuple-element.68), channel_id=1, source_target_pairs={{0,8},{1,9},{2,10},{3,11},{4,12},{5,13},{6,14},{7,15},{8,0},{9,1},... | collective-permute-start | bytes 104456 | tf_op jit(solution)/shard_map/ppermute | solution.py:347
  62.9 7.2 %collective-permute-start.26 = (bf16[8,2176]{1,0:T(8,128)(2,1)S(1)}, bf16[8,2176]{1,0:T(8,128)(2,1)S(1)}, u32[]{:S(2)}, u32[]{:S(2)}) collective-permute-start(bf16[8,2176]{1,0:T(8,128)(2,1)S(1)} %get-tuple-element.69), channel_id=1, source_target_pairs={{0,4},{1,5},{2,6},{3,7},{4,0},{5,1},{6,2},{7,3},{8,12},{9,13},{10,... | collective-permute-start | bytes 104456 | tf_op jit(solution)/shard_map/ppermute | solution.py:347
  65.7 5.9 %collective-permute-start.21 = (bf16[8,2176]{1,0:T(8,128)(2,1)S(1)}, bf16[8,2176]{1,0:T(8,128)(2,1)S(1)}, u32[]{:S(2)}, u32[]{:S(2)}) collective-permute-start(bf16[8,2176]{1,0:T(8,128)(2,1)S(1)} %get-tuple-element.63), channel_id=1, source_target_pairs={{0,12},{1,13},{2,14},{3,15},{4,8},{5,9},{6,10},{7,11},{8,4},{9,5},... | collective-permute-start | bytes 104456 | tf_op jit(solution)/shard_map/ppermute | solution.py:347
  68.5 4.8 %collective-permute-start.22 = (bf16[8,2176]{1,0:T(8,128)(2,1)S(1)}, bf16[8,2176]{1,0:T(8,128)(2,1)S(1)}, u32[]{:S(2)}, u32[]{:S(2)}) collective-permute-start(bf16[8,2176]{1,0:T(8,128)(2,1)S(1)} %get-tuple-element.64), channel_id=1, source_target_pairs={{0,8},{1,9},{2,10},{3,11},{4,12},{5,13},{6,14},{7,15},{8,0},{9,1},... | collective-permute-start | bytes 104456 | tf_op jit(solution)/shard_map/ppermute | solution.py:347
  68.6 4.8 %collective-permute-start.23 = (bf16[8,2176]{1,0:T(8,128)(2,1)S(1)}, bf16[8,2176]{1,0:T(8,128)(2,1)S(1)}, u32[]{:S(2)}, u32[]{:S(2)}) collective-permute-start(bf16[8,2176]{1,0:T(8,128)(2,1)S(1)} %get-tuple-element.65), channel_id=1, source_target_pairs={{0,4},{1,5},{2,6},{3,7},{4,0},{5,1},{6,2},{7,3},{8,12},{9,13},{10,... | collective-permute-start | bytes 104456 | tf_op jit(solution)/shard_map/ppermute | solution.py:347

commit v3 on v2

--- a/solution.py
+++ b/solution.py
@@ -65,7 +65,7 @@
     return values, top, totals
 
 
-def call(body, outs, *args, scratch=(), scalars=0, after=(), far=0, near=True, near_out=True, limit=16, cost=None):
+def call(body, outs, *args, scratch=(), scalars=0, after=(), far=0, near=True, near_out=True, limit=12, cost=None):
     smem = pl.BlockSpec(memory_space=pltpu.SMEM)
     vmem = pl.BlockSpec(memory_space=pltpu.VMEM)
     hbm = pl.BlockSpec(memory_space=pltpu.HBM)
@@ -101,13 +101,22 @@
     return copies
 
 
+def fetch_body(source, target, semaphores):
+    for copy in fetch((source,), (target,), semaphores):
+        copy.wait()
+
+
 def normed_rows(values, gain):
     return values * lax.rsqrt(jnp.mean(values * values, axis=-1, keepdims=True) + EPSILON) * gain[None, :]
 
 
-def enter_body(tokens_far, gain_far, ids_far, scores_far, out, tokens, gain, ids, scores, semaphores):
+def enter_body(tokens_far, gain_far, ids_far, scores_far, logits_far, map_far, *refs):
+    *outs, entries, tokens, gain, ids, scores, vocab_map, semaphores = refs
+    count = logits_far.shape[0]
     copies = fetch(
-        (ids_far, scores_far, tokens_far, gain_far), (ids, scores, tokens, gain), semaphores
+        (ids_far, scores_far, tokens_far, gain_far, map_far, logits_far),
+        (ids, scores, tokens, gain, vocab_map, entries.at[:count]),
+        semaphores,
     )
     for copy in copies[:2]:
         copy.wait()
@@ -127,10 +136,15 @@
         total = total + score
     block = block / total
     high = block.astype(BF16).astype(F32)
-    out[:, features:] = jnp.where(lanes(rows) < 64, high, block - high).astype(BF16)
+    table = jnp.where(lanes(rows) < 64, high, block - high).astype(BF16)
     for copy in copies[2:]:
         copy.wait()
-    out[:, :features] = normed_rows(tokens[...].astype(F32), gain[...]).astype(BF16)
+    normed = normed_rows(tokens[...].astype(F32), gain[...]).astype(BF16)
+    for out in outs:
+        out[:, :features] = normed
+        out[:, features:] = table
+    places = vocab_map[...].astype(F32)[None, :]
+    entries[count:, :] = jnp.broadcast_to(places, (16, places.shape[1])).astype(BF16)
 
 
 def paired(out):
@@ -139,7 +153,7 @@
 
 def join_body(*refs):
     *parts, out = refs
-    for rows, pair in zip(paired(out), zip(*[iter(parts)] * 2)):
+    for rows, pair in zip(paired(out), zip(*[iter(reversed(parts))] * 2)):
         out[rows, :] = jnp.concatenate([p[...].astype(F32) for p in pair]).astype(BF16)
 
 
@@ -190,70 +204,79 @@
         send[...] = total[at : at + rows].astype(BF16)
 
 
-def hidden_body(received, *refs):
-    parts, (tokens, gain, out) = refs[: received + 1], refs[received + 1 :]
+def hidden_body(received, passing, *refs):
+    parts, (tokens, gain, *refs) = refs[: received + 1], refs[received + 1 :]
+    passed, outs = refs[:passing], refs[passing:]
     total = sum((ref[...].astype(F32) for ref in parts[1:]), parts[0][...])
-    out[...] = normed_rows(tokens[...].astype(F32) + total, gain[...]).astype(BF16)
-
-
-def student_body(devices, order, prefetched, me, vocab_far, logits_far, head_far, *refs):
-    sources, (moved, moved_head, keep, send, *refs) = refs[:prefetched], refs[prefetched:]
-    targets, (vocab_map, logits, head, scratch, semaphores) = refs[:prefetched], refs[prefetched:]
-    copies = fetch(
-        (vocab_far, logits_far, head_far, *sources), (vocab_map, logits, head, *targets), semaphores
-    )
-    for copy in copies[:3]:
-        copy.wait()
-    entries = logits.shape[1]
-    tok_dev = logits.shape[0] // devices
-    place = lax.broadcasted_iota(jnp.int32, (entries, entries), 0) == vocab_map[...][None, :]
-    place = jnp.where(place, 1.0, 0.0).astype(BF16)
-    scratch[...] = dot_t(logits[...], place)
-    moved_head[...] = dot_t(head[...], place).astype(BF16)
+    normed = normed_rows(tokens[...].astype(F32) + total, gain[...]).astype(BF16)
+    for out in outs[: len(outs) - passing]:
+        out[...] = normed
+    for source, target in zip(passed, outs[len(outs) - passing :]):
+        target[...] = source[...]
+
+
+def student_body(devices, order, prefetched, me, ours, theirs, their_head, head_far, *refs):
+    sources, (moved, moved_head, *refs) = refs[:prefetched], refs[prefetched:]
+    outs = len(refs) - prefetched - 3
+    parts, targets, (head, scratch, semaphores) = (
+        refs[:outs],
+        refs[outs : outs + prefetched],
+        refs[outs + prefetched :],
+    )
+    copies = fetch((head_far, *sources), (head, *targets), semaphores)
+    copies[0].wait()
+    count = scratch.shape[0]
+    entries = head.shape[1]
+    tok_dev = count // devices
+    for i, (rows, weights) in enumerate(((ours, head), (theirs, their_head))):
+        cols = slice(i * entries, (i + 1) * entries)
+        index = lax.broadcasted_iota(jnp.int32, (entries, entries), 0).astype(F32)
+        place = index == rows[count:, :].astype(F32)[:1, :]
+        place = jnp.where(place, 1.0, 0.0).astype(BF16)
+        scratch[:, cols] = dot_t(rows[:count, :], place)
+        moved_head[:, cols] = dot_t(weights[...], place).astype(BF16)
     for slot, offset in enumerate(order):
         source = pl.multiple_of((me[0] ^ offset) * tok_dev, tok_dev)
         moved[slot * tok_dev : (slot + 1) * tok_dev, :] = scratch[pl.ds(source, tok_dev), :]
-    half = keep.shape[0]
-    width = moved_head.shape[0]
-    step = min(half, BLOCK)
-    for at in range(0, 2 * half, step):
+    step = min(moved.shape[0], BLOCK)
+    for at in range(0, moved.shape[0], step):
         student = moved[at : at + step, :]
         top = jnp.max(student, axis=1, keepdims=True)
         exps = jnp.exp(student - top)
         total = jnp.sum(exps, axis=1, keepdims=True)
-        emit(at, step, half, width, exps, moved_head, [top, total, jnp.zeros_like(top)], send, keep)
-    for copy in copies[3:]:
+        emit(at, step, exps, moved_head, [top, total, jnp.zeros_like(top)], parts)
+    for copy in copies[1:]:
         copy.wait()
 
 
-def emit(at, step, half, width, exps, head, columns, send, keep):
+def emit(at, step, exps, head, columns, targets):
     stats = pack(columns)
     values = dot_t(exps.astype(BF16), head[...])
-    for start, stop, target in ((0, half, keep), (half, 2 * half, send)):
-        low, high = max(at, start), min(at + step, stop)
+    width = head.shape[0]
+    for i, target in enumerate(targets):
+        rows = target.shape[0]
+        low, high = max(at, i * rows), min(at + step, (i + 1) * rows)
         if low < high:
-            inner, outer = slice(low - at, high - at), slice(low - start, high - start)
+            inner, outer = slice(low - at, high - at), slice(low - i * rows, high - i * rows)
             target[outer, :width] = values[inner].astype(target.dtype)
-            block = stats[inner]
-            target[outer, width:] = block if target is keep else split(block)
+            target[outer, width:] = stats[inner] if i == 0 else split(stats[inner])
 
 
 def teacher_body(parts, *refs):
-    inputs, (head, moved, moved_head, keep, send, rows_ref) = refs[:parts], refs[parts:]
+    inputs, (head, their_head, moved, moved_head, *targets, rows_ref) = refs[:parts], refs[parts:]
     count = inputs[0].shape[0]
     for i, ref in enumerate(inputs):
         rows_ref[i * count : (i + 1) * count, :] = ref[...]
-    half = keep.shape[0]
-    width = moved_head.shape[0]
-    step = BLOCK
-    for at in range(0, 2 * half, step):
-        teacher = dot(rows_ref[at : at + step, :], head[...])
+    step = min(parts * count, BLOCK)
+    for at in range(0, parts * count, step):
+        rows = rows_ref[at : at + step, :]
+        teacher = jnp.concatenate([dot(rows, head[...]), dot(rows, their_head[...])], axis=1)
         student = moved[at : at + step, :]
         top = jnp.max(teacher, axis=1, keepdims=True)
         exps = jnp.exp(teacher - top)
         total = jnp.sum(exps, axis=1, keepdims=True)
         cross = jnp.sum(exps * (teacher - student), axis=1, keepdims=True)
-        emit(at, step, half, width, exps, moved_head, [top, total, cross], send, keep)
+        emit(at, step, exps, moved_head, [top, total, cross], targets)
 
 
 def combine_split_body(received, *refs):
@@ -270,13 +293,6 @@
         inner = slice(at, at + rows)
         send[:, :width] = values[inner].astype(BF16)
         send[:, width:] = coded[inner]
-
-
-def add_both_body(size_x, size_z, *refs):
-    moe, refs = refs[:size_x], refs[size_x:]
-    student, refs = refs[:2], refs[2:]
-    add_split_body(size_x - 1, *moe, *refs[:size_z])
-    combine_split_body(1, *student, *refs[size_z:])
 
 
 def pass_body(*refs):
@@ -333,13 +349,7 @@
     all_rows = devices * tok_dev
     half, quarter = all_rows // 2, all_rows // (2 * size_x)
     entries = student_head.shape[1]
-    order = [
-        kz * 2 * size_x + kx * 2 + kc
-        for kc in range(2)
-        for kx in range(size_x)
-        for kz in range(size_z)
-    ]
-
+    order = [kz * 2 * size_x + kx * 2 for kx in range(size_x) for kz in range(size_z)]
     near = all_rows <= BLOCK
     run = functools.partial(call, near=near)
 
@@ -347,7 +357,8 @@
         return lax.ppermute(values, "expert", [(i, i ^ offset) for i in range(devices)])
 
     def along_z(rows):
-        return [rows] + [swap(rows, kz * 2 * size_x) for kz in range(1, size_z)]
+        far = [swap(a, kz * 2 * size_x) for kz, a in reversed(list(enumerate(rows))[1:])]
+        return [*far, rows[0]]
 
     def along_x(column):
         return [column] + [swap(column, kx * 2) for kx in range(1, size_x)]
@@ -369,53 +380,60 @@
     def from_z(keep, sends):
         return [keep] + [swap(s, 2 * size_x * (size_z - 1 - i)) for i, s in enumerate(sends)]
 
-    (message,) = run(
+    *messages, ours = run(
         enter_body,
-        [((tok_dev, features + BLOCK), BF16)],
+        [((tok_dev, features + BLOCK), BF16)] * size_z + [((all_rows + 16, entries), BF16)],
         tokens,
         moe_gain,
         expert_ids.T,
         gate_scores.T,
+        student_logits,
+        vocab_map,
         scratch=[
             pltpu.VMEM((tok_dev, features), BF16),
             pltpu.VMEM((features,), F32),
             pltpu.VMEM(expert_ids.T.shape, jnp.int32),
             pltpu.VMEM(expert_ids.T.shape, F32),
-            pltpu.SemaphoreType.DMA((4,)),
+            pltpu.VMEM((entries,), jnp.int32),
+            pltpu.SemaphoreType.DMA((6,)),
         ],
-        far=4,
-    )
-    (column_rows,) = run(join_body, [((quarter, features + BLOCK), BF16)], *along_z(message))
+        far=6,
+    )
+    (column_rows,) = run(join_body, [((quarter, features + BLOCK), BF16)], *along_z(messages))
     plane = along_x(column_rows)
+    theirs = swap(ours, 1)
+    their_teacher = swap(teacher_head, 1)
+    their_head = swap(student_head, 1)
     prefetched = [w_gate, w_up, w_down, teacher_head, tokens, final_gain]
     fetched = prefetched if near else []
-    moved, moved_head, stud_keep, stud_send, *ready = run(
+    split_rows = [((quarter, width + BLOCK), d) for d in [F32] + [BF16] * (size_x - 1)]
+    split_dev = [((tok_dev, width + BLOCK), d) for d in [F32] + [BF16] * (size_z - 1)]
+    outs = run(
         functools.partial(student_body, devices, order, len(fetched)),
         [
-            ((all_rows, entries), F32),
-            ((width, entries), BF16),
-            ((half, width + BLOCK), F32),
-            ((half, width + BLOCK), BF16),
+            ((half, 2 * entries), F32),
+            ((width, 2 * entries), BF16),
+            *split_rows,
             *[(a.shape, a.dtype) for a in fetched],
         ],
         me,
-        vocab_map,
-        student_logits,
+        ours,
+        theirs,
+        their_head,
         student_head,
         *fetched,
         scratch=[
-            pltpu.VMEM((entries,), jnp.int32),
-            pltpu.VMEM((all_rows, entries), BF16),
             pltpu.VMEM((width, entries), BF16),
-            pltpu.VMEM((all_rows, entries), F32),
-            pltpu.SemaphoreType.DMA((3 + len(fetched),)),
+            pltpu.VMEM((all_rows, 2 * entries), F32),
+            pltpu.SemaphoreType.DMA((1 + len(fetched),)),
         ],
         scalars=1,
-        far=3 + len(fetched),
-        cost=(2 * entries * width * (all_rows + entries), 2 * sum(a.size for a in prefetched)),
+        far=1 + len(fetched),
+        cost=(4 * entries * width * (half + entries), 2 * sum(a.size for a in prefetched)),
         after=[column_rows],
     )
-    w_gate, w_up, w_down, teacher_head, tokens, final_gain = ready if near else prefetched
+    moved, moved_head, stud_keep, *stud_sends = outs[: 2 + size_x]
+    w_gate, w_up, w_down, teacher_head, tokens, final_gain = outs[2 + size_x :] if near else prefetched
     crossed = run(
         pass_body, [(p.shape, p.dtype) for p in plane[1:]], *plane[1:], after=[stud_keep]
     )
@@ -432,44 +450,45 @@
         scalars=1,
     )
     keep, *sends = add_cores(keep, send, add_split_body)
+    summed = from_z(*take(add_x(keep, along(sends), add_split_body)))
     outs = run(
-        functools.partial(add_both_body, size_x, size_z),
-        [((tok_dev, features), d) for d in [F32] + [BF16] * (size_z - 1)]
-        + [((quarter, width + BLOCK), d) for d in [F32] + [BF16] * (size_x - 1)],
-        keep,
-        *along(sends),
-        stud_keep,
-        swap(stud_send, 1),
-    )
-    summed = from_z(*take(outs[:size_z]))
-    stud_keep, *stud_sends = outs[size_z:]
-    (final_norm,) = run(
-        functools.partial(hidden_body, len(summed) - 1),
-        [((tok_dev, features), BF16)],
+        functools.partial(hidden_body, len(summed) - 1, len(stud_sends)),
+        [((tok_dev, features), BF16)] * size_z + [(a.shape, BF16) for a in stud_sends],
         *summed,
         tokens,
         final_gain,
-    )
+        *stud_sends,
+    )
+    final_norms, stud_sends = outs[:size_z], outs[size_z:]
     column_rows, *outs = run(
         functools.partial(join_both_body, size_z, size_x),
-        [((quarter, features), BF16)]
-        + [((tok_dev, width + BLOCK), d) for d in [F32] + [BF16] * (size_z - 1)],
-        *along_z(final_norm),
+        [((quarter, features), BF16), *split_dev],
+        *along_z(final_norms),
         stud_keep,
         *along(stud_sends),
     )
     student = from_z(*take(outs))
-    arrived = over_cores(along_x(column_rows))
-    keep, send = run(
-        functools.partial(teacher_body, len(arrived)),
-        [((half, width + BLOCK), F32), ((half, width + BLOCK), BF16)],
-        *arrived,
+    plane = along_x(column_rows)
+    if near:
+        (their_teacher,) = run(
+            fetch_body,
+            [(their_teacher.shape, BF16)],
+            their_teacher,
+            scratch=[pltpu.SemaphoreType.DMA((1,))],
+            far=1,
+            cost=(0, 2 * their_teacher.size),
+            after=[column_rows],
+        )
+    keep, *sends = run(
+        functools.partial(teacher_body, len(plane)),
+        split_rows,
+        *plane,
         teacher_head,
+        their_teacher,
         moved,
         moved_head,
-        scratch=[pltpu.VMEM((all_rows, features), BF16)],
-    )
-    keep, *sends = add_cores(keep, send, combine_split_body)
+        scratch=[pltpu.VMEM((half, features), BF16)],
+    )
     teacher = from_z(*take(add_x(keep, along(sends), combine_split_body)))
     divergence, grad = run(
         functools.partial(leave_body, len(teacher) - 1),

time: 74.4 us -> 70.6 us (0.949)
  waiting for transfers between devices: 34.5 us -> 27.6 us
  Pallas kernels: 8.66 us -> 10.1 us
  local copies, waits for them, and re-layouts: 0 us -> 1.25 us
    ppermute x27 -> x26, waiting for transfers between devices: 34.5 us -> 27.6 us  [swap(): lax.ppermute(values, 'expert', [(i, i ^ offset) for i in range(devices)])]
    pallas_call x13, Pallas kernels: 8.66 us -> 10.1 us  [call(): pl.pallas_call(run, out_shape=[kind(s, d) for s, d in outs], in_specs=[sm...]
    unnamed x0 -> x2, local copies, waits for them, and re-layouts: none -> 1.25 us
    ppermute x27 -> x26, starting transfers between devices: 30.2 us -> 30.7 us  [swap(): lax.ppermute(values, 'expert', [(i, i ^ offset) for i in range(devices)])]
  transfers between devices with their start and end apart: 27 -> 26, of which waited for: 16 -> 15; matrix products, arithmetic and copies ran while one was open for 0% -> 0% of each run, Pallas kernels for 5% -> 11%
where the time goes in v3:
time: 70.6 us; the launch traced here: 70.4 us
  starting transfers between devices  30.7 us (43%)
  waiting for transfers between devices  27.6 us (39%)
  Pallas kernels  10.1 us (14%)
  local copies, waits for them, and re-layouts  1.25 us (2%)
  between operations  0.74 us (1%)
    ppermute x26, starting transfers between devices, swap(): lax.ppermute(values, 'expert', [(i, i ^ offset) for i in range(devices)])  30.7 us
    ppermute x26, waiting for transfers between devices, swap(): lax.ppermute(values, 'expert', [(i, i ^ offset) for i in range(devices)])  27.6 us
    pallas_call x13, Pallas kernels, call(): pl.pallas_call(run, out_shape=[kind(s, d) for s, d in outs], in_specs=[sm...  10.1 us
  transfers between devices with their start and end apart: 26, of which 15 were waited for; matrix products, arithmetic and copies ran while one was open for 0% of the time, Pallas kernels for 11%

profile of v3, /device:TPU:0, one launch (start us, length us, event | category | flops | bytes accessed | tf_op | source)
XLA Modules:
  0.0 70.4 jit_solution(1320306855915446907)
XLA Ops:
  0.6 0.5 collective-permute-start.5
  1.1 0.1 collective-permute-start.18
  1.2 1.1 %shard_map.131 = (bf16[8,3712]{1,0:T(8,128)(2,1)S(1)}, bf16[8,3712]{1,0:T(8,128)(2,1)S(1)}, bf16[8,3712]{1,0:T(8,128)(2,1)S(1)}, bf16[8,3712]{1,0:T(8,128)(2,1)S(1)}, bf16[144,256]{1,0:T(8,128)(2,1)S(1)}) custom-call(bf16[8,3584]{1,0:T(8,128)(2,1)} %refs_9_.1, f32[3584]{0:T(1024)} %refs_1_.1, s32[2,8]{1,0:T(2,128)} %bitcast.4, f32[2,8]{1,0:T(2,128)} %bitcast.5, ...), custom_call_target="tpu_custom_call" | custom-call | tf_op jit(solution)/shard_map/pallas_call | solution.py:83
  2.4 5.1 %collective-permute-start = (bf16[8,3712]{1,0:T(8,128)(2,1)S(1)}, bf16[8,3712]{1,0:T(8,128)(2,1)S(1)}, u32[]{:S(2)}, u32[]{:S(2)}) collective-permute-start(bf16[8,3712]{1,0:T(8,128)(2,1)S(1)} %get-tuple-element.43), channel_id=1, source_target_pairs={{0,12},{1,13},{2,14},{3,15},{4,8},{5,9},{6,10},{7,11},{8,4},{9,5},... | collective-permute-start | bytes 178184 | tf_op jit(solution)/shard_map/ppermute | solution.py:357
  7.5 0.0 collective-permute-start.1
  7.5 0.6 collective-permute-start.2
  8.1 1.7 %collective-permute-done.refs_0_ = bf16[8,3712]{1,0:T(8,128)(2,1)S(1)} collective-permute-done((bf16[8,3712]{1,0:T(8,128)(2,1)S(1)}, bf16[8,3712]{1,0:T(8,128)(2,1)S(1)}, u32[]{:S(2)}, u32[]{:S(2)}) %collective-permute-start) | collective-permute-done | bytes 59424 | tf_op jit(solution)/shard_map/ppermute | solution.py:357
  9.8 3.0 %collective-permute-done.1.refs_1_ = bf16[8,3712]{1,0:T(8,128)(2,1)S(1)} collective-permute-done((bf16[8,3712]{1,0:T(8,128)(2,1)S(1)}, bf16[8,3712]{1,0:T(8,128)(2,1)S(1)}, u32[]{:S(2)}, u32[]{:S(2)}) %collective-permute-start.1) | collective-permute-done | bytes 59424 | tf_op jit(solution)/shard_map/ppermute | solution.py:357
  12.8 0.0 collective-permute-done.2.refs_2_
  12.9 1.6 %collective-permute-start.3 = (bf16[32,3712]{1,0:T(8,128)(2,1)S(1)}, bf16[32,3712]{1,0:T(8,128)(2,1)S(1)}, u32[]{:S(2)}, u32[]{:S(2)}) collective-permute-start(bf16[32,3712]{1,0:T(8,128)(2,1)S(1)} %shard_map.132.refs_11_.refs_1_), channel_id=1, source_target_pairs={{0,2},{1,3},{2,0},{3,1},{4,6},{5,7},{6,4},{7,5},{8,10},{9,11},{10,... | collective-permute-start | bytes 712712 | tf_op jit(solution)/shard_map/ppermute | solution.py:357
  14.5 0.0 collective-permute-start.4
  14.5 0.5 collective-permute-start.6
  15.0 0.8 %collective-permute-done.4.refs_2_ = bf16[144,256]{1,0:T(8,128)(2,1)S(1)} collective-permute-done((bf16[144,256]{1,0:T(8,128)(2,1)S(1)}, bf16[144,256]{1,0:T(8,128)(2,1)S(1)}, u32[]{:S(2)}, u32[]{:S(2)}) %collective-permute-start.4) | collective-permute-done | bytes 73760 | tf_op jit(solution)/shard_map/ppermute | solution.py:357
  15.7 0.0 collective-permute-done.5.refs_3_
  15.7 3.5 %shard_map.133 = (f32[64,512]{1,0:T(8,128)S(1)}, bf16[2048,512]{1,0:T(8,128)(2,1)S(1)}, f32[32,2176]{1,0:T(8,128)S(1)}, bf16[32,2176]{1,0:T(8,128)(2,1)S(1)}, bf...) custom-call(s32[1]{0:T(128)} %bitcast.refs_0_, ...), custom_call_target="tpu_custom_call" | custom-call | flops 671088640 | bytes 7404544 | tf_op jit(solution)/shard_map/pallas_call | solution.py:83
  19.3 1.1 %collective-permute-done.3.refs_0_ = bf16[32,3712]{1,0:T(8,128)(2,1)S(1)} collective-permute-done((bf16[32,3712]{1,0:T(8,128)(2,1)S(1)}, bf16[32,3712]{1,0:T(8,128)(2,1)S(1)}, u32[]{:S(2)}, u32[]{:S(2)}) %collective-permute-start.3) | collective-permute-done | bytes 237600 | tf_op jit(solution)/shard_map/ppermute | solution.py:357
  20.4 0.1 collective-permute-start.7
  20.5 0.0 collective-permute-done.6.refs_3_
  20.5 1.5 %collective-permute-done.7.refs_4_ = bf16[32,3712]{1,0:T(8,128)(2,1)S(1)} collective-permute-done((bf16[32,3712]{1,0:T(8,128)(2,1)S(1)}, bf16[32,3712]{1,0:T(8,128)(2,1)S(1)}, u32[]{:S(2)}, u32[]{:S(2)}) %collective-permute-start.7) | collective-permute-done | bytes 237600 | tf_op jit(solution)/shard_map/ppermute | solution.py:357
  21.9 1.0 %shard_map.135 = (f32[64,3584]{1,0:T(8,128)S(1)}, bf16[64,3584]{1,0:T(8,128)(2,1)S(1)}) custom-call(s32[1]{0:T(128)} %bitcast.refs_0_, bf16[32,3712]{1,0:T(8,128)(2,1)S(1)} %shard_map.132.refs_11_.refs_1_, bf16[32,3712]{1,0:T(8,128)(2,1)S(1)} %shard_map.134.refs_2_, bf16[32,3712]{1,0:T(8,128)(2,1)S(1)} %collective-permute-done.6.refs_3_, ...), custom_call_target="tpu_custom_call" | custom-call | tf_op jit(solution)/shard_map/pallas_call | solution.py:83
  23.0 0.2 collective-permute-start.8
  23.2 1.7 %collective-permute-done.8.refs_1_ = bf16[64,3584]{1,0:T(8,128)(2,1)S(1)} collective-permute-done((bf16[64,3584]{1,0:T(8,128)(2,1)S(1)}, bf16[64,3584]{1,0:T(8,128)(2,1)S(1)}, u32[]{:S(2)}, u32[]{:S(2)}) %collective-permute-start.8) | collective-permute-done | bytes 458784 | tf_op jit(solution)/shard_map/ppermute | solution.py:357
  24.9 0.1 shard_map.136
  25.0 1.6 %collective-permute-start.9 = (bf16[32,3584]{1,0:T(8,128)(2,1)S(1)}, bf16[32,3584]{1,0:T(8,128)(2,1)S(1)}, u32[]{:S(2)}, u32[]{:S(2)}) collective-permute-start(bf16[32,3584]{1,0:T(8,128)(2,1)S(1)} %get-tuple-element.55), channel_id=1, source_target_pairs={{0,2},{1,3},{2,0},{3,1},{4,6},{5,7},{6,4},{7,5},{8,10},{9,11},{10,... | collective-permute-start | bytes 688136 | tf_op jit(solution)/shard_map/ppermute | solution.py:357
  26.5 6.2 %collective-permute-done.9.refs_1_ = bf16[32,3584]{1,0:T(8,128)(2,1)S(1)} collective-permute-done((bf16[32,3584]{1,0:T(8,128)(2,1)S(1)}, bf16[32,3584]{1,0:T(8,128)(2,1)S(1)}, u32[]{:S(2)}, u32[]{:S(2)}) %collective-permute-start.9) | collective-permute-done | bytes 229408 | tf_op jit(solution)/shard_map/ppermute | solution.py:357
  32.7 0.1 shard_map.137
  32.7 2.1 %collective-permute-start.10 = (bf16[8,3584]{1,0:T(8,128)(2,1)S(1)}, bf16[8,3584]{1,0:T(8,128)(2,1)S(1)}, u32[]{:S(2)}, u32[]{:S(2)}) collective-permute-start(bf16[8,3584]{1,0:T(8,128)(2,1)S(1)} %get-tuple-element.57), channel_id=1, source_target_pairs={{0,12},{1,13},{2,14},{3,15},{4,8},{5,9},{6,10},{7,11},{8,4},{9,5},... | collective-permute-start | bytes 172040 | tf_op jit(solution)/shard_map/ppermute | solution.py:357
  34.8 0.0 collective-permute-start.11
  34.8 2.4 %collective-permute-start.12 = (bf16[8,3584]{1,0:T(8,128)(2,1)S(1)}, bf16[8,3584]{1,0:T(8,128)(2,1)S(1)}, u32[]{:S(2)}, u32[]{:S(2)}) collective-permute-start(bf16[8,3584]{1,0:T(8,128)(2,1)S(1)} %get-tuple-element.59), channel_id=1, source_target_pairs={{0,4},{1,5},{2,6},{3,7},{4,0},{5,1},{6,2},{7,3},{8,12},{9,13},{10,... | collective-permute-start | bytes 172040 | tf_op jit(solution)/shard_map/ppermute | solution.py:357
  37.2 2.0 %collective-permute-done.10.refs_1_ = bf16[8,3584]{1,0:T(8,128)(2,1)S(1)} collective-permute-done((bf16[8,3584]{1,0:T(8,128)(2,1)S(1)}, bf16[8,3584]{1,0:T(8,128)(2,1)S(1)}, u32[]{:S(2)}, u32[]{:S(2)}) %collective-permute-start.10) | collective-permute-done | bytes 57376 | tf_op jit(solution)/shard_map/ppermute | solution.py:357
  39.2 1.3 %collective-permute-done.11.refs_2_ = bf16[8,3584]{1,0:T(8,128)(2,1)S(1)} collective-permute-done((bf16[8,3584]{1,0:T(8,128)(2,1)S(1)}, bf16[8,3584]{1,0:T(8,128)(2,1)S(1)}, u32[]{:S(2)}, u32[]{:S(2)}) %collective-permute-start.11) | collective-permute-done | bytes 57376 | tf_op jit(solution)/shard_map/ppermute | solution.py:357
  40.4 0.0 collective-permute-done.12.refs_3_
  40.5 0.1 shard_map.138
  40.6 1.6 %collective-permute-start.16 = (bf16[32,2176]{1,0:T(8,128)(2,1)S(1)}, bf16[32,2176]{1,0:T(8,128)(2,1)S(1)}, u32[]{:S(2)}, u32[]{:S(2)}) collective-permute-start(bf16[32,2176]{1,0:T(8,128)(2,1)S(1)} %get-tuple-element.67), channel_id=1, source_target_pairs={{0,2},{1,3},{2,0},{3,1},{4,6},{5,7},{6,4},{7,5},{8,10},{9,11},{10,... | collective-permute-start | bytes 417800 | tf_op jit(solution)/shard_map/ppermute | solution.py:357
  42.2 1.9 %collective-permute-start.13 = (bf16[8,3584]{1,0:T(8,128)(2,1)S(1)}, bf16[8,3584]{1,0:T(8,128)(2,1)S(1)}, u32[]{:S(2)}, u32[]{:S(2)}) collective-permute-start(bf16[8,3584]{1,0:T(8,128)(2,1)S(1)} %get-tuple-element.63), channel_id=1, source_target_pairs={{0,12},{1,13},{2,14},{3,15},{4,8},{5,9},{6,10},{7,11},{8,4},{9,5},... | collective-permute-start | bytes 172040 | tf_op jit(solution)/shard_map/ppermute | solution.py:357
  44.0 0.5 collective-permute-start.14
  44.5 2.0 %collective-permute-start.15 = (bf16[8,3584]{1,0:T(8,128)(2,1)S(1)}, bf16[8,3584]{1,0:T(8,128)(2,1)S(1)}, u32[]{:S(2)}, u32[]{:S(2)}) collective-permute-start(bf16[8,3584]{1,0:T(8,128)(2,1)S(1)} %get-tuple-element.65), channel_id=1, source_target_pairs={{0,4},{1,5},{2,6},{3,7},{4,0},{5,1},{6,2},{7,3},{8,12},{9,13},{10,... | collective-permute-start | bytes 172040 | tf_op jit(solution)/shard_map/ppermute | solution.py:357
  46.6 1.6 %collective-permute-done.13.refs_0_ = bf16[8,3584]{1,0:T(8,128)(2,1)S(1)} collective-permute-done((bf16[8,3584]{1,0:T(8,128)(2,1)S(1)}, bf16[8,3584]{1,0:T(8,128)(2,1)S(1)}, u32[]{:S(2)}, u32[]{:S(2)}) %collective-permute-start.13) | collective-permute-done | bytes 57376 | tf_op jit(solution)/shard_map/ppermute | solution.py:357
  48.1 1.2 %collective-permute-done.14.refs_1_ = bf16[8,3584]{1,0:T(8,128)(2,1)S(1)} collective-permute-done((bf16[8,3584]{1,0:T(8,128)(2,1)S(1)}, bf16[8,3584]{1,0:T(8,128)(2,1)S(1)}, u32[]{:S(2)}, u32[]{:S(2)}) %collective-permute-start.14) | collective-permute-done | bytes 57376 | tf_op jit(solution)/shard_map/ppermute | solution.py:357
  49.4 0.0 collective-permute-done.15.refs_2_
  49.4 0.0 collective-permute-done.16.refs_5_
  49.4 0.2 shard_map.139
  49.5 0.6 collective-permute-start.17
  50.1 0.0 collective-permute-done.18.refs_0_
  50.1 1.2 %copy-done = bf16[3584,256]{1,0:T(8,128)(2,1)} copy-done((bf16[3584,256]{1,0:T(8,128)(2,1)}, bf16[3584,256]{1,0:T(8,128)(2,1)S(1)}, u32[]{:S(2)}) %copy-start) | copy-done | bytes 1835032
  51.4 1.5 %shard_map.140.refs_3_ = bf16[3584,256]{1,0:T(8,128)(2,1)S(1)} custom-call(bf16[3584,256]{1,0:T(8,128)(2,1)} %copy-done, bf16[32,3584]{1,0:T(8,128)(2,1)S(1)} %get-tuple-element.68.refs_1_.refs_0_), custom_call_target="tpu_custom_call" | custom-call | bytes 1835008 | tf_op jit(solution)/shard_map/pallas_call | solution.py:83
  52.9 2.7 %collective-permute-done.17.refs_1_ = bf16[32,3584]{1,0:T(8,128)(2,1)S(1)} collective-permute-done((bf16[32,3584]{1,0:T(8,128)(2,1)S(1)}, bf16[32,3584]{1,0:T(8,128)(2,1)S(1)}, u32[]{:S(2)}, u32[]{:S(2)}) %collective-permute-start.17) | collective-permute-done | bytes 229408 | tf_op jit(solution)/shard_map/ppermute | solution.py:357
  55.6 1.5 %shard_map.141 = (f32[32,2176]{1,0:T(8,128)S(1)}, bf16[32,2176]{1,0:T(8,128)(2,1)S(1)}) custom-call(bf16[32,3584]{1,0:T(8,128)(2,1)S(1)} %get-tuple-element.68.refs_1_.refs_0_, bf16[32,3584]{1,0:T(8,128)(2,1)S(1)} %collective-permute-done.17.refs_1_, bf16[3584,256]{1,0:T(8,128)(2,1)S(1)} %get-tuple-element.69.refs_2_, ...), custom_call_target="tpu_custom_call" | custom-call | tf_op jit(solution)/shard_map/pallas_call | solution.py:83
  57.1 0.6 collective-permute-start.19
  57.7 2.0 %collective-permute-start.23 = (bf16[8,2176]{1,0:T(8,128)(2,1)S(1)}, bf16[8,2176]{1,0:T(8,128)(2,1)S(1)}, u32[]{:S(2)}, u32[]{:S(2)}) collective-permute-start(bf16[8,2176]{1,0:T(8,128)(2,1)S(1)} %get-tuple-element.79), channel_id=1, source_target_pairs={{0,12},{1,13},{2,14},{3,15},{4,8},{5,9},{6,10},{7,11},{8,4},{9,5},... | collective-permute-start | bytes 104456 | tf_op jit(solution)/shard_map/ppermute | solution.py:357
  59.7 0.8 %collective-permute-start.24 = (bf16[8,2176]{1,0:T(8,128)(2,1)S(1)}, bf16[8,2176]{1,0:T(8,128)(2,1)S(1)}, u32[]{:S(2)}, u32[]{:S(2)}) collective-permute-start(bf16[8,2176]{1,0:T(8,128)(2,1)S(1)} %get-tuple-element.80), channel_id=1, source_target_pairs={{0,8},{1,9},{2,10},{3,11},{4,12},{5,13},{6,14},{7,15},{8,0},{9,1},... | collective-permute-start | bytes 104456 | tf_op jit(solution)/shard_map/ppermute | solution.py:357
  60.6 1.6 %collective-permute-start.25 = (bf16[8,2176]{1,0:T(8,128)(2,1)S(1)}, bf16[8,2176]{1,0:T(8,128)(2,1)S(1)}, u32[]{:S(2)}, u32[]{:S(2)}) collective-permute-start(bf16[8,2176]{1,0:T(8,128)(2,1)S(1)} %get-tuple-element.81), channel_id=1, source_target_pairs={{0,4},{1,5},{2,6},{3,7},{4,0},{5,1},{6,2},{7,3},{8,12},{9,13},{10,... | collective-permute-start | bytes 104456 | tf_op jit(solution)/shard_map/ppermute | solution.py:357
  62.1 0.1 collective-permute-done.19.refs_1_
  62.3 0.1 shard_map.142
  62.4 2.1 %collective-permute-start.20 = (bf16[8,2176]{1,0:T(8,128)(2,1)S(1)}, bf16[8,2176]{1,0:T(8,128)(2,1)S(1)}, u32[]{:S(2)}, u32[]{:S(2)}) collective-permute-start(bf16[8,2176]{1,0:T(8,128)(2,1)S(1)} %get-tuple-element.75), channel_id=1, source_target_pairs={{0,12},{1,13},{2,14},{3,15},{4,8},{5,9},{6,10},{7,11},{8,4},{9,5},... | collective-permute-start | bytes 104456 | tf_op jit(solution)/shard_map/ppermute | solution.py:357
  64.5 0.8 %collective-permute-start.21 = (bf16[8,2176]{1,0:T(8,128)(2,1)S(1)}, bf16[8,2176]{1,0:T(8,128)(2,1)S(1)}, u32[]{:S(2)}, u32[]{:S(2)}) collective-permute-start(bf16[8,2176]{1,0:T(8,128)(2,1)S(1)} %get-tuple-element.76), channel_id=1, source_target_pairs={{0,8},{1,9},{2,10},{3,11},{4,12},{5,13},{6,14},{7,15},{8,0},{9,1},... | collective-permute-start | bytes 104456 | tf_op jit(solution)/shard_map/ppermute | solution.py:357
  65.3 0.0 collective-permute-done.23.refs_5_
  65.3 1.6 %collective-permute-start.22 = (bf16[8,2176]{1,0:T(8,128)(2,1)S(1)}, bf16[8,2176]{1,0:T(8,128)(2,1)S(1)}, u32[]{:S(2)}, u32[]{:S(2)}) collective-permute-start(bf16[8,2176]{1,0:T(8,128)(2,1)S(1)} %get-tuple-element.77), channel_id=1, source_target_pairs={{0,4},{1,5},{2,6},{3,7},{4,0},{5,1},{6,2},{7,3},{8,12},{9,13},{10,... | collective-permute-start | bytes 104456 | tf_op jit(solution)/shard_map/ppermute | solution.py:357
  66.9 0.0 collective-permute-done.24.refs_6_
  66.9 0.0 collective-permute-done.25.refs_7_
  66.9 1.3 %collective-permute-done.20.refs_1_ = bf16[8,2176]{1,0:T(8,128)(2,1)S(1)} collective-permute-done((bf16[8,2176]{1,0:T(8,128)(2,1)S(1)}, bf16[8,2176]{1,0:T(8,128)(2,1)S(1)}, u32[]{:S(2)}, u32[]{:S(2)}) %collective-permute-start.20) | collective-permute-done | bytes 34848 | tf_op jit(solution)/shard_map/ppermute | solution.py:357
  68.2 1.4 %collective-permute-done.21.refs_2_ = bf16[8,2176]{1,0:T(8,128)(2,1)S(1)} collective-permute-done((bf16[8,2176]{1,0:T(8,128)(2,1)S(1)}, bf16[8,2176]{1,0:T(8,128)(2,1)S(1)}, u32[]{:S(2)}, u32[]{:S(2)}) %collective-permute-start.21) | collective-permute-done | bytes 34848 | tf_op jit(solution)/shard_map/ppermute | solution.py:357
  69.6 0.0 collective-permute-done.22.refs_3_
  69.6 0.8 %shard_map.143 = (f32[1,8]{1,0:T(1,128)}, f32[8,2048]{1,0:T(8,128)}) custom-call(f32[8,2176]{1,0:T(8,128)S(1)} %get-tuple-element.74.refs_0_, bf16[8,2176]{1,0:T(8,128)(2,1)S(1)} %collective-permute-done.20.refs_1_, bf16[8,2176]{1,0:T(8,128)(2,1)S(1)} %collective-permute-done.21.refs_2_, bf16[8,2176]{1,0:T(8,128)(2,1)S(1)} %collective-permute-done.22.refs_3_, ...), custom_call_target="tpu_custom_call" | custom-call | tf_op jit(solution)/shard_map/pallas_call | solution.py:83
  (3 shorter events, 0.0 us)
Async XLA Ops:
  0.6 15.1 %collective-permute-start.5 = (bf16[2048,256]{1,0:T(8,128)(2,1)}, bf16[2048,256]{1,0:T(8,128)(2,1)S(1)}, u32[]{:S(2)}, u32[]{:S(2)}) collective-permute-start(bf16[2048,256]{1,0:T(8,128)(2,1)} %refs_4_.3), channel_id=1, source_target_pairs={{0,1},{1,0},{2,3},{3,2},{4,5},{5,4},{6,7},{7,6},{8,9},{9,8},{10,11... | collective-permute-start | bytes 3145736 | tf_op jit(solution)/shard_map/ppermute | solution.py:357
  1.1 49.0 %collective-permute-start.18 = (bf16[3584,256]{1,0:T(8,128)(2,1)}, bf16[3584,256]{1,0:T(8,128)(2,1)S(1)}, u32[]{:S(2)}, u32[]{:S(2)}) collective-permute-start(bf16[3584,256]{1,0:T(8,128)(2,1)} %refs_8_.1), channel_id=1, source_target_pairs={{0,1},{1,0},{2,3},{3,2},{4,5},{5,4},{6,7},{7,6},{8,9},{9,8},{10,11... | collective-permute-start | bytes 5505032 | tf_op jit(solution)/shard_map/ppermute | solution.py:357
  2.4 7.5 %collective-permute-start = (bf16[8,3712]{1,0:T(8,128)(2,1)S(1)}, bf16[8,3712]{1,0:T(8,128)(2,1)S(1)}, u32[]{:S(2)}, u32[]{:S(2)}) collective-permute-start(bf16[8,3712]{1,0:T(8,128)(2,1)S(1)} %get-tuple-element.43), channel_id=1, source_target_pairs={{0,12},{1,13},{2,14},{3,15},{4,8},{5,9},{6,10},{7,11},{8,4},{9,5},... | collective-permute-start | bytes 178184 | tf_op jit(solution)/shard_map/ppermute | solution.py:357
  7.5 5.4 %collective-permute-start.1 = (bf16[8,3712]{1,0:T(8,128)(2,1)S(1)}, bf16[8,3712]{1,0:T(8,128)(2,1)S(1)}, u32[]{:S(2)}, u32[]{:S(2)}) collective-permute-start(bf16[8,3712]{1,0:T(8,128)(2,1)S(1)} %get-tuple-element.44), channel_id=1, source_target_pairs={{0,8},{1,9},{2,10},{3,11},{4,12},{5,13},{6,14},{7,15},{8,0},{9,1},... | collective-permute-start | bytes 178184 | tf_op jit(solution)/shard_map/ppermute | solution.py:357
  7.5 5.4 %collective-permute-start.2 = (bf16[8,3712]{1,0:T(8,128)(2,1)S(1)}, bf16[8,3712]{1,0:T(8,128)(2,1)S(1)}, u32[]{:S(2)}, u32[]{:S(2)}) collective-permute-start(bf16[8,3712]{1,0:T(8,128)(2,1)S(1)} %get-tuple-element.45), channel_id=1, source_target_pairs={{0,4},{1,5},{2,6},{3,7},{4,0},{5,1},{6,2},{7,3},{8,12},{9,13},{10,... | collective-permute-start | bytes 178184 | tf_op jit(solution)/shard_map/ppermute | solution.py:357
  12.9 7.5 %collective-permute-start.3 = (bf16[32,3712]{1,0:T(8,128)(2,1)S(1)}, bf16[32,3712]{1,0:T(8,128)(2,1)S(1)}, u32[]{:S(2)}, u32[]{:S(2)}) collective-permute-start(bf16[32,3712]{1,0:T(8,128)(2,1)S(1)} %shard_map.132.refs_11_.refs_1_), channel_id=1, source_target_pairs={{0,2},{1,3},{2,0},{3,1},{4,6},{5,7},{6,4},{7,5},{8,10},{9,11},{10,... | collective-permute-start | bytes 712712 | tf_op jit(solution)/shard_map/ppermute | solution.py:357
  14.5 1.3 %collective-permute-start.4 = (bf16[144,256]{1,0:T(8,128)(2,1)S(1)}, bf16[144,256]{1,0:T(8,128)(2,1)S(1)}, u32[]{:S(2)}, u32[]{:S(2)}) collective-permute-start(bf16[144,256]{1,0:T(8,128)(2,1)S(1)} %get-tuple-element.47.refs_1_), channel_id=1, source_target_pairs={{0,1},{1,0},{2,3},{3,2},{4,5},{5,4},{6,7},{7,6},{8,9},{9,8},{10,11... | collective-permute-start | bytes 221192 | tf_op jit(solution)/shard_map/ppermute | solution.py:357
  14.5 6.0 %collective-permute-start.6 = (bf16[32,3712]{1,0:T(8,128)(2,1)S(1)}, bf16[32,3712]{1,0:T(8,128)(2,1)S(1)}, u32[]{:S(2)}, u32[]{:S(2)}) collective-permute-start(bf16[32,3712]{1,0:T(8,128)(2,1)S(1)} %shard_map.132.refs_11_.refs_1_), channel_id=1, source_target_pairs={{0,1},{1,0},{2,3},{3,2},{4,5},{5,4},{6,7},{7,6},{8,9},{9,8},{10,11... | collective-permute-start | bytes 712712 | tf_op jit(solution)/shard_map/ppermute | solution.py:357
  20.4 1.6 %collective-permute-start.7 = (bf16[32,3712]{1,0:T(8,128)(2,1)S(1)}, bf16[32,3712]{1,0:T(8,128)(2,1)S(1)}, u32[]{:S(2)}, u32[]{:S(2)}) collective-permute-start(bf16[32,3712]{1,0:T(8,128)(2,1)S(1)} %shard_map.134.refs_2_), channel_id=1, source_target_pairs={{0,1},{1,0},{2,3},{3,2},{4,5},{5,4},{6,7},{7,6},{8,9},{9,8},{10,11... | collective-permute-start | bytes 712712 | tf_op jit(solution)/shard_map/ppermute | solution.py:357
  23.0 1.9 %collective-permute-start.8 = (bf16[64,3584]{1,0:T(8,128)(2,1)S(1)}, bf16[64,3584]{1,0:T(8,128)(2,1)S(1)}, u32[]{:S(2)}, u32[]{:S(2)}) collective-permute-start(bf16[64,3584]{1,0:T(8,128)(2,1)S(1)} %get-tuple-element.53), channel_id=1, source_target_pairs={{0,1},{1,0},{2,3},{3,2},{4,5},{5,4},{6,7},{7,6},{8,9},{9,8},{10,11... | collective-permute-start | bytes 1376264 | tf_op jit(solution)/shard_map/ppermute | solution.py:357
  25.0 7.7 %collective-permute-start.9 = (bf16[32,3584]{1,0:T(8,128)(2,1)S(1)}, bf16[32,3584]{1,0:T(8,128)(2,1)S(1)}, u32[]{:S(2)}, u32[]{:S(2)}) collective-permute-start(bf16[32,3584]{1,0:T(8,128)(2,1)S(1)} %get-tuple-element.55), channel_id=1, source_target_pairs={{0,2},{1,3},{2,0},{3,1},{4,6},{5,7},{6,4},{7,5},{8,10},{9,11},{10,... | collective-permute-start | bytes 688136 | tf_op jit(solution)/shard_map/ppermute | solution.py:357
  32.7 6.4 %collective-permute-start.10 = (bf16[8,3584]{1,0:T(8,128)(2,1)S(1)}, bf16[8,3584]{1,0:T(8,128)(2,1)S(1)}, u32[]{:S(2)}, u32[]{:S(2)}) collective-permute-start(bf16[8,3584]{1,0:T(8,128)(2,1)S(1)} %get-tuple-element.57), channel_id=1, source_target_pairs={{0,12},{1,13},{2,14},{3,15},{4,8},{5,9},{6,10},{7,11},{8,4},{9,5},... | collective-permute-start | bytes 172040 | tf_op jit(solution)/shard_map/ppermute | solution.py:357
  34.8 5.6 %collective-permute-start.11 = (bf16[8,3584]{1,0:T(8,128)(2,1)S(1)}, bf16[8,3584]{1,0:T(8,128)(2,1)S(1)}, u32[]{:S(2)}, u32[]{:S(2)}) collective-permute-start(bf16[8,3584]{1,0:T(8,128)(2,1)S(1)} %get-tuple-element.58), channel_id=1, source_target_pairs={{0,8},{1,9},{2,10},{3,11},{4,12},{5,13},{6,14},{7,15},{8,0},{9,1},... | collective-permute-start | bytes 172040 | tf_op jit(solution)/shard_map/ppermute | solution.py:357
  34.8 5.6 %collective-permute-start.12 = (bf16[8,3584]{1,0:T(8,128)(2,1)S(1)}, bf16[8,3584]{1,0:T(8,128)(2,1)S(1)}, u32[]{:S(2)}, u32[]{:S(2)}) collective-permute-start(bf16[8,3584]{1,0:T(8,128)(2,1)S(1)} %get-tuple-element.59), channel_id=1, source_target_pairs={{0,4},{1,5},{2,6},{3,7},{4,0},{5,1},{6,2},{7,3},{8,12},{9,13},{10,... | collective-permute-start | bytes 172040 | tf_op jit(solution)/shard_map/ppermute | solution.py:357
  40.6 8.8 %collective-permute-start.16 = (bf16[32,2176]{1,0:T(8,128)(2,1)S(1)}, bf16[32,2176]{1,0:T(8,128)(2,1)S(1)}, u32[]{:S(2)}, u32[]{:S(2)}) collective-permute-start(bf16[32,2176]{1,0:T(8,128)(2,1)S(1)} %get-tuple-element.67), channel_id=1, source_target_pairs={{0,2},{1,3},{2,0},{3,1},{4,6},{5,7},{6,4},{7,5},{8,10},{9,11},{10,... | collective-permute-start | bytes 417800 | tf_op jit(solution)/shard_map/ppermute | solution.py:357
  42.2 6.0 %collective-permute-start.13 = (bf16[8,3584]{1,0:T(8,128)(2,1)S(1)}, bf16[8,3584]{1,0:T(8,128)(2,1)S(1)}, u32[]{:S(2)}, u32[]{:S(2)}) collective-permute-start(bf16[8,3584]{1,0:T(8,128)(2,1)S(1)} %get-tuple-element.63), channel_id=1, source_target_pairs={{0,12},{1,13},{2,14},{3,15},{4,8},{5,9},{6,10},{7,11},{8,4},{9,5},... | collective-permute-start | bytes 172040 | tf_op jit(solution)/shard_map/ppermute | solution.py:357
  44.0 5.4 %collective-permute-start.14 = (bf16[8,3584]{1,0:T(8,128)(2,1)S(1)}, bf16[8,3584]{1,0:T(8,128)(2,1)S(1)}, u32[]{:S(2)}, u32[]{:S(2)}) collective-permute-start(bf16[8,3584]{1,0:T(8,128)(2,1)S(1)} %get-tuple-element.64), channel_id=1, source_target_pairs={{0,8},{1,9},{2,10},{3,11},{4,12},{5,13},{6,14},{7,15},{8,0},{9,1},... | collective-permute-start | bytes 172040 | tf_op jit(solution)/shard_map/ppermute | solution.py:357
  44.5 4.8 %collective-permute-start.15 = (bf16[8,3584]{1,0:T(8,128)(2,1)S(1)}, bf16[8,3584]{1,0:T(8,128)(2,1)S(1)}, u32[]{:S(2)}, u32[]{:S(2)}) collective-permute-start(bf16[8,3584]{1,0:T(8,128)(2,1)S(1)} %get-tuple-element.65), channel_id=1, source_target_pairs={{0,4},{1,5},{2,6},{3,7},{4,0},{5,1},{6,2},{7,3},{8,12},{9,13},{10,... | collective-permute-start | bytes 172040 | tf_op jit(solution)/shard_map/ppermute | solution.py:357
  49.5 6.1 %collective-permute-start.17 = (bf16[32,3584]{1,0:T(8,128)(2,1)S(1)}, bf16[32,3584]{1,0:T(8,128)(2,1)S(1)}, u32[]{:S(2)}, u32[]{:S(2)}) collective-permute-start(bf16[32,3584]{1,0:T(8,128)(2,1)S(1)} %get-tuple-element.68.refs_1_.refs_0_), channel_id=1, source_target_pairs={{0,2},{1,3},{2,0},{3,1},{4,6},{5,7},{6,4},{7,5},{8,10},{9,11},{10,... | collective-permute-start | bytes 688136 | tf_op jit(solution)/shard_map/ppermute | solution.py:357
  50.1 1.3 %copy-start = (bf16[3584,256]{1,0:T(8,128)(2,1)}, bf16[3584,256]{1,0:T(8,128)(2,1)S(1)}, u32[]{:S(2)}) copy-start(bf16[3584,256]{1,0:T(8,128)(2,1)S(1)} %collective-permute-done.18.refs_0_) | copy-start | bytes 5505028
  57.1 5.1 %collective-permute-start.19 = (bf16[32,2176]{1,0:T(8,128)(2,1)S(1)}, bf16[32,2176]{1,0:T(8,128)(2,1)S(1)}, u32[]{:S(2)}, u32[]{:S(2)}) collective-permute-start(bf16[32,2176]{1,0:T(8,128)(2,1)S(1)} %get-tuple-element.73), channel_id=1, source_target_pairs={{0,2},{1,3},{2,0},{3,1},{4,6},{5,7},{6,4},{7,5},{8,10},{9,11},{10,... | collective-permute-start | bytes 417800 | tf_op jit(solution)/shard_map/ppermute | solution.py:357
  57.7 7.6 %collective-permute-start.23 = (bf16[8,2176]{1,0:T(8,128)(2,1)S(1)}, bf16[8,2176]{1,0:T(8,128)(2,1)S(1)}, u32[]{:S(2)}, u32[]{:S(2)}) collective-permute-start(bf16[8,2176]{1,0:T(8,128)(2,1)S(1)} %get-tuple-element.79), channel_id=1, source_target_pairs={{0,12},{1,13},{2,14},{3,15},{4,8},{5,9},{6,10},{7,11},{8,4},{9,5},... | collective-permute-start | bytes 104456 | tf_op jit(solution)/shard_map/ppermute | solution.py:357
  59.7 7.1 %collective-permute-start.24 = (bf16[8,2176]{1,0:T(8,128)(2,1)S(1)}, bf16[8,2176]{1,0:T(8,128)(2,1)S(1)}, u32[]{:S(2)}, u32[]{:S(2)}) collective-permute-start(bf16[8,2176]{1,0:T(8,128)(2,1)S(1)} %get-tuple-element.80), channel_id=1, source_target_pairs={{0,8},{1,9},{2,10},{3,11},{4,12},{5,13},{6,14},{7,15},{8,0},{9,1},... | collective-permute-start | bytes 104456 | tf_op jit(solution)/shard_map/ppermute | solution.py:357
  60.6 6.3 %collective-permute-start.25 = (bf16[8,2176]{1,0:T(8,128)(2,1)S(1)}, bf16[8,2176]{1,0:T(8,128)(2,1)S(1)}, u32[]{:S(2)}, u32[]{:S(2)}) collective-permute-start(bf16[8,2176]{1,0:T(8,128)(2,1)S(1)} %get-tuple-element.81), channel_id=1, source_target_pairs={{0,4},{1,5},{2,6},{3,7},{4,0},{5,1},{6,2},{7,3},{8,12},{9,13},{10,... | collective-permute-start | bytes 104456 | tf_op jit(solution)/shard_map/ppermute | solution.py:357
  62.4 5.8 %collective-permute-start.20 = (bf16[8,2176]{1,0:T(8,128)(2,1)S(1)}, bf16[8,2176]{1,0:T(8,128)(2,1)S(1)}, u32[]{:S(2)}, u32[]{:S(2)}) collective-permute-start(bf16[8,2176]{1,0:T(8,128)(2,1)S(1)} %get-tuple-element.75), channel_id=1, source_target_pairs={{0,12},{1,13},{2,14},{3,15},{4,8},{5,9},{6,10},{7,11},{8,4},{9,5},... | collective-permute-start | bytes 104456 | tf_op jit(solution)/shard_map/ppermute | solution.py:357
  64.5 5.1 %collective-permute-start.21 = (bf16[8,2176]{1,0:T(8,128)(2,1)S(1)}, bf16[8,2176]{1,0:T(8,128)(2,1)S(1)}, u32[]{:S(2)}, u32[]{:S(2)}) collective-permute-start(bf16[8,2176]{1,0:T(8,128)(2,1)S(1)} %get-tuple-element.76), channel_id=1, source_target_pairs={{0,8},{1,9},{2,10},{3,11},{4,12},{5,13},{6,14},{7,15},{8,0},{9,1},... | collective-permute-start | bytes 104456 | tf_op jit(solution)/shard_map/ppermute | solution.py:357
  65.3 4.3 %collective-permute-start.22 = (bf16[8,2176]{1,0:T(8,128)(2,1)S(1)}, bf16[8,2176]{1,0:T(8,128)(2,1)S(1)}, u32[]{:S(2)}, u32[]{:S(2)}) collective-permute-start(bf16[8,2176]{1,0:T(8,128)(2,1)S(1)} %get-tuple-element.77), channel_id=1, source_target_pairs={{0,4},{1,5},{2,6},{3,7},{4,0},{5,1},{6,2},{7,3},{8,12},{9,13},{10,... | collective-permute-start | bytes 104456 | tf_op jit(solution)/shard_map/ppermute | solution.py:357

commit v4 on v3

--- a/solution.py
+++ b/solution.py
@@ -65,7 +65,7 @@
     return values, top, totals
 
 
-def call(body, outs, *args, scratch=(), scalars=0, after=(), far=0, near=True, near_out=True, limit=12, cost=None):
+def call(body, outs, *args, scratch=(), scalars=0, after=(), far=0, near=True, near_out=True, limit=12, cost=None, aliases=None):
     smem = pl.BlockSpec(memory_space=pltpu.SMEM)
     vmem = pl.BlockSpec(memory_space=pltpu.VMEM)
     hbm = pl.BlockSpec(memory_space=pltpu.HBM)
@@ -86,6 +86,7 @@
         in_specs=[smem] * scalars + [vmem] * middle + [hbm] * far + [unread] * len(after),
         out_specs=[vmem] * len(outs),
         scratch_shapes=list(scratch),
+        input_output_aliases=aliases or {},
         compiler_params=pltpu.CompilerParams(vmem_limit_bytes=(limit if near else 56) * 2**20),
         cost_estimate=cost and pl.CostEstimate(flops=cost[0], bytes_accessed=cost[1], transcendentals=0),
     )(*args, *after)
@@ -101,8 +102,9 @@
     return copies
 
 
-def fetch_body(source, target, semaphores):
-    for copy in fetch((source,), (target,), semaphores):
+def fetch_body(*refs):
+    *refs, semaphores = refs
+    for copy in fetch(refs[: len(refs) // 2], refs[len(refs) // 2 :], semaphores):
         copy.wait()
 
 
@@ -110,77 +112,44 @@
     return values * lax.rsqrt(jnp.mean(values * values, axis=-1, keepdims=True) + EPSILON) * gain[None, :]
 
 
-def enter_body(tokens_far, gain_far, ids_far, scores_far, logits_far, map_far, *refs):
-    *outs, entries, tokens, gain, ids, scores, vocab_map, semaphores = refs
-    count = logits_far.shape[0]
-    copies = fetch(
-        (ids_far, scores_far, tokens_far, gain_far, map_far, logits_far),
-        (ids, scores, tokens, gain, vocab_map, entries.at[:count]),
-        semaphores,
-    )
-    for copy in copies[:2]:
-        copy.wait()
-    rows, features = tokens.shape
-    diagonal = lax.broadcasted_iota(jnp.int32, (rows, rows), 0) == lax.broadcasted_iota(
-        jnp.int32, (rows, rows), 1
-    )
-    lane = lanes(rows) % 64
-    block = jnp.zeros(lane.shape, F32)
-    total = jnp.zeros((rows, 1), F32)
-    for k in range(ids.shape[0]):
-        chosen = jnp.where(diagonal, ids[k : k + 1, :].astype(F32), 0.0)
-        chosen = jnp.sum(chosen, axis=1, keepdims=True)
-        score = jnp.where(diagonal, scores[k : k + 1, :], 0.0)
-        score = jnp.sum(score, axis=1, keepdims=True)
-        block = block + jnp.where(lane.astype(F32) == chosen, score, 0.0)
-        total = total + score
-    block = block / total
-    high = block.astype(BF16).astype(F32)
-    table = jnp.where(lanes(rows) < 64, high, block - high).astype(BF16)
-    for copy in copies[2:]:
-        copy.wait()
-    normed = normed_rows(tokens[...].astype(F32), gain[...]).astype(BF16)
-    for out in outs:
-        out[:, :features] = normed
-        out[:, features:] = table
-    places = vocab_map[...].astype(F32)[None, :]
-    entries[count:, :] = jnp.broadcast_to(places, (16, places.shape[1])).astype(BF16)
-
-
 def paired(out):
     return [slice(at, at + 16) for at in range(0, out.shape[0], 16)]
 
 
-def join_body(*refs):
+def join_body(turns, *refs):
     *parts, out = refs
-    for rows, pair in zip(paired(out), zip(*[iter(reversed(parts))] * 2)):
+    parts = [parts[i] for i in turns]
+    for rows, pair in zip(paired(out), zip(*[iter(parts)] * 2)):
         out[rows, :] = jnp.concatenate([p[...].astype(F32) for p in pair]).astype(BF16)
 
 
-def experts_body(slices, parts, me, *refs):
+def join_normed_body(turns, gain, *refs):
+    *parts, out = refs
+    parts = [parts[i] for i in turns]
+    for rows, pair in zip(paired(out), zip(*[iter(parts)] * 2)):
+        joined = jnp.concatenate([p[...].astype(F32) for p in pair])
+        out[rows, :] = normed_rows(joined, gain[...]).astype(BF16)
+
+
+def experts_body(parts, *refs):
     inputs, (w_gate, w_up, w_down, keep, send, rows_ref) = refs[:parts], refs[parts:]
     count = inputs[0].shape[0]
     features = w_gate.shape[1]
     for i, ref in enumerate(inputs):
         rows_ref[i * count : (i + 1) * count, :] = ref[:, : rows_ref.shape[1]]
-    expert = me[0] // slices
 
     def block(start, size):
-        rows = rows_ref[pl.ds(start, size), :features]
+        rows = rows_ref[pl.ds(start, size), :]
         gate = dot(rows, w_gate[0])
         up = dot(rows, w_up[0])
-        lane = lanes(size) % 64
-        table = rows_ref[pl.ds(start, size), features:].astype(F32)
-        weight = jnp.sum(jnp.where(lane == expert, table, 0.0), axis=1, keepdims=True)
-        activated = (gate / (1.0 + jnp.exp(-gate)) * up).astype(BF16)
-        return activated, weight
+        return (gate / (1.0 + jnp.exp(-gate)) * up).astype(BF16)
 
     half = parts * count // 2
     if half < BLOCK:
-        activated, weight = block(0, 2 * half)
+        activated = block(0, 2 * half)
         step = 512
         for at in range(0, features, step):
-            out = dot(activated, w_down[0, :, at : at + step]) * weight
+            out = dot(activated, w_down[0, :, at : at + step])
             keep[:, at : at + step] = out[:half]
             send[:, at : at + step] = out[half:].astype(BF16)
     else:
@@ -189,8 +158,8 @@
             @pl.loop(0, half // BLOCK)
             def _(i):
                 start = pl.multiple_of(i * BLOCK, BLOCK)
-                activated, weight = block(h * half + start, BLOCK)
-                out = dot(activated, w_down[0]) * weight
+                activated = block(h * half + start, BLOCK)
+                out = dot(activated, w_down[0])
                 target[pl.ds(start, BLOCK), :] = out.astype(target.dtype)
 
 
@@ -204,61 +173,101 @@
         send[...] = total[at : at + rows].astype(BF16)
 
 
-def hidden_body(received, passing, *refs):
-    parts, (tokens, gain, *refs) = refs[: received + 1], refs[received + 1 :]
+def hidden_body(offsets, slices, passing, me, *refs):
+    parts, (tokens, gain, ids, scores, *refs) = refs[: len(offsets)], refs[len(offsets) :]
     passed, outs = refs[:passing], refs[passing:]
-    total = sum((ref[...].astype(F32) for ref in parts[1:]), parts[0][...])
-    normed = normed_rows(tokens[...].astype(F32) + total, gain[...]).astype(BF16)
+    rows = tokens.shape[0]
+    diagonal = lax.broadcasted_iota(jnp.int32, (rows, rows), 0) == lax.broadcasted_iota(
+        jnp.int32, (rows, rows), 1
+    )
+
+    def down(values):
+        return jnp.sum(jnp.where(diagonal, values, 0.0), axis=1, keepdims=True)
+
+    chosen = [down(ids[k : k + 1, :].astype(F32)) for k in range(ids.shape[0])]
+    score = [down(scores[k : k + 1, :]) for k in range(ids.shape[0])]
+    whole = sum(score)
+    total = tokens[...].astype(F32)
+    for ref, offset in zip(parts, offsets):
+        expert = ((me[0] ^ offset) // slices).astype(F32)
+        weight = sum(jnp.where(c == expert, v, 0.0) for c, v in zip(chosen, score)) / whole
+        total = total + ref[...].astype(F32) * weight
+    normed = normed_rows(total, gain[...]).astype(BF16)
     for out in outs[: len(outs) - passing]:
         out[...] = normed
     for source, target in zip(passed, outs[len(outs) - passing :]):
         target[...] = source[...]
 
 
-def student_body(devices, order, prefetched, me, ours, theirs, their_head, head_far, *refs):
+def student_body(devices, order, prefetched, me, their_map, their_logits, their_head, *refs):
+    (map_far, logits_far, head_far, *refs) = refs
     sources, (moved, moved_head, *refs) = refs[:prefetched], refs[prefetched:]
-    outs = len(refs) - prefetched - 3
-    parts, targets, (head, scratch, semaphores) = (
-        refs[:outs],
-        refs[outs : outs + prefetched],
-        refs[outs + prefetched :],
-    )
-    copies = fetch((head_far, *sources), (head, *targets), semaphores)
-    copies[0].wait()
-    count = scratch.shape[0]
+    parts = refs[: len(refs) - prefetched - 5]
+    refs = refs[len(parts) :]
+    targets, (own_map, logits, head, scratch, semaphores) = refs[:prefetched], refs[prefetched:]
+    copies = fetch(
+        (map_far, logits_far, head_far, *sources), (own_map, logits, head, *targets), semaphores
+    )
+    for copy in copies[:3]:
+        copy.wait()
     entries = head.shape[1]
-    tok_dev = count // devices
-    for i, (rows, weights) in enumerate(((ours, head), (theirs, their_head))):
+    tok_dev = logits.shape[0] // devices
+    own, other = (own_map, logits, head), (their_map, their_logits, their_head)
+    for i, (places, rows, weights) in enumerate((own, other)):
         cols = slice(i * entries, (i + 1) * entries)
-        index = lax.broadcasted_iota(jnp.int32, (entries, entries), 0).astype(F32)
-        place = index == rows[count:, :].astype(F32)[:1, :]
+        place = lax.broadcasted_iota(jnp.int32, (entries, entries), 0) == places[...]
         place = jnp.where(place, 1.0, 0.0).astype(BF16)
-        scratch[:, cols] = dot_t(rows[:count, :], place)
+        scratch[:, cols] = dot_t(rows[...], place)
         moved_head[:, cols] = dot_t(weights[...], place).astype(BF16)
     for slot, offset in enumerate(order):
         source = pl.multiple_of((me[0] ^ offset) * tok_dev, tok_dev)
         moved[slot * tok_dev : (slot + 1) * tok_dev, :] = scratch[pl.ds(source, tok_dev), :]
+
+    width = moved_head.shape[0]
+    student_part(moved, moved_head, parts, 0, late(width))
+
+    @pl.when(me[0] % 2 == 1)
+    def _():
+        student_part(moved, moved_head, parts, late(width), width)
+
+    for copy in copies[3:]:
+        copy.wait()
+
+
+def late(width):
+    return width - width // 2 // BLOCK * BLOCK
+
+
+def student_part(moved, moved_head, targets, start, stop):
     step = min(moved.shape[0], BLOCK)
     for at in range(0, moved.shape[0], step):
         student = moved[at : at + step, :]
         top = jnp.max(student, axis=1, keepdims=True)
         exps = jnp.exp(student - top)
         total = jnp.sum(exps, axis=1, keepdims=True)
-        emit(at, step, exps, moved_head, [top, total, jnp.zeros_like(top)], parts)
-    for copy in copies[1:]:
-        copy.wait()
-
-
-def emit(at, step, exps, head, columns, targets):
+        emit(at, step, exps, moved_head, [top, total, jnp.zeros_like(top)], targets, start, stop)
+
+
+def add_student_body(parts, received, me, moved, moved_head, *refs):
+    summands, refs = refs[: received + 1], refs[received + 1 + parts :]
+    add_split_body(received, *summands, *refs[:-parts])
+
+    @pl.when(me[0] % 2 == 0)
+    def _():
+        width = moved_head.shape[0]
+        student_part(moved, moved_head, refs[-parts:], late(width), width)
+
+
+def emit(at, step, exps, head, columns, targets, start, stop):
     stats = pack(columns)
-    values = dot_t(exps.astype(BF16), head[...])
+    values = dot_t(exps.astype(BF16), head[start:stop, :])
     width = head.shape[0]
     for i, target in enumerate(targets):
         rows = target.shape[0]
         low, high = max(at, i * rows), min(at + step, (i + 1) * rows)
         if low < high:
             inner, outer = slice(low - at, high - at), slice(low - i * rows, high - i * rows)
-            target[outer, :width] = values[inner].astype(target.dtype)
+            target[outer, start:stop] = values[inner].astype(target.dtype)
             target[outer, width:] = stats[inner] if i == 0 else split(stats[inner])
 
 
@@ -276,7 +285,7 @@
         exps = jnp.exp(teacher - top)
         total = jnp.sum(exps, axis=1, keepdims=True)
         cross = jnp.sum(exps * (teacher - student), axis=1, keepdims=True)
-        emit(at, step, exps, moved_head, [top, total, cross], targets)
+        emit(at, step, exps, moved_head, [top, total, cross], targets, 0, moved_head.shape[0])
 
 
 def combine_split_body(received, *refs):
@@ -300,10 +309,10 @@
         target[...] = source[...]
 
 
-def join_both_body(size_z, size_x, *refs):
-    parts, refs = refs[:size_z], refs[size_z:]
+def join_both_body(turns, size_x, *refs):
+    parts, refs = refs[: len(turns)], refs[len(turns) :]
     student, (out, *outs) = refs[:size_x], refs[size_x:]
-    join_body(*parts, out)
+    join_body(turns, *parts, out)
     combine_split_body(size_x - 1, *student, *outs)
 
 
@@ -356,19 +365,17 @@
     def swap(values, offset):
         return lax.ppermute(values, "expert", [(i, i ^ offset) for i in range(devices)])
 
-    def along_z(rows):
-        far = [swap(a, kz * 2 * size_x) for kz, a in reversed(list(enumerate(rows))[1:])]
-        return [*far, rows[0]]
+    def places(turn):
+        return [list(turn).index(kz) if kz else len(turn) for kz in range(size_z)]
+
+    def along_z(rows, turn):
+        return [*(swap(rows[kz], kz * 2 * size_x) for kz in turn), rows[0]]
 
     def along_x(column):
         return [column] + [swap(column, kx * 2) for kx in range(1, size_x)]
 
     def over_cores(plane):
         return plane + [swap(part, 1) for part in plane]
-
-    def add_cores(keep, send, body, after=()):
-        outs = [((quarter, keep.shape[1]), d) for d in [F32] + [BF16] * (size_x - 1)]
-        return run(functools.partial(body, 1), outs, keep, swap(send, 1), after=after)
 
     def add_x(keep, sends, body, after=()):
         outs = [((tok_dev, keep.shape[1]), d) for d in [F32] + [BF16] * (size_z - 1)]
@@ -380,31 +387,27 @@
     def from_z(keep, sends):
         return [keep] + [swap(s, 2 * size_x * (size_z - 1 - i)) for i, s in enumerate(sends)]
 
-    *messages, ours = run(
-        enter_body,
-        [((tok_dev, features + BLOCK), BF16)] * size_z + [((all_rows + 16, entries), BF16)],
-        tokens,
-        moe_gain,
-        expert_ids.T,
-        gate_scores.T,
-        student_logits,
-        vocab_map,
-        scratch=[
-            pltpu.VMEM((tok_dev, features), BF16),
-            pltpu.VMEM((features,), F32),
-            pltpu.VMEM(expert_ids.T.shape, jnp.int32),
-            pltpu.VMEM(expert_ids.T.shape, F32),
-            pltpu.VMEM((entries,), jnp.int32),
-            pltpu.SemaphoreType.DMA((6,)),
-        ],
-        far=6,
-    )
-    (column_rows,) = run(join_body, [((quarter, features + BLOCK), BF16)], *along_z(messages))
+    turn = list(range(size_z - 1, 0, -1))
+    first_turn = [size_z - 1, *range(1, size_z - 1)]
+    parts = along_z([tokens] * size_z, first_turn)
+    if near:
+        moe_gain, tokens = run(
+            fetch_body,
+            [(moe_gain.shape, F32), (tokens.shape, BF16)],
+            moe_gain,
+            tokens,
+            scratch=[pltpu.SemaphoreType.DMA((2,))],
+            far=2,
+            after=parts[:1],
+        )
+        parts[-1] = tokens
+    (column_rows,) = run(
+        functools.partial(join_normed_body, places(first_turn)), [((quarter, features), BF16)], moe_gain, *parts)
     plane = along_x(column_rows)
-    theirs = swap(ours, 1)
+    own_map = vocab_map.reshape(1, -1)
+    theirs = [swap(a, 1) for a in (own_map, student_logits, student_head)]
     their_teacher = swap(teacher_head, 1)
-    their_head = swap(student_head, 1)
-    prefetched = [w_gate, w_up, w_down, teacher_head, tokens, final_gain]
+    prefetched = [w_gate, w_up, w_down, teacher_head, final_gain, expert_ids.T, gate_scores.T]
     fetched = prefetched if near else []
     split_rows = [((quarter, width + BLOCK), d) for d in [F32] + [BF16] * (size_x - 1)]
     split_dev = [((tok_dev, width + BLOCK), d) for d in [F32] + [BF16] * (size_z - 1)]
@@ -417,68 +420,82 @@
             *[(a.shape, a.dtype) for a in fetched],
         ],
         me,
-        ours,
-        theirs,
-        their_head,
+        *theirs,
+        own_map,
+        student_logits,
         student_head,
         *fetched,
         scratch=[
+            pltpu.VMEM((1, entries), jnp.int32),
+            pltpu.VMEM((all_rows, entries), BF16),
             pltpu.VMEM((width, entries), BF16),
             pltpu.VMEM((all_rows, 2 * entries), F32),
-            pltpu.SemaphoreType.DMA((1 + len(fetched),)),
+            pltpu.SemaphoreType.DMA((3 + len(fetched),)),
         ],
         scalars=1,
-        far=1 + len(fetched),
+        far=3 + len(fetched),
         cost=(4 * entries * width * (half + entries), 2 * sum(a.size for a in prefetched)),
         after=[column_rows],
     )
-    moved, moved_head, stud_keep, *stud_sends = outs[: 2 + size_x]
-    w_gate, w_up, w_down, teacher_head, tokens, final_gain = outs[2 + size_x :] if near else prefetched
+    moved, moved_head, *stud_parts = outs[: 2 + size_x]
+    w_gate, w_up, w_down, teacher_head, final_gain, ids, scores = (
+        outs[2 + size_x :] if near else prefetched
+    )
     crossed = run(
-        pass_body, [(p.shape, p.dtype) for p in plane[1:]], *plane[1:], after=[stud_keep]
+        pass_body, [(p.shape, p.dtype) for p in plane[1:]], *plane[1:], after=[moved]
     )
     arrived = over_cores([column_rows, *crossed])
     keep, send = run(
-        functools.partial(experts_body, slices, len(arrived)),
+        functools.partial(experts_body, len(arrived)),
         [((half, features), F32), ((half, features), BF16)],
-        me,
         *arrived,
         w_gate,
         w_up,
         w_down,
-        scratch=[pltpu.VMEM((all_rows, features + BLOCK), BF16)],
+        scratch=[pltpu.VMEM((all_rows, features), BF16)],
+    )
+    outs = run(
+        functools.partial(add_student_body, size_x, 1),
+        [((quarter, features), d) for d in [F32] + [BF16] * (size_x - 1)] + split_rows,
+        me,
+        moved,
+        moved_head,
+        keep,
+        swap(send, 1),
+        *stud_parts,
         scalars=1,
-    )
-    keep, *sends = add_cores(keep, send, add_split_body)
+        aliases={5 + i: size_x + i for i in range(size_x)},
+    )
+    keep, *sends = outs[:size_x]
+    stud_keep, *stud_sends = outs[size_x:]
     summed = from_z(*take(add_x(keep, along(sends), add_split_body)))
     outs = run(
-        functools.partial(hidden_body, len(summed) - 1, len(stud_sends)),
+        functools.partial(
+            hidden_body,
+            [0] + [2 * size_x * kz for kz in range(size_z - 1, 0, -1)],
+            slices,
+            len(stud_sends),
+        ),
         [((tok_dev, features), BF16)] * size_z + [(a.shape, BF16) for a in stud_sends],
+        me,
         *summed,
         tokens,
         final_gain,
+        ids,
+        scores,
         *stud_sends,
+        scalars=1,
     )
     final_norms, stud_sends = outs[:size_z], outs[size_z:]
     column_rows, *outs = run(
-        functools.partial(join_both_body, size_z, size_x),
+        functools.partial(join_both_body, places(turn), size_x),
         [((quarter, features), BF16), *split_dev],
-        *along_z(final_norms),
+        *along_z(final_norms, turn),
         stud_keep,
         *along(stud_sends),
     )
     student = from_z(*take(outs))
     plane = along_x(column_rows)
-    if near:
-        (their_teacher,) = run(
-            fetch_body,
-            [(their_teacher.shape, BF16)],
-            their_teacher,
-            scratch=[pltpu.SemaphoreType.DMA((1,))],
-            far=1,
-            cost=(0, 2 * their_teacher.size),
-            after=[column_rows],
-        )
     keep, *sends = run(
         functools.partial(teacher_body, len(plane)),
         split_rows,

time: 70.6 us -> 69.7 us (0.987)
  waiting for transfers between devices: 27.6 us -> 29.9 us
  local copies, waits for them, and re-layouts: 1.25 us -> 0 us
  Pallas kernels: 10.1 us -> 9.08 us
  starting transfers between devices: 30.7 us -> 29.7 us
    ppermute x26 -> x27, waiting for transfers between devices: 27.6 us -> 29.9 us  [swap(): lax.ppermute(values, 'expert', [(i, i ^ offset) for i in range(devices)])]
    unnamed x2 -> x0, local copies, waits for them, and re-layouts: 1.25 us -> none
    pallas_call x13 -> x12, Pallas kernels: 10.1 us -> 9.08 us  [call(): pl.pallas_call(run, out_shape=[kind(s, d) for s, d in outs], in_specs=[sm...]
    ppermute x26 -> x27, starting transfers between devices: 30.7 us -> 29.7 us  [swap(): lax.ppermute(values, 'expert', [(i, i ^ offset) for i in range(devices)])]
  transfers between devices with their start and end apart: 26 -> 27, of which waited for: 15 -> 14; matrix products, arithmetic and copies ran while one was open for 0% -> 0% of each run, Pallas kernels for 11% -> 10%
where the time goes in v4:
time: 69.7 us; the launch traced here: 69.5 us
  waiting for transfers between devices  29.9 us (43%)
  starting transfers between devices  29.7 us (43%)
  Pallas kernels  9.08 us (13%)
  between operations  0.73 us (1%)
    ppermute x27, waiting for transfers between devices, swap(): lax.ppermute(values, 'expert', [(i, i ^ offset) for i in range(devices)])  29.9 us
    ppermute x27, starting transfers between devices, swap(): lax.ppermute(values, 'expert', [(i, i ^ offset) for i in range(devices)])  29.7 us
    pallas_call x12, Pallas kernels, call(): pl.pallas_call(run, out_shape=[kind(s, d) for s, d in outs], in_specs=[sm...  9.08 us
  transfers between devices with their start and end apart: 27, of which 14 were waited for; matrix products, arithmetic and copies ran while one was open for 0% of the time, Pallas kernels for 10%

profile of v4, /device:TPU:0, one launch (start us, length us, event | category | flops | bytes accessed | tf_op | source)
XLA Modules:
  0.0 69.5 jit_solution(14808152775455088620)
XLA Ops:
  0.6 0.5 collective-permute-start.2
  1.1 0.1 collective-permute-start.19
  1.2 5.0 %collective-permute-start.3 = (bf16[8,3584]{1,0:T(8,128)(2,1)}, bf16[8,3584]{1,0:T(8,128)(2,1)S(1)}, u32[]{:S(2)}, u32[]{:S(2)}) collective-permute-start(bf16[8,3584]{1,0:T(8,128)(2,1)} %refs_1_.1), channel_id=1, source_target_pairs={{0,12},{1,13},{2,14},{3,15},{4,8},{5,9},{6,10},{7,11},{8,4},{9,5},... | collective-permute-start | bytes 172040 | tf_op jit(solution)/shard_map/ppermute | solution.py:366
  6.3 0.0 collective-permute-start.4
  6.3 0.6 collective-permute-start.5
  6.8 2.4 %collective-permute-done.3.refs_2_.refs_1_ = bf16[8,3584]{1,0:T(8,128)(2,1)S(1)} collective-permute-done((bf16[8,3584]{1,0:T(8,128)(2,1)}, bf16[8,3584]{1,0:T(8,128)(2,1)S(1)}, u32[]{:S(2)}, u32[]{:S(2)}) %collective-permute-start.3) | collective-permute-done | bytes 57376 | tf_op jit(solution)/shard_map/ppermute | solution.py:366
  9.2 0.9 %shard_map.131 = (f32[3584]{0:T(1024)S(1)}, bf16[8,3584]{1,0:T(8,128)(2,1)S(1)}) custom-call(f32[3584]{0:T(1024)} %refs_0_.1, bf16[8,3584]{1,0:T(8,128)(2,1)} %refs_1_.1, bf16[8,3584]{1,0:T(8,128)(2,1)S(1)} %collective-permute-done.3.refs_2_.refs_1_), custom_call_target="tpu_custom_call" | custom-call | tf_op jit(solution)/shard_map/pallas_call | solution.py:83
  10.0 1.0 %collective-permute-done.4.refs_2_ = bf16[8,3584]{1,0:T(8,128)(2,1)S(1)} collective-permute-done((bf16[8,3584]{1,0:T(8,128)(2,1)}, bf16[8,3584]{1,0:T(8,128)(2,1)S(1)}, u32[]{:S(2)}, u32[]{:S(2)}) %collective-permute-start.4) | collective-permute-done | bytes 57376 | tf_op jit(solution)/shard_map/ppermute | solution.py:366
  11.0 1.2 %collective-permute-done.5.refs_3_ = bf16[8,3584]{1,0:T(8,128)(2,1)S(1)} collective-permute-done((bf16[8,3584]{1,0:T(8,128)(2,1)}, bf16[8,3584]{1,0:T(8,128)(2,1)S(1)}, u32[]{:S(2)}, u32[]{:S(2)}) %collective-permute-start.5) | collective-permute-done | bytes 57376 | tf_op jit(solution)/shard_map/ppermute | solution.py:366
  12.2 0.2 shard_map.132.refs_14_.refs_0_
  12.3 1.6 %collective-permute-start.6 = (bf16[32,3584]{1,0:T(8,128)(2,1)S(1)}, bf16[32,3584]{1,0:T(8,128)(2,1)S(1)}, u32[]{:S(2)}, u32[]{:S(2)}) collective-permute-start(bf16[32,3584]{1,0:T(8,128)(2,1)S(1)} %shard_map.132.refs_14_.refs_0_), channel_id=1, source_target_pairs={{0,2},{1,3},{2,0},{3,1},{4,6},{5,7},{6,4},{7,5},{8,10},{9,11},{10,... | collective-permute-start | bytes 688136 | tf_op jit(solution)/shard_map/ppermute | solution.py:366
  13.9 0.0 collective-permute-start.1
  13.9 0.5 collective-permute-start
  14.4 1.0 %collective-permute-done.refs_1_ = s32[1,256]{1,0:T(1,128)S(1)} collective-permute-done((s32[1,256]{1,0:T(1,128)}, s32[1,256]{1,0:T(1,128)S(1)}, u32[]{:S(2)}, u32[]{:S(2)}) %collective-permute-start) | collective-permute-done | bytes 1056 | tf_op jit(solution)/shard_map/ppermute | solution.py:366
  15.4 0.3 collective-permute-start.7
  15.7 0.0 collective-permute-done.1.refs_2_
  15.8 0.0 collective-permute-done.2.refs_3_
  15.8 3.6 %shard_map.133 = (f32[64,512]{1,0:T(8,128)S(1)}, bf16[2048,512]{1,0:T(8,128)(2,1)S(1)}, f32[32,2176]{1,0:T(8,128)S(1)}, bf16[32,2176]{1,0:T(8,128)(2,1)S(1)}, bf...) custom-call(s32[1]{0:T(128)} %bitcast.refs_0_, ...), custom_call_target="tpu_custom_call" | custom-call | flops 671088640 | bytes 7347264 | tf_op jit(solution)/shard_map/pallas_call | solution.py:83
  19.4 0.0 collective-permute-done.6.refs_0_
  19.4 0.3 collective-permute-start.8
  19.6 0.0 collective-permute-done.7.refs_2_
  19.7 1.3 %collective-permute-done.8.refs_3_ = bf16[32,3584]{1,0:T(8,128)(2,1)S(1)} collective-permute-done((bf16[32,3584]{1,0:T(8,128)(2,1)S(1)}, bf16[32,3584]{1,0:T(8,128)(2,1)S(1)}, u32[]{:S(2)}, u32[]{:S(2)}) %collective-permute-start.8) | collective-permute-done | bytes 229408 | tf_op jit(solution)/shard_map/ppermute | solution.py:366
  20.9 1.0 %shard_map.135 = (f32[64,3584]{1,0:T(8,128)S(1)}, bf16[64,3584]{1,0:T(8,128)(2,1)S(1)}) custom-call(bf16[32,3584]{1,0:T(8,128)(2,1)S(1)} %shard_map.132.refs_14_.refs_0_, bf16[32,3584]{1,0:T(8,128)(2,1)S(1)} %shard_map.134.refs_1_, bf16[32,3584]{1,0:T(8,128)(2,1)S(1)} %collective-permute-done.7.refs_2_, bf16[32,3584]{1,0:T(8,128)(2,1)S(1)} %collective-permute-done.8.refs_3_, ...), custom_call_target="tpu_custom_call" | custom-call | tf_op jit(solution)/shard_map/pallas_call | solution.py:83
  22.0 0.3 collective-permute-start.9
  22.2 1.6 %collective-permute-done.9.refs_4_ = bf16[64,3584]{1,0:T(8,128)(2,1)S(1)} collective-permute-done((bf16[64,3584]{1,0:T(8,128)(2,1)S(1)}, bf16[64,3584]{1,0:T(8,128)(2,1)S(1)}, u32[]{:S(2)}, u32[]{:S(2)}) %collective-permute-start.9) | collective-permute-done | bytes 458784 | tf_op jit(solution)/shard_map/ppermute | solution.py:366
  23.9 0.6 shard_map.136
  24.4 0.6 collective-permute-start.10
  25.0 6.7 %collective-permute-done.10.refs_1_ = bf16[32,3584]{1,0:T(8,128)(2,1)S(1)} collective-permute-done((bf16[32,3584]{1,0:T(8,128)(2,1)S(1)}, bf16[32,3584]{1,0:T(8,128)(2,1)S(1)}, u32[]{:S(2)}, u32[]{:S(2)}) %collective-permute-start.10) | collective-permute-done | bytes 229408 | tf_op jit(solution)/shard_map/ppermute | solution.py:366
  31.7 0.1 shard_map.137
  31.8 1.9 %collective-permute-start.11 = (bf16[8,3584]{1,0:T(8,128)(2,1)S(1)}, bf16[8,3584]{1,0:T(8,128)(2,1)S(1)}, u32[]{:S(2)}, u32[]{:S(2)}) collective-permute-start(bf16[8,3584]{1,0:T(8,128)(2,1)S(1)} %get-tuple-element.57), channel_id=1, source_target_pairs={{0,12},{1,13},{2,14},{3,15},{4,8},{5,9},{6,10},{7,11},{8,4},{9,5},... | collective-permute-start | bytes 172040 | tf_op jit(solution)/shard_map/ppermute | solution.py:366
  33.7 1.0 %collective-permute-start.12 = (bf16[8,3584]{1,0:T(8,128)(2,1)S(1)}, bf16[8,3584]{1,0:T(8,128)(2,1)S(1)}, u32[]{:S(2)}, u32[]{:S(2)}) collective-permute-start(bf16[8,3584]{1,0:T(8,128)(2,1)S(1)} %get-tuple-element.58), channel_id=1, source_target_pairs={{0,8},{1,9},{2,10},{3,11},{4,12},{5,13},{6,14},{7,15},{8,0},{9,1},... | collective-permute-start | bytes 172040 | tf_op jit(solution)/shard_map/ppermute | solution.py:366
  34.7 1.5 %collective-permute-start.13 = (bf16[8,3584]{1,0:T(8,128)(2,1)S(1)}, bf16[8,3584]{1,0:T(8,128)(2,1)S(1)}, u32[]{:S(2)}, u32[]{:S(2)}) collective-permute-start(bf16[8,3584]{1,0:T(8,128)(2,1)S(1)} %get-tuple-element.59), channel_id=1, source_target_pairs={{0,4},{1,5},{2,6},{3,7},{4,0},{5,1},{6,2},{7,3},{8,12},{9,13},{10,... | collective-permute-start | bytes 172040 | tf_op jit(solution)/shard_map/ppermute | solution.py:366
  36.2 1.9 %collective-permute-done.11.refs_2_ = bf16[8,3584]{1,0:T(8,128)(2,1)S(1)} collective-permute-done((bf16[8,3584]{1,0:T(8,128)(2,1)S(1)}, bf16[8,3584]{1,0:T(8,128)(2,1)S(1)}, u32[]{:S(2)}, u32[]{:S(2)}) %collective-permute-start.11) | collective-permute-done | bytes 57376 | tf_op jit(solution)/shard_map/ppermute | solution.py:366
  38.2 1.3 %collective-permute-done.12.refs_3_ = bf16[8,3584]{1,0:T(8,128)(2,1)S(1)} collective-permute-done((bf16[8,3584]{1,0:T(8,128)(2,1)S(1)}, bf16[8,3584]{1,0:T(8,128)(2,1)S(1)}, u32[]{:S(2)}, u32[]{:S(2)}) %collective-permute-start.12) | collective-permute-done | bytes 57376 | tf_op jit(solution)/shard_map/ppermute | solution.py:366
  39.5 0.0 collective-permute-done.13.refs_4_
  39.5 0.2 shard_map.138
  39.8 0.8 %collective-permute-start.17 = (bf16[32,2176]{1,0:T(8,128)(2,1)S(1)}, bf16[32,2176]{1,0:T(8,128)(2,1)S(1)}, u32[]{:S(2)}, u32[]{:S(2)}) collective-permute-start(bf16[32,2176]{1,0:T(8,128)(2,1)S(1)} %get-tuple-element.69), channel_id=1, source_target_pairs={{0,2},{1,3},{2,0},{3,1},{4,6},{5,7},{6,4},{7,5},{8,10},{9,11},{10,... | collective-permute-start | bytes 417800 | tf_op jit(solution)/shard_map/ppermute | solution.py:366
  40.5 2.1 %collective-permute-start.14 = (bf16[8,3584]{1,0:T(8,128)(2,1)S(1)}, bf16[8,3584]{1,0:T(8,128)(2,1)S(1)}, u32[]{:S(2)}, u32[]{:S(2)}) collective-permute-start(bf16[8,3584]{1,0:T(8,128)(2,1)S(1)} %get-tuple-element.64), channel_id=1, source_target_pairs={{0,12},{1,13},{2,14},{3,15},{4,8},{5,9},{6,10},{7,11},{8,4},{9,5},... | collective-permute-start | bytes 172040 | tf_op jit(solution)/shard_map/ppermute | solution.py:366
  42.6 0.1 collective-permute-start.15
  42.7 2.2 %collective-permute-start.16 = (bf16[8,3584]{1,0:T(8,128)(2,1)S(1)}, bf16[8,3584]{1,0:T(8,128)(2,1)S(1)}, u32[]{:S(2)}, u32[]{:S(2)}) collective-permute-start(bf16[8,3584]{1,0:T(8,128)(2,1)S(1)} %get-tuple-element.66), channel_id=1, source_target_pairs={{0,4},{1,5},{2,6},{3,7},{4,0},{5,1},{6,2},{7,3},{8,12},{9,13},{10,... | collective-permute-start | bytes 172040 | tf_op jit(solution)/shard_map/ppermute | solution.py:366
  44.9 2.2 %collective-permute-done.14.refs_0_ = bf16[8,3584]{1,0:T(8,128)(2,1)S(1)} collective-permute-done((bf16[8,3584]{1,0:T(8,128)(2,1)S(1)}, bf16[8,3584]{1,0:T(8,128)(2,1)S(1)}, u32[]{:S(2)}, u32[]{:S(2)}) %collective-permute-start.14) | collective-permute-done | bytes 57376 | tf_op jit(solution)/shard_map/ppermute | solution.py:366
  47.1 1.2 %collective-permute-done.15.refs_1_ = bf16[8,3584]{1,0:T(8,128)(2,1)S(1)} collective-permute-done((bf16[8,3584]{1,0:T(8,128)(2,1)S(1)}, bf16[8,3584]{1,0:T(8,128)(2,1)S(1)}, u32[]{:S(2)}, u32[]{:S(2)}) %collective-permute-start.15) | collective-permute-done | bytes 57376 | tf_op jit(solution)/shard_map/ppermute | solution.py:366
  48.3 0.0 collective-permute-done.16.refs_2_
  48.3 0.0 collective-permute-done.17.refs_5_
  48.3 0.2 shard_map.139
  48.5 0.8 %collective-permute-start.18 = (bf16[32,3584]{1,0:T(8,128)(2,1)S(1)}, bf16[32,3584]{1,0:T(8,128)(2,1)S(1)}, u32[]{:S(2)}, u32[]{:S(2)}) collective-permute-start(bf16[32,3584]{1,0:T(8,128)(2,1)S(1)} %get-tuple-element.70.refs_0_), channel_id=1, source_target_pairs={{0,2},{1,3},{2,0},{3,1},{4,6},{5,7},{6,4},{7,5},{8,10},{9,11},{10,... | collective-permute-start | bytes 688136 | tf_op jit(solution)/shard_map/ppermute | solution.py:366
  49.3 0.0 collective-permute-done.19.refs_3_
  49.3 5.3 %collective-permute-done.18.refs_1_ = bf16[32,3584]{1,0:T(8,128)(2,1)S(1)} collective-permute-done((bf16[32,3584]{1,0:T(8,128)(2,1)S(1)}, bf16[32,3584]{1,0:T(8,128)(2,1)S(1)}, u32[]{:S(2)}, u32[]{:S(2)}) %collective-permute-start.18) | collective-permute-done | bytes 229408 | tf_op jit(solution)/shard_map/ppermute | solution.py:366
  54.6 1.5 %shard_map.140 = (f32[32,2176]{1,0:T(8,128)S(1)}, bf16[32,2176]{1,0:T(8,128)(2,1)S(1)}) custom-call(bf16[32,3584]{1,0:T(8,128)(2,1)S(1)} %get-tuple-element.70.refs_0_, bf16[32,3584]{1,0:T(8,128)(2,1)S(1)} %collective-permute-done.18.refs_1_, bf16[3584,256]{1,0:T(8,128)(2,1)S(1)} %get-tuple-element.71.refs_2_, ...), custom_call_target="tpu_custom_call" | custom-call | tf_op jit(solution)/shard_map/pallas_call | solution.py:83
  56.1 0.8 %collective-permute-start.20 = (bf16[32,2176]{1,0:T(8,128)(2,1)S(1)}, bf16[32,2176]{1,0:T(8,128)(2,1)S(1)}, u32[]{:S(2)}, u32[]{:S(2)}) collective-permute-start(bf16[32,2176]{1,0:T(8,128)(2,1)S(1)} %get-tuple-element.73), channel_id=1, source_target_pairs={{0,2},{1,3},{2,0},{3,1},{4,6},{5,7},{6,4},{7,5},{8,10},{9,11},{10,... | collective-permute-start | bytes 417800 | tf_op jit(solution)/shard_map/ppermute | solution.py:366
  56.9 2.0 %collective-permute-start.24 = (bf16[8,2176]{1,0:T(8,128)(2,1)S(1)}, bf16[8,2176]{1,0:T(8,128)(2,1)S(1)}, u32[]{:S(2)}, u32[]{:S(2)}) collective-permute-start(bf16[8,2176]{1,0:T(8,128)(2,1)S(1)} %get-tuple-element.79), channel_id=1, source_target_pairs={{0,12},{1,13},{2,14},{3,15},{4,8},{5,9},{6,10},{7,11},{8,4},{9,5},... | collective-permute-start | bytes 104456 | tf_op jit(solution)/shard_map/ppermute | solution.py:366
  58.9 1.0 %collective-permute-start.25 = (bf16[8,2176]{1,0:T(8,128)(2,1)S(1)}, bf16[8,2176]{1,0:T(8,128)(2,1)S(1)}, u32[]{:S(2)}, u32[]{:S(2)}) collective-permute-start(bf16[8,2176]{1,0:T(8,128)(2,1)S(1)} %get-tuple-element.80), channel_id=1, source_target_pairs={{0,8},{1,9},{2,10},{3,11},{4,12},{5,13},{6,14},{7,15},{8,0},{9,1},... | collective-permute-start | bytes 104456 | tf_op jit(solution)/shard_map/ppermute | solution.py:366
  59.9 1.4 %collective-permute-start.26 = (bf16[8,2176]{1,0:T(8,128)(2,1)S(1)}, bf16[8,2176]{1,0:T(8,128)(2,1)S(1)}, u32[]{:S(2)}, u32[]{:S(2)}) collective-permute-start(bf16[8,2176]{1,0:T(8,128)(2,1)S(1)} %get-tuple-element.81), channel_id=1, source_target_pairs={{0,4},{1,5},{2,6},{3,7},{4,0},{5,1},{6,2},{7,3},{8,12},{9,13},{10,... | collective-permute-start | bytes 104456 | tf_op jit(solution)/shard_map/ppermute | solution.py:366
  61.3 0.0 collective-permute-done.20.refs_1_
  61.3 0.1 shard_map.141
  61.4 2.4 %collective-permute-start.21 = (bf16[8,2176]{1,0:T(8,128)(2,1)S(1)}, bf16[8,2176]{1,0:T(8,128)(2,1)S(1)}, u32[]{:S(2)}, u32[]{:S(2)}) collective-permute-start(bf16[8,2176]{1,0:T(8,128)(2,1)S(1)} %get-tuple-element.75), channel_id=1, source_target_pairs={{0,12},{1,13},{2,14},{3,15},{4,8},{5,9},{6,10},{7,11},{8,4},{9,5},... | collective-permute-start | bytes 104456 | tf_op jit(solution)/shard_map/ppermute | solution.py:366
  63.8 0.0 collective-permute-start.22
  63.8 0.0 collective-permute-done.24.refs_5_
  63.9 2.0 %collective-permute-start.23 = (bf16[8,2176]{1,0:T(8,128)(2,1)S(1)}, bf16[8,2176]{1,0:T(8,128)(2,1)S(1)}, u32[]{:S(2)}, u32[]{:S(2)}) collective-permute-start(bf16[8,2176]{1,0:T(8,128)(2,1)S(1)} %get-tuple-element.77), channel_id=1, source_target_pairs={{0,4},{1,5},{2,6},{3,7},{4,0},{5,1},{6,2},{7,3},{8,12},{9,13},{10,... | collective-permute-start | bytes 104456 | tf_op jit(solution)/shard_map/ppermute | solution.py:366
  65.9 0.0 collective-permute-done.25.refs_6_
  65.9 0.0 collective-permute-done.26.refs_7_
  65.9 1.3 %collective-permute-done.21.refs_1_ = bf16[8,2176]{1,0:T(8,128)(2,1)S(1)} collective-permute-done((bf16[8,2176]{1,0:T(8,128)(2,1)S(1)}, bf16[8,2176]{1,0:T(8,128)(2,1)S(1)}, u32[]{:S(2)}, u32[]{:S(2)}) %collective-permute-start.21) | collective-permute-done | bytes 34848 | tf_op jit(solution)/shard_map/ppermute | solution.py:366
  67.2 1.5 %collective-permute-done.22.refs_2_ = bf16[8,2176]{1,0:T(8,128)(2,1)S(1)} collective-permute-done((bf16[8,2176]{1,0:T(8,128)(2,1)S(1)}, bf16[8,2176]{1,0:T(8,128)(2,1)S(1)}, u32[]{:S(2)}, u32[]{:S(2)}) %collective-permute-start.22) | collective-permute-done | bytes 34848 | tf_op jit(solution)/shard_map/ppermute | solution.py:366
  68.7 0.8 %shard_map.142 = (f32[1,8]{1,0:T(1,128)}, f32[8,2048]{1,0:T(8,128)}) custom-call(f32[8,2176]{1,0:T(8,128)S(1)} %get-tuple-element.74.refs_0_, bf16[8,2176]{1,0:T(8,128)(2,1)S(1)} %collective-permute-done.21.refs_1_, bf16[8,2176]{1,0:T(8,128)(2,1)S(1)} %collective-permute-done.22.refs_2_, bf16[8,2176]{1,0:T(8,128)(2,1)S(1)} %collective-permute-done.23.refs_3_, ...), custom_call_target="tpu_custom_call" | custom-call | tf_op jit(solution)/shard_map/pallas_call | solution.py:83
  (2 shorter events, 0.0 us)
Async XLA Ops:
  0.6 15.1 %collective-permute-start.2 = (bf16[2048,256]{1,0:T(8,128)(2,1)}, bf16[2048,256]{1,0:T(8,128)(2,1)S(1)}, u32[]{:S(2)}, u32[]{:S(2)}) collective-permute-start(bf16[2048,256]{1,0:T(8,128)(2,1)} %refs_6_.1), channel_id=1, source_target_pairs={{0,1},{1,0},{2,3},{3,2},{4,5},{5,4},{6,7},{7,6},{8,9},{9,8},{10,11... | collective-permute-start | bytes 3145736 | tf_op jit(solution)/shard_map/ppermute | solution.py:366
  1.1 48.1 %collective-permute-start.19 = (bf16[3584,256]{1,0:T(8,128)(2,1)}, bf16[3584,256]{1,0:T(8,128)(2,1)S(1)}, u32[]{:S(2)}, u32[]{:S(2)}) collective-permute-start(bf16[3584,256]{1,0:T(8,128)(2,1)} %refs_10_.1), channel_id=1, source_target_pairs={{0,1},{1,0},{2,3},{3,2},{4,5},{5,4},{6,7},{7,6},{8,9},{9,8},{10,11... | collective-permute-start | bytes 5505032 | tf_op jit(solution)/shard_map/ppermute | solution.py:366
  1.2 8.0 %collective-permute-start.3 = (bf16[8,3584]{1,0:T(8,128)(2,1)}, bf16[8,3584]{1,0:T(8,128)(2,1)S(1)}, u32[]{:S(2)}, u32[]{:S(2)}) collective-permute-start(bf16[8,3584]{1,0:T(8,128)(2,1)} %refs_1_.1), channel_id=1, source_target_pairs={{0,12},{1,13},{2,14},{3,15},{4,8},{5,9},{6,10},{7,11},{8,4},{9,5},... | collective-permute-start | bytes 172040 | tf_op jit(solution)/shard_map/ppermute | solution.py:366
  6.3 4.7 %collective-permute-start.4 = (bf16[8,3584]{1,0:T(8,128)(2,1)}, bf16[8,3584]{1,0:T(8,128)(2,1)S(1)}, u32[]{:S(2)}, u32[]{:S(2)}) collective-permute-start(bf16[8,3584]{1,0:T(8,128)(2,1)} %refs_1_.1), channel_id=1, source_target_pairs={{0,4},{1,5},{2,6},{3,7},{4,0},{5,1},{6,2},{7,3},{8,12},{9,13},{10,... | collective-permute-start | bytes 172040 | tf_op jit(solution)/shard_map/ppermute | solution.py:366
  6.3 5.9 %collective-permute-start.5 = (bf16[8,3584]{1,0:T(8,128)(2,1)}, bf16[8,3584]{1,0:T(8,128)(2,1)S(1)}, u32[]{:S(2)}, u32[]{:S(2)}) collective-permute-start(bf16[8,3584]{1,0:T(8,128)(2,1)} %refs_1_.1), channel_id=1, source_target_pairs={{0,8},{1,9},{2,10},{3,11},{4,12},{5,13},{6,14},{7,15},{8,0},{9,1},... | collective-permute-start | bytes 172040 | tf_op jit(solution)/shard_map/ppermute | solution.py:366
  12.3 7.0 %collective-permute-start.6 = (bf16[32,3584]{1,0:T(8,128)(2,1)S(1)}, bf16[32,3584]{1,0:T(8,128)(2,1)S(1)}, u32[]{:S(2)}, u32[]{:S(2)}) collective-permute-start(bf16[32,3584]{1,0:T(8,128)(2,1)S(1)} %shard_map.132.refs_14_.refs_0_), channel_id=1, source_target_pairs={{0,2},{1,3},{2,0},{3,1},{4,6},{5,7},{6,4},{7,5},{8,10},{9,11},{10,... | collective-permute-start | bytes 688136 | tf_op jit(solution)/shard_map/ppermute | solution.py:366
  13.9 1.9 %collective-permute-start.1 = (bf16[128,256]{1,0:T(8,128)(2,1)}, bf16[128,256]{1,0:T(8,128)(2,1)S(1)}, u32[]{:S(2)}, u32[]{:S(2)}) collective-permute-start(bf16[128,256]{1,0:T(8,128)(2,1)} %refs_5_.1), channel_id=1, source_target_pairs={{0,1},{1,0},{2,3},{3,2},{4,5},{5,4},{6,7},{7,6},{8,9},{9,8},{10,11... | collective-permute-start | bytes 196616 | tf_op jit(solution)/shard_map/ppermute | solution.py:366
  13.9 1.5 %collective-permute-start = (s32[1,256]{1,0:T(1,128)}, s32[1,256]{1,0:T(1,128)S(1)}, u32[]{:S(2)}, u32[]{:S(2)}) collective-permute-start(s32[1,256]{1,0:T(1,128)} %bitcast.5), channel_id=1, source_target_pairs={{0,1},{1,0},{2,3},{3,2},{4,5},{5,4},{6,7},{7,6},{8,9},{9,8},{10,11... | collective-permute-start | bytes 3080 | tf_op jit(solution)/shard_map/ppermute | solution.py:366
  15.4 4.2 %collective-permute-start.7 = (bf16[32,3584]{1,0:T(8,128)(2,1)S(1)}, bf16[32,3584]{1,0:T(8,128)(2,1)S(1)}, u32[]{:S(2)}, u32[]{:S(2)}) collective-permute-start(bf16[32,3584]{1,0:T(8,128)(2,1)S(1)} %shard_map.132.refs_14_.refs_0_), channel_id=1, source_target_pairs={{0,1},{1,0},{2,3},{3,2},{4,5},{5,4},{6,7},{7,6},{8,9},{9,8},{10,11... | collective-permute-start | bytes 688136 | tf_op jit(solution)/shard_map/ppermute | solution.py:366
  19.4 1.6 %collective-permute-start.8 = (bf16[32,3584]{1,0:T(8,128)(2,1)S(1)}, bf16[32,3584]{1,0:T(8,128)(2,1)S(1)}, u32[]{:S(2)}, u32[]{:S(2)}) collective-permute-start(bf16[32,3584]{1,0:T(8,128)(2,1)S(1)} %shard_map.134.refs_1_), channel_id=1, source_target_pairs={{0,1},{1,0},{2,3},{3,2},{4,5},{5,4},{6,7},{7,6},{8,9},{9,8},{10,11... | collective-permute-start | bytes 688136 | tf_op jit(solution)/shard_map/ppermute | solution.py:366
  22.0 1.9 %collective-permute-start.9 = (bf16[64,3584]{1,0:T(8,128)(2,1)S(1)}, bf16[64,3584]{1,0:T(8,128)(2,1)S(1)}, u32[]{:S(2)}, u32[]{:S(2)}) collective-permute-start(bf16[64,3584]{1,0:T(8,128)(2,1)S(1)} %get-tuple-element.51), channel_id=1, source_target_pairs={{0,1},{1,0},{2,3},{3,2},{4,5},{5,4},{6,7},{7,6},{8,9},{9,8},{10,11... | collective-permute-start | bytes 1376264 | tf_op jit(solution)/shard_map/ppermute | solution.py:366
  24.4 7.3 %collective-permute-start.10 = (bf16[32,3584]{1,0:T(8,128)(2,1)S(1)}, bf16[32,3584]{1,0:T(8,128)(2,1)S(1)}, u32[]{:S(2)}, u32[]{:S(2)}) collective-permute-start(bf16[32,3584]{1,0:T(8,128)(2,1)S(1)} %get-tuple-element.55), channel_id=1, source_target_pairs={{0,2},{1,3},{2,0},{3,1},{4,6},{5,7},{6,4},{7,5},{8,10},{9,11},{10,... | collective-permute-start | bytes 688136 | tf_op jit(solution)/shard_map/ppermute | solution.py:366
  31.8 6.4 %collective-permute-start.11 = (bf16[8,3584]{1,0:T(8,128)(2,1)S(1)}, bf16[8,3584]{1,0:T(8,128)(2,1)S(1)}, u32[]{:S(2)}, u32[]{:S(2)}) collective-permute-start(bf16[8,3584]{1,0:T(8,128)(2,1)S(1)} %get-tuple-element.57), channel_id=1, source_target_pairs={{0,12},{1,13},{2,14},{3,15},{4,8},{5,9},{6,10},{7,11},{8,4},{9,5},... | collective-permute-start | bytes 172040 | tf_op jit(solution)/shard_map/ppermute | solution.py:366
  33.7 5.8 %collective-permute-start.12 = (bf16[8,3584]{1,0:T(8,128)(2,1)S(1)}, bf16[8,3584]{1,0:T(8,128)(2,1)S(1)}, u32[]{:S(2)}, u32[]{:S(2)}) collective-permute-start(bf16[8,3584]{1,0:T(8,128)(2,1)S(1)} %get-tuple-element.58), channel_id=1, source_target_pairs={{0,8},{1,9},{2,10},{3,11},{4,12},{5,13},{6,14},{7,15},{8,0},{9,1},... | collective-permute-start | bytes 172040 | tf_op jit(solution)/shard_map/ppermute | solution.py:366
  34.7 4.8 %collective-permute-start.13 = (bf16[8,3584]{1,0:T(8,128)(2,1)S(1)}, bf16[8,3584]{1,0:T(8,128)(2,1)S(1)}, u32[]{:S(2)}, u32[]{:S(2)}) collective-permute-start(bf16[8,3584]{1,0:T(8,128)(2,1)S(1)} %get-tuple-element.59), channel_id=1, source_target_pairs={{0,4},{1,5},{2,6},{3,7},{4,0},{5,1},{6,2},{7,3},{8,12},{9,13},{10,... | collective-permute-start | bytes 172040 | tf_op jit(solution)/shard_map/ppermute | solution.py:366
  39.8 8.6 %collective-permute-start.17 = (bf16[32,2176]{1,0:T(8,128)(2,1)S(1)}, bf16[32,2176]{1,0:T(8,128)(2,1)S(1)}, u32[]{:S(2)}, u32[]{:S(2)}) collective-permute-start(bf16[32,2176]{1,0:T(8,128)(2,1)S(1)} %get-tuple-element.69), channel_id=1, source_target_pairs={{0,2},{1,3},{2,0},{3,1},{4,6},{5,7},{6,4},{7,5},{8,10},{9,11},{10,... | collective-permute-start | bytes 417800 | tf_op jit(solution)/shard_map/ppermute | solution.py:366
  40.5 6.6 %collective-permute-start.14 = (bf16[8,3584]{1,0:T(8,128)(2,1)S(1)}, bf16[8,3584]{1,0:T(8,128)(2,1)S(1)}, u32[]{:S(2)}, u32[]{:S(2)}) collective-permute-start(bf16[8,3584]{1,0:T(8,128)(2,1)S(1)} %get-tuple-element.64), channel_id=1, source_target_pairs={{0,12},{1,13},{2,14},{3,15},{4,8},{5,9},{6,10},{7,11},{8,4},{9,5},... | collective-permute-start | bytes 172040 | tf_op jit(solution)/shard_map/ppermute | solution.py:366
  42.6 5.7 %collective-permute-start.15 = (bf16[8,3584]{1,0:T(8,128)(2,1)S(1)}, bf16[8,3584]{1,0:T(8,128)(2,1)S(1)}, u32[]{:S(2)}, u32[]{:S(2)}) collective-permute-start(bf16[8,3584]{1,0:T(8,128)(2,1)S(1)} %get-tuple-element.65), channel_id=1, source_target_pairs={{0,8},{1,9},{2,10},{3,11},{4,12},{5,13},{6,14},{7,15},{8,0},{9,1},... | collective-permute-start | bytes 172040 | tf_op jit(solution)/shard_map/ppermute | solution.py:366
  42.7 5.6 %collective-permute-start.16 = (bf16[8,3584]{1,0:T(8,128)(2,1)S(1)}, bf16[8,3584]{1,0:T(8,128)(2,1)S(1)}, u32[]{:S(2)}, u32[]{:S(2)}) collective-permute-start(bf16[8,3584]{1,0:T(8,128)(2,1)S(1)} %get-tuple-element.66), channel_id=1, source_target_pairs={{0,4},{1,5},{2,6},{3,7},{4,0},{5,1},{6,2},{7,3},{8,12},{9,13},{10,... | collective-permute-start | bytes 172040 | tf_op jit(solution)/shard_map/ppermute | solution.py:366
  48.5 6.1 %collective-permute-start.18 = (bf16[32,3584]{1,0:T(8,128)(2,1)S(1)}, bf16[32,3584]{1,0:T(8,128)(2,1)S(1)}, u32[]{:S(2)}, u32[]{:S(2)}) collective-permute-start(bf16[32,3584]{1,0:T(8,128)(2,1)S(1)} %get-tuple-element.70.refs_0_), channel_id=1, source_target_pairs={{0,2},{1,3},{2,0},{3,1},{4,6},{5,7},{6,4},{7,5},{8,10},{9,11},{10,... | collective-permute-start | bytes 688136 | tf_op jit(solution)/shard_map/ppermute | solution.py:366
  56.1 5.2 %collective-permute-start.20 = (bf16[32,2176]{1,0:T(8,128)(2,1)S(1)}, bf16[32,2176]{1,0:T(8,128)(2,1)S(1)}, u32[]{:S(2)}, u32[]{:S(2)}) collective-permute-start(bf16[32,2176]{1,0:T(8,128)(2,1)S(1)} %get-tuple-element.73), channel_id=1, source_target_pairs={{0,2},{1,3},{2,0},{3,1},{4,6},{5,7},{6,4},{7,5},{8,10},{9,11},{10,... | collective-permute-start | bytes 417800 | tf_op jit(solution)/shard_map/ppermute | solution.py:366
  56.9 7.0 %collective-permute-start.24 = (bf16[8,2176]{1,0:T(8,128)(2,1)S(1)}, bf16[8,2176]{1,0:T(8,128)(2,1)S(1)}, u32[]{:S(2)}, u32[]{:S(2)}) collective-permute-start(bf16[8,2176]{1,0:T(8,128)(2,1)S(1)} %get-tuple-element.79), channel_id=1, source_target_pairs={{0,12},{1,13},{2,14},{3,15},{4,8},{5,9},{6,10},{7,11},{8,4},{9,5},... | collective-permute-start | bytes 104456 | tf_op jit(solution)/shard_map/ppermute | solution.py:366
  58.9 7.0 %collective-permute-start.25 = (bf16[8,2176]{1,0:T(8,128)(2,1)S(1)}, bf16[8,2176]{1,0:T(8,128)(2,1)S(1)}, u32[]{:S(2)}, u32[]{:S(2)}) collective-permute-start(bf16[8,2176]{1,0:T(8,128)(2,1)S(1)} %get-tuple-element.80), channel_id=1, source_target_pairs={{0,8},{1,9},{2,10},{3,11},{4,12},{5,13},{6,14},{7,15},{8,0},{9,1},... | collective-permute-start | bytes 104456 | tf_op jit(solution)/shard_map/ppermute | solution.py:366
  59.9 6.0 %collective-permute-start.26 = (bf16[8,2176]{1,0:T(8,128)(2,1)S(1)}, bf16[8,2176]{1,0:T(8,128)(2,1)S(1)}, u32[]{:S(2)}, u32[]{:S(2)}) collective-permute-start(bf16[8,2176]{1,0:T(8,128)(2,1)S(1)} %get-tuple-element.81), channel_id=1, source_target_pairs={{0,4},{1,5},{2,6},{3,7},{4,0},{5,1},{6,2},{7,3},{8,12},{9,13},{10,... | collective-permute-start | bytes 104456 | tf_op jit(solution)/shard_map/ppermute | solution.py:366
  61.4 5.8 %collective-permute-start.21 = (bf16[8,2176]{1,0:T(8,128)(2,1)S(1)}, bf16[8,2176]{1,0:T(8,128)(2,1)S(1)}, u32[]{:S(2)}, u32[]{:S(2)}) collective-permute-start(bf16[8,2176]{1,0:T(8,128)(2,1)S(1)} %get-tuple-element.75), channel_id=1, source_target_pairs={{0,12},{1,13},{2,14},{3,15},{4,8},{5,9},{6,10},{7,11},{8,4},{9,5},... | collective-permute-start | bytes 104456 | tf_op jit(solution)/shard_map/ppermute | solution.py:366
  63.8 4.8 %collective-permute-start.22 = (bf16[8,2176]{1,0:T(8,128)(2,1)S(1)}, bf16[8,2176]{1,0:T(8,128)(2,1)S(1)}, u32[]{:S(2)}, u32[]{:S(2)}) collective-permute-start(bf16[8,2176]{1,0:T(8,128)(2,1)S(1)} %get-tuple-element.76), channel_id=1, source_target_pairs={{0,8},{1,9},{2,10},{3,11},{4,12},{5,13},{6,14},{7,15},{8,0},{9,1},... | collective-permute-start | bytes 104456 | tf_op jit(solution)/shard_map/ppermute | solution.py:366
  63.9 4.8 %collective-permute-start.23 = (bf16[8,2176]{1,0:T(8,128)(2,1)S(1)}, bf16[8,2176]{1,0:T(8,128)(2,1)S(1)}, u32[]{:S(2)}, u32[]{:S(2)}) collective-permute-start(bf16[8,2176]{1,0:T(8,128)(2,1)S(1)} %get-tuple-element.77), channel_id=1, source_target_pairs={{0,4},{1,5},{2,6},{3,7},{4,0},{5,1},{6,2},{7,3},{8,12},{9,13},{10,... | collective-permute-start | bytes 104456 | tf_op jit(solution)/shard_map/ppermute | solution.py:366

commit v5 on v4

--- a/solution.py
+++ b/solution.py
@@ -407,7 +407,7 @@
     own_map = vocab_map.reshape(1, -1)
     theirs = [swap(a, 1) for a in (own_map, student_logits, student_head)]
     their_teacher = swap(teacher_head, 1)
-    prefetched = [w_gate, w_up, w_down, teacher_head, final_gain, expert_ids.T, gate_scores.T]
+    prefetched = [w_gate, w_up, w_down, final_gain, expert_ids.T, gate_scores.T]
     fetched = prefetched if near else []
     split_rows = [((quarter, width + BLOCK), d) for d in [F32] + [BF16] * (size_x - 1)]
     split_dev = [((tok_dev, width + BLOCK), d) for d in [F32] + [BF16] * (size_z - 1)]
@@ -438,7 +438,7 @@
         after=[column_rows],
     )
     moved, moved_head, *stud_parts = outs[: 2 + size_x]
-    w_gate, w_up, w_down, teacher_head, final_gain, ids, scores = (
+    w_gate, w_up, w_down, final_gain, ids, scores = (
         outs[2 + size_x :] if near else prefetched
     )
     crossed = run(
@@ -496,6 +496,16 @@
     )
     student = from_z(*take(outs))
     plane = along_x(column_rows)
+    if near:
+        (teacher_head,) = run(
+            fetch_body,
+            [(teacher_head.shape, BF16)],
+            teacher_head,
+            scratch=[pltpu.SemaphoreType.DMA((1,))],
+            far=1,
+            cost=(0, 2 * teacher_head.size),
+            after=[column_rows],
+        )
     keep, *sends = run(
         functools.partial(teacher_body, len(plane)),
         split_rows,

time: 69.7 us -> 69.1 us (level)
  waiting for transfers between devices: 29.9 us -> 27.9 us
  Pallas kernels: 9.08 us -> 10.1 us
    ppermute x27, waiting for transfers between devices: 29.9 us -> 27.9 us  [swap(): lax.ppermute(values, 'expert', [(i, i ^ offset) for i in range(devices)])]
    pallas_call x12 -> x13, Pallas kernels: 9.08 us -> 10.1 us  [call(): pl.pallas_call(run, out_shape=[kind(s, d) for s, d in outs], in_specs=[sm...]
  transfers between devices with their start and end apart: 27 -> 27, of which waited for: 14 -> 15; matrix products, arithmetic and copies ran while one was open for 0% -> 0% of each run, Pallas kernels for 10% -> 11%
where the time goes in v5:
time: 69.1 us; the launch traced here: 68.8 us
  starting transfers between devices  30.1 us (44%)
  waiting for transfers between devices  27.9 us (40%)
  Pallas kernels  10.1 us (15%)
  between operations  0.75 us (1%)
    ppermute x27, starting transfers between devices, swap(): lax.ppermute(values, 'expert', [(i, i ^ offset) for i in range(devices)])  30.1 us
    ppermute x27, waiting for transfers between devices, swap(): lax.ppermute(values, 'expert', [(i, i ^ offset) for i in range(devices)])  27.9 us
    pallas_call x13, Pallas kernels, call(): pl.pallas_call(run, out_shape=[kind(s, d) for s, d in outs], in_specs=[sm...  10.1 us
  transfers between devices with their start and end apart: 27, of which 15 were waited for; matrix products, arithmetic and copies ran while one was open for 0% of the time, Pallas kernels for 11%

profile of v5, /device:TPU:0, one launch (start us, length us, event | category | flops | bytes accessed | tf_op | source)
XLA Modules:
  0.0 68.8 jit_solution(17988777421181986574)
XLA Ops:
  0.6 0.5 collective-permute-start.2
  1.1 0.1 collective-permute-start.19
  1.2 5.0 %collective-permute-start.3 = (bf16[8,3584]{1,0:T(8,128)(2,1)}, bf16[8,3584]{1,0:T(8,128)(2,1)S(1)}, u32[]{:S(2)}, u32[]{:S(2)}) collective-permute-start(bf16[8,3584]{1,0:T(8,128)(2,1)} %refs_1_.1), channel_id=1, source_target_pairs={{0,12},{1,13},{2,14},{3,15},{4,8},{5,9},{6,10},{7,11},{8,4},{9,5},... | collective-permute-start | bytes 172040 | tf_op jit(solution)/shard_map/ppermute | solution.py:366
  6.3 0.0 collective-permute-start.4
  6.3 0.6 collective-permute-start.5
  6.8 2.4 %collective-permute-done.3.refs_2_.refs_1_ = bf16[8,3584]{1,0:T(8,128)(2,1)S(1)} collective-permute-done((bf16[8,3584]{1,0:T(8,128)(2,1)}, bf16[8,3584]{1,0:T(8,128)(2,1)S(1)}, u32[]{:S(2)}, u32[]{:S(2)}) %collective-permute-start.3) | collective-permute-done | bytes 57376 | tf_op jit(solution)/shard_map/ppermute | solution.py:366
  9.2 0.9 %shard_map.131 = (f32[3584]{0:T(1024)S(1)}, bf16[8,3584]{1,0:T(8,128)(2,1)S(1)}) custom-call(f32[3584]{0:T(1024)} %refs_0_.2, bf16[8,3584]{1,0:T(8,128)(2,1)} %refs_1_.1, bf16[8,3584]{1,0:T(8,128)(2,1)S(1)} %collective-permute-done.3.refs_2_.refs_1_), custom_call_target="tpu_custom_call" | custom-call | tf_op jit(solution)/shard_map/pallas_call | solution.py:83
  10.0 1.0 %collective-permute-done.4.refs_2_ = bf16[8,3584]{1,0:T(8,128)(2,1)S(1)} collective-permute-done((bf16[8,3584]{1,0:T(8,128)(2,1)}, bf16[8,3584]{1,0:T(8,128)(2,1)S(1)}, u32[]{:S(2)}, u32[]{:S(2)}) %collective-permute-start.4) | collective-permute-done | bytes 57376 | tf_op jit(solution)/shard_map/ppermute | solution.py:366
  11.0 1.2 %collective-permute-done.5.refs_3_ = bf16[8,3584]{1,0:T(8,128)(2,1)S(1)} collective-permute-done((bf16[8,3584]{1,0:T(8,128)(2,1)}, bf16[8,3584]{1,0:T(8,128)(2,1)S(1)}, u32[]{:S(2)}, u32[]{:S(2)}) %collective-permute-start.5) | collective-permute-done | bytes 57376 | tf_op jit(solution)/shard_map/ppermute | solution.py:366
  12.2 0.2 shard_map.132.refs_13_.refs_0_
  12.3 1.6 %collective-permute-start.6 = (bf16[32,3584]{1,0:T(8,128)(2,1)S(1)}, bf16[32,3584]{1,0:T(8,128)(2,1)S(1)}, u32[]{:S(2)}, u32[]{:S(2)}) collective-permute-start(bf16[32,3584]{1,0:T(8,128)(2,1)S(1)} %shard_map.132.refs_13_.refs_0_), channel_id=1, source_target_pairs={{0,2},{1,3},{2,0},{3,1},{4,6},{5,7},{6,4},{7,5},{8,10},{9,11},{10,... | collective-permute-start | bytes 688136 | tf_op jit(solution)/shard_map/ppermute | solution.py:366
  13.9 0.0 collective-permute-start.1
  13.9 0.5 collective-permute-start
  14.4 1.0 %collective-permute-done.refs_1_ = s32[1,256]{1,0:T(1,128)S(1)} collective-permute-done((s32[1,256]{1,0:T(1,128)}, s32[1,256]{1,0:T(1,128)S(1)}, u32[]{:S(2)}, u32[]{:S(2)}) %collective-permute-start) | collective-permute-done | bytes 1056 | tf_op jit(solution)/shard_map/ppermute | solution.py:366
  15.4 0.3 collective-permute-start.7
  15.7 0.0 collective-permute-done.1.refs_2_
  15.8 0.0 collective-permute-done.2.refs_3_
  15.8 3.1 %shard_map.133 = (f32[64,512]{1,0:T(8,128)S(1)}, bf16[2048,512]{1,0:T(8,128)(2,1)S(1)}, f32[32,2176]{1,0:T(8,128)S(1)}, bf16[32,2176]{1,0:T(8,128)(2,1)S(1)}, bf...) custom-call(s32[1]{0:T(128)} %bitcast.refs_0_, ...), custom_call_target="tpu_custom_call" | custom-call | flops 671088640 | bytes 5512256 | tf_op jit(solution)/shard_map/pallas_call | solution.py:83
  18.8 0.0 collective-permute-done.6.refs_0_
  18.9 0.3 collective-permute-start.8
  19.1 0.0 collective-permute-done.7.refs_2_
  19.1 1.3 %collective-permute-done.8.refs_3_ = bf16[32,3584]{1,0:T(8,128)(2,1)S(1)} collective-permute-done((bf16[32,3584]{1,0:T(8,128)(2,1)S(1)}, bf16[32,3584]{1,0:T(8,128)(2,1)S(1)}, u32[]{:S(2)}, u32[]{:S(2)}) %collective-permute-start.8) | collective-permute-done | bytes 229408 | tf_op jit(solution)/shard_map/ppermute | solution.py:366
  20.4 1.0 %shard_map.135 = (f32[64,3584]{1,0:T(8,128)S(1)}, bf16[64,3584]{1,0:T(8,128)(2,1)S(1)}) custom-call(bf16[32,3584]{1,0:T(8,128)(2,1)S(1)} %shard_map.132.refs_13_.refs_0_, bf16[32,3584]{1,0:T(8,128)(2,1)S(1)} %shard_map.134.refs_1_, bf16[32,3584]{1,0:T(8,128)(2,1)S(1)} %collective-permute-done.7.refs_2_, bf16[32,3584]{1,0:T(8,128)(2,1)S(1)} %collective-permute-done.8.refs_3_, ...), custom_call_target="tpu_custom_call" | custom-call | tf_op jit(solution)/shard_map/pallas_call | solution.py:83
  21.4 0.3 collective-permute-start.9
  21.7 1.6 %collective-permute-done.9.refs_4_ = bf16[64,3584]{1,0:T(8,128)(2,1)S(1)} collective-permute-done((bf16[64,3584]{1,0:T(8,128)(2,1)S(1)}, bf16[64,3584]{1,0:T(8,128)(2,1)S(1)}, u32[]{:S(2)}, u32[]{:S(2)}) %collective-permute-start.9) | collective-permute-done | bytes 458784 | tf_op jit(solution)/shard_map/ppermute | solution.py:366
  23.3 0.6 shard_map.136
  23.9 1.1 %collective-permute-start.10 = (bf16[32,3584]{1,0:T(8,128)(2,1)S(1)}, bf16[32,3584]{1,0:T(8,128)(2,1)S(1)}, u32[]{:S(2)}, u32[]{:S(2)}) collective-permute-start(bf16[32,3584]{1,0:T(8,128)(2,1)S(1)} %get-tuple-element.54), channel_id=1, source_target_pairs={{0,2},{1,3},{2,0},{3,1},{4,6},{5,7},{6,4},{7,5},{8,10},{9,11},{10,... | collective-permute-start | bytes 688136 | tf_op jit(solution)/shard_map/ppermute | solution.py:366
  25.0 6.2 %collective-permute-done.10.refs_1_ = bf16[32,3584]{1,0:T(8,128)(2,1)S(1)} collective-permute-done((bf16[32,3584]{1,0:T(8,128)(2,1)S(1)}, bf16[32,3584]{1,0:T(8,128)(2,1)S(1)}, u32[]{:S(2)}, u32[]{:S(2)}) %collective-permute-start.10) | collective-permute-done | bytes 229408 | tf_op jit(solution)/shard_map/ppermute | solution.py:366
  31.2 0.1 shard_map.137
  31.2 2.1 %collective-permute-start.11 = (bf16[8,3584]{1,0:T(8,128)(2,1)S(1)}, bf16[8,3584]{1,0:T(8,128)(2,1)S(1)}, u32[]{:S(2)}, u32[]{:S(2)}) collective-permute-start(bf16[8,3584]{1,0:T(8,128)(2,1)S(1)} %get-tuple-element.56), channel_id=1, source_target_pairs={{0,12},{1,13},{2,14},{3,15},{4,8},{5,9},{6,10},{7,11},{8,4},{9,5},... | collective-permute-start | bytes 172040 | tf_op jit(solution)/shard_map/ppermute | solution.py:366
  33.4 0.8 %collective-permute-start.12 = (bf16[8,3584]{1,0:T(8,128)(2,1)S(1)}, bf16[8,3584]{1,0:T(8,128)(2,1)S(1)}, u32[]{:S(2)}, u32[]{:S(2)}) collective-permute-start(bf16[8,3584]{1,0:T(8,128)(2,1)S(1)} %get-tuple-element.57), channel_id=1, source_target_pairs={{0,8},{1,9},{2,10},{3,11},{4,12},{5,13},{6,14},{7,15},{8,0},{9,1},... | collective-permute-start | bytes 172040 | tf_op jit(solution)/shard_map/ppermute | solution.py:366
  34.2 1.5 %collective-permute-start.13 = (bf16[8,3584]{1,0:T(8,128)(2,1)S(1)}, bf16[8,3584]{1,0:T(8,128)(2,1)S(1)}, u32[]{:S(2)}, u32[]{:S(2)}) collective-permute-start(bf16[8,3584]{1,0:T(8,128)(2,1)S(1)} %get-tuple-element.58), channel_id=1, source_target_pairs={{0,4},{1,5},{2,6},{3,7},{4,0},{5,1},{6,2},{7,3},{8,12},{9,13},{10,... | collective-permute-start | bytes 172040 | tf_op jit(solution)/shard_map/ppermute | solution.py:366
  35.7 2.1 %collective-permute-done.11.refs_2_ = bf16[8,3584]{1,0:T(8,128)(2,1)S(1)} collective-permute-done((bf16[8,3584]{1,0:T(8,128)(2,1)S(1)}, bf16[8,3584]{1,0:T(8,128)(2,1)S(1)}, u32[]{:S(2)}, u32[]{:S(2)}) %collective-permute-start.11) | collective-permute-done | bytes 57376 | tf_op jit(solution)/shard_map/ppermute | solution.py:366
  37.8 1.2 %collective-permute-done.12.refs_3_ = bf16[8,3584]{1,0:T(8,128)(2,1)S(1)} collective-permute-done((bf16[8,3584]{1,0:T(8,128)(2,1)S(1)}, bf16[8,3584]{1,0:T(8,128)(2,1)S(1)}, u32[]{:S(2)}, u32[]{:S(2)}) %collective-permute-start.12) | collective-permute-done | bytes 57376 | tf_op jit(solution)/shard_map/ppermute | solution.py:366
  39.0 0.0 collective-permute-done.13.refs_4_
  39.0 0.2 shard_map.138
  39.3 1.2 %collective-permute-start.17 = (bf16[32,2176]{1,0:T(8,128)(2,1)S(1)}, bf16[32,2176]{1,0:T(8,128)(2,1)S(1)}, u32[]{:S(2)}, u32[]{:S(2)}) collective-permute-start(bf16[32,2176]{1,0:T(8,128)(2,1)S(1)} %get-tuple-element.68), channel_id=1, source_target_pairs={{0,2},{1,3},{2,0},{3,1},{4,6},{5,7},{6,4},{7,5},{8,10},{9,11},{10,... | collective-permute-start | bytes 417800 | tf_op jit(solution)/shard_map/ppermute | solution.py:366
  40.5 2.2 %collective-permute-start.14 = (bf16[8,3584]{1,0:T(8,128)(2,1)S(1)}, bf16[8,3584]{1,0:T(8,128)(2,1)S(1)}, u32[]{:S(2)}, u32[]{:S(2)}) collective-permute-start(bf16[8,3584]{1,0:T(8,128)(2,1)S(1)} %get-tuple-element.63), channel_id=1, source_target_pairs={{0,12},{1,13},{2,14},{3,15},{4,8},{5,9},{6,10},{7,11},{8,4},{9,5},... | collective-permute-start | bytes 172040 | tf_op jit(solution)/shard_map/ppermute | solution.py:366
  42.6 0.0 collective-permute-start.15
  42.7 2.2 %collective-permute-start.16 = (bf16[8,3584]{1,0:T(8,128)(2,1)S(1)}, bf16[8,3584]{1,0:T(8,128)(2,1)S(1)}, u32[]{:S(2)}, u32[]{:S(2)}) collective-permute-start(bf16[8,3584]{1,0:T(8,128)(2,1)S(1)} %get-tuple-element.65), channel_id=1, source_target_pairs={{0,4},{1,5},{2,6},{3,7},{4,0},{5,1},{6,2},{7,3},{8,12},{9,13},{10,... | collective-permute-start | bytes 172040 | tf_op jit(solution)/shard_map/ppermute | solution.py:366
  44.9 2.1 %collective-permute-done.14.refs_0_ = bf16[8,3584]{1,0:T(8,128)(2,1)S(1)} collective-permute-done((bf16[8,3584]{1,0:T(8,128)(2,1)S(1)}, bf16[8,3584]{1,0:T(8,128)(2,1)S(1)}, u32[]{:S(2)}, u32[]{:S(2)}) %collective-permute-start.14) | collective-permute-done | bytes 57376 | tf_op jit(solution)/shard_map/ppermute | solution.py:366
  47.0 1.3 %collective-permute-done.15.refs_1_ = bf16[8,3584]{1,0:T(8,128)(2,1)S(1)} collective-permute-done((bf16[8,3584]{1,0:T(8,128)(2,1)S(1)}, bf16[8,3584]{1,0:T(8,128)(2,1)S(1)}, u32[]{:S(2)}, u32[]{:S(2)}) %collective-permute-start.15) | collective-permute-done | bytes 57376 | tf_op jit(solution)/shard_map/ppermute | solution.py:366
  48.3 0.0 collective-permute-done.16.refs_2_
  48.3 0.0 collective-permute-done.17.refs_5_
  48.3 0.2 shard_map.139
  48.4 0.5 collective-permute-start.18
  49.0 1.5 %shard_map.140.refs_2_ = bf16[3584,256]{1,0:T(8,128)(2,1)S(1)} custom-call(bf16[3584,256]{1,0:T(8,128)(2,1)} %refs_0_.3, bf16[32,3584]{1,0:T(8,128)(2,1)S(1)} %get-tuple-element.69.refs_1_.refs_0_), custom_call_target="tpu_custom_call" | custom-call | bytes 1835008 | tf_op jit(solution)/shard_map/pallas_call | solution.py:83
  50.5 4.0 %collective-permute-done.18.refs_1_ = bf16[32,3584]{1,0:T(8,128)(2,1)S(1)} collective-permute-done((bf16[32,3584]{1,0:T(8,128)(2,1)S(1)}, bf16[32,3584]{1,0:T(8,128)(2,1)S(1)}, u32[]{:S(2)}, u32[]{:S(2)}) %collective-permute-start.18) | collective-permute-done | bytes 229408 | tf_op jit(solution)/shard_map/ppermute | solution.py:366
  54.5 1.5 %shard_map.141 = (f32[32,2176]{1,0:T(8,128)S(1)}, bf16[32,2176]{1,0:T(8,128)(2,1)S(1)}) custom-call(bf16[32,3584]{1,0:T(8,128)(2,1)S(1)} %get-tuple-element.69.refs_1_.refs_0_, bf16[32,3584]{1,0:T(8,128)(2,1)S(1)} %collective-permute-done.18.refs_1_, bf16[3584,256]{1,0:T(8,128)(2,1)S(1)} %shard_map.140.refs_2_, ...), custom_call_target="tpu_custom_call" | custom-call | tf_op jit(solution)/shard_map/pallas_call | solution.py:83
  56.0 0.5 collective-permute-start.20
  56.6 1.8 %collective-permute-start.24 = (bf16[8,2176]{1,0:T(8,128)(2,1)S(1)}, bf16[8,2176]{1,0:T(8,128)(2,1)S(1)}, u32[]{:S(2)}, u32[]{:S(2)}) collective-permute-start(bf16[8,2176]{1,0:T(8,128)(2,1)S(1)} %get-tuple-element.77), channel_id=1, source_target_pairs={{0,12},{1,13},{2,14},{3,15},{4,8},{5,9},{6,10},{7,11},{8,4},{9,5},... | collective-permute-start | bytes 104456 | tf_op jit(solution)/shard_map/ppermute | solution.py:366
  58.4 1.1 %collective-permute-start.25 = (bf16[8,2176]{1,0:T(8,128)(2,1)S(1)}, bf16[8,2176]{1,0:T(8,128)(2,1)S(1)}, u32[]{:S(2)}, u32[]{:S(2)}) collective-permute-start(bf16[8,2176]{1,0:T(8,128)(2,1)S(1)} %get-tuple-element.78), channel_id=1, source_target_pairs={{0,8},{1,9},{2,10},{3,11},{4,12},{5,13},{6,14},{7,15},{8,0},{9,1},... | collective-permute-start | bytes 104456 | tf_op jit(solution)/shard_map/ppermute | solution.py:366
  59.4 1.5 %collective-permute-start.26 = (bf16[8,2176]{1,0:T(8,128)(2,1)S(1)}, bf16[8,2176]{1,0:T(8,128)(2,1)S(1)}, u32[]{:S(2)}, u32[]{:S(2)}) collective-permute-start(bf16[8,2176]{1,0:T(8,128)(2,1)S(1)} %get-tuple-element.79), channel_id=1, source_target_pairs={{0,4},{1,5},{2,6},{3,7},{4,0},{5,1},{6,2},{7,3},{8,12},{9,13},{10,... | collective-permute-start | bytes 104456 | tf_op jit(solution)/shard_map/ppermute | solution.py:366
  60.9 0.2 collective-permute-done.20.refs_1_
  61.2 0.1 shard_map.142
  61.3 1.9 %collective-permute-start.21 = (bf16[8,2176]{1,0:T(8,128)(2,1)S(1)}, bf16[8,2176]{1,0:T(8,128)(2,1)S(1)}, u32[]{:S(2)}, u32[]{:S(2)}) collective-permute-start(bf16[8,2176]{1,0:T(8,128)(2,1)S(1)} %get-tuple-element.73), channel_id=1, source_target_pairs={{0,12},{1,13},{2,14},{3,15},{4,8},{5,9},{6,10},{7,11},{8,4},{9,5},... | collective-permute-start | bytes 104456 | tf_op jit(solution)/shard_map/ppermute | solution.py:366
  63.2 0.4 collective-permute-start.22
  63.6 0.0 collective-permute-done.24.refs_5_
  63.6 2.2 %collective-permute-start.23 = (bf16[8,2176]{1,0:T(8,128)(2,1)S(1)}, bf16[8,2176]{1,0:T(8,128)(2,1)S(1)}, u32[]{:S(2)}, u32[]{:S(2)}) collective-permute-start(bf16[8,2176]{1,0:T(8,128)(2,1)S(1)} %get-tuple-element.75), channel_id=1, source_target_pairs={{0,4},{1,5},{2,6},{3,7},{4,0},{5,1},{6,2},{7,3},{8,12},{9,13},{10,... | collective-permute-start | bytes 104456 | tf_op jit(solution)/shard_map/ppermute | solution.py:366
  65.8 0.0 collective-permute-done.25.refs_6_
  65.8 0.0 collective-permute-done.26.refs_7_
  65.8 1.3 %collective-permute-done.21.refs_1_ = bf16[8,2176]{1,0:T(8,128)(2,1)S(1)} collective-permute-done((bf16[8,2176]{1,0:T(8,128)(2,1)S(1)}, bf16[8,2176]{1,0:T(8,128)(2,1)S(1)}, u32[]{:S(2)}, u32[]{:S(2)}) %collective-permute-start.21) | collective-permute-done | bytes 34848 | tf_op jit(solution)/shard_map/ppermute | solution.py:366
  67.1 0.9 %collective-permute-done.22.refs_2_ = bf16[8,2176]{1,0:T(8,128)(2,1)S(1)} collective-permute-done((bf16[8,2176]{1,0:T(8,128)(2,1)S(1)}, bf16[8,2176]{1,0:T(8,128)(2,1)S(1)}, u32[]{:S(2)}, u32[]{:S(2)}) %collective-permute-start.22) | collective-permute-done | bytes 34848 | tf_op jit(solution)/shard_map/ppermute | solution.py:366
  68.1 0.8 %shard_map.143 = (f32[1,8]{1,0:T(1,128)}, f32[8,2048]{1,0:T(8,128)}) custom-call(f32[8,2176]{1,0:T(8,128)S(1)} %get-tuple-element.72.refs_0_, bf16[8,2176]{1,0:T(8,128)(2,1)S(1)} %collective-permute-done.21.refs_1_, bf16[8,2176]{1,0:T(8,128)(2,1)S(1)} %collective-permute-done.22.refs_2_, bf16[8,2176]{1,0:T(8,128)(2,1)S(1)} %collective-permute-done.23.refs_3_, ...), custom_call_target="tpu_custom_call" | custom-call | tf_op jit(solution)/shard_map/pallas_call | solution.py:83
  (3 shorter events, 0.0 us)
Async XLA Ops:
  0.6 15.1 %collective-permute-start.2 = (bf16[2048,256]{1,0:T(8,128)(2,1)}, bf16[2048,256]{1,0:T(8,128)(2,1)S(1)}, u32[]{:S(2)}, u32[]{:S(2)}) collective-permute-start(bf16[2048,256]{1,0:T(8,128)(2,1)} %refs_6_.1), channel_id=1, source_target_pairs={{0,1},{1,0},{2,3},{3,2},{4,5},{5,4},{6,7},{7,6},{8,9},{9,8},{10,11... | collective-permute-start | bytes 3145736 | tf_op jit(solution)/shard_map/ppermute | solution.py:366
  1.1 49.3 %collective-permute-start.19 = (bf16[3584,256]{1,0:T(8,128)(2,1)}, bf16[3584,256]{1,0:T(8,128)(2,1)S(1)}, u32[]{:S(2)}, u32[]{:S(2)}) collective-permute-start(bf16[3584,256]{1,0:T(8,128)(2,1)} %refs_0_.3), channel_id=1, source_target_pairs={{0,1},{1,0},{2,3},{3,2},{4,5},{5,4},{6,7},{7,6},{8,9},{9,8},{10,11... | collective-permute-start | bytes 5505032 | tf_op jit(solution)/shard_map/ppermute | solution.py:366
  1.2 8.0 %collective-permute-start.3 = (bf16[8,3584]{1,0:T(8,128)(2,1)}, bf16[8,3584]{1,0:T(8,128)(2,1)S(1)}, u32[]{:S(2)}, u32[]{:S(2)}) collective-permute-start(bf16[8,3584]{1,0:T(8,128)(2,1)} %refs_1_.1), channel_id=1, source_target_pairs={{0,12},{1,13},{2,14},{3,15},{4,8},{5,9},{6,10},{7,11},{8,4},{9,5},... | collective-permute-start | bytes 172040 | tf_op jit(solution)/shard_map/ppermute | solution.py:366
  6.3 4.7 %collective-permute-start.4 = (bf16[8,3584]{1,0:T(8,128)(2,1)}, bf16[8,3584]{1,0:T(8,128)(2,1)S(1)}, u32[]{:S(2)}, u32[]{:S(2)}) collective-permute-start(bf16[8,3584]{1,0:T(8,128)(2,1)} %refs_1_.1), channel_id=1, source_target_pairs={{0,4},{1,5},{2,6},{3,7},{4,0},{5,1},{6,2},{7,3},{8,12},{9,13},{10,... | collective-permute-start | bytes 172040 | tf_op jit(solution)/shard_map/ppermute | solution.py:366
  6.3 5.9 %collective-permute-start.5 = (bf16[8,3584]{1,0:T(8,128)(2,1)}, bf16[8,3584]{1,0:T(8,128)(2,1)S(1)}, u32[]{:S(2)}, u32[]{:S(2)}) collective-permute-start(bf16[8,3584]{1,0:T(8,128)(2,1)} %refs_1_.1), channel_id=1, source_target_pairs={{0,8},{1,9},{2,10},{3,11},{4,12},{5,13},{6,14},{7,15},{8,0},{9,1},... | collective-permute-start | bytes 172040 | tf_op jit(solution)/shard_map/ppermute | solution.py:366
  12.3 6.5 %collective-permute-start.6 = (bf16[32,3584]{1,0:T(8,128)(2,1)S(1)}, bf16[32,3584]{1,0:T(8,128)(2,1)S(1)}, u32[]{:S(2)}, u32[]{:S(2)}) collective-permute-start(bf16[32,3584]{1,0:T(8,128)(2,1)S(1)} %shard_map.132.refs_13_.refs_0_), channel_id=1, source_target_pairs={{0,2},{1,3},{2,0},{3,1},{4,6},{5,7},{6,4},{7,5},{8,10},{9,11},{10,... | collective-permute-start | bytes 688136 | tf_op jit(solution)/shard_map/ppermute | solution.py:366
  13.9 1.9 %collective-permute-start.1 = (bf16[128,256]{1,0:T(8,128)(2,1)}, bf16[128,256]{1,0:T(8,128)(2,1)S(1)}, u32[]{:S(2)}, u32[]{:S(2)}) collective-permute-start(bf16[128,256]{1,0:T(8,128)(2,1)} %refs_5_.1), channel_id=1, source_target_pairs={{0,1},{1,0},{2,3},{3,2},{4,5},{5,4},{6,7},{7,6},{8,9},{9,8},{10,11... | collective-permute-start | bytes 196616 | tf_op jit(solution)/shard_map/ppermute | solution.py:366
  13.9 1.5 %collective-permute-start = (s32[1,256]{1,0:T(1,128)}, s32[1,256]{1,0:T(1,128)S(1)}, u32[]{:S(2)}, u32[]{:S(2)}) collective-permute-start(s32[1,256]{1,0:T(1,128)} %bitcast.5), channel_id=1, source_target_pairs={{0,1},{1,0},{2,3},{3,2},{4,5},{5,4},{6,7},{7,6},{8,9},{9,8},{10,11... | collective-permute-start | bytes 3080 | tf_op jit(solution)/shard_map/ppermute | solution.py:366
  15.4 3.7 %collective-permute-start.7 = (bf16[32,3584]{1,0:T(8,128)(2,1)S(1)}, bf16[32,3584]{1,0:T(8,128)(2,1)S(1)}, u32[]{:S(2)}, u32[]{:S(2)}) collective-permute-start(bf16[32,3584]{1,0:T(8,128)(2,1)S(1)} %shard_map.132.refs_13_.refs_0_), channel_id=1, source_target_pairs={{0,1},{1,0},{2,3},{3,2},{4,5},{5,4},{6,7},{7,6},{8,9},{9,8},{10,11... | collective-permute-start | bytes 688136 | tf_op jit(solution)/shard_map/ppermute | solution.py:366
  18.9 1.6 %collective-permute-start.8 = (bf16[32,3584]{1,0:T(8,128)(2,1)S(1)}, bf16[32,3584]{1,0:T(8,128)(2,1)S(1)}, u32[]{:S(2)}, u32[]{:S(2)}) collective-permute-start(bf16[32,3584]{1,0:T(8,128)(2,1)S(1)} %shard_map.134.refs_1_), channel_id=1, source_target_pairs={{0,1},{1,0},{2,3},{3,2},{4,5},{5,4},{6,7},{7,6},{8,9},{9,8},{10,11... | collective-permute-start | bytes 688136 | tf_op jit(solution)/shard_map/ppermute | solution.py:366
  21.4 1.9 %collective-permute-start.9 = (bf16[64,3584]{1,0:T(8,128)(2,1)S(1)}, bf16[64,3584]{1,0:T(8,128)(2,1)S(1)}, u32[]{:S(2)}, u32[]{:S(2)}) collective-permute-start(bf16[64,3584]{1,0:T(8,128)(2,1)S(1)} %get-tuple-element.50), channel_id=1, source_target_pairs={{0,1},{1,0},{2,3},{3,2},{4,5},{5,4},{6,7},{7,6},{8,9},{9,8},{10,11... | collective-permute-start | bytes 1376264 | tf_op jit(solution)/shard_map/ppermute | solution.py:366
  23.9 7.3 %collective-permute-start.10 = (bf16[32,3584]{1,0:T(8,128)(2,1)S(1)}, bf16[32,3584]{1,0:T(8,128)(2,1)S(1)}, u32[]{:S(2)}, u32[]{:S(2)}) collective-permute-start(bf16[32,3584]{1,0:T(8,128)(2,1)S(1)} %get-tuple-element.54), channel_id=1, source_target_pairs={{0,2},{1,3},{2,0},{3,1},{4,6},{5,7},{6,4},{7,5},{8,10},{9,11},{10,... | collective-permute-start | bytes 688136 | tf_op jit(solution)/shard_map/ppermute | solution.py:366
  31.2 6.5 %collective-permute-start.11 = (bf16[8,3584]{1,0:T(8,128)(2,1)S(1)}, bf16[8,3584]{1,0:T(8,128)(2,1)S(1)}, u32[]{:S(2)}, u32[]{:S(2)}) collective-permute-start(bf16[8,3584]{1,0:T(8,128)(2,1)S(1)} %get-tuple-element.56), channel_id=1, source_target_pairs={{0,12},{1,13},{2,14},{3,15},{4,8},{5,9},{6,10},{7,11},{8,4},{9,5},... | collective-permute-start | bytes 172040 | tf_op jit(solution)/shard_map/ppermute | solution.py:366
  33.4 5.6 %collective-permute-start.12 = (bf16[8,3584]{1,0:T(8,128)(2,1)S(1)}, bf16[8,3584]{1,0:T(8,128)(2,1)S(1)}, u32[]{:S(2)}, u32[]{:S(2)}) collective-permute-start(bf16[8,3584]{1,0:T(8,128)(2,1)S(1)} %get-tuple-element.57), channel_id=1, source_target_pairs={{0,8},{1,9},{2,10},{3,11},{4,12},{5,13},{6,14},{7,15},{8,0},{9,1},... | collective-permute-start | bytes 172040 | tf_op jit(solution)/shard_map/ppermute | solution.py:366
  34.2 4.8 %collective-permute-start.13 = (bf16[8,3584]{1,0:T(8,128)(2,1)S(1)}, bf16[8,3584]{1,0:T(8,128)(2,1)S(1)}, u32[]{:S(2)}, u32[]{:S(2)}) collective-permute-start(bf16[8,3584]{1,0:T(8,128)(2,1)S(1)} %get-tuple-element.58), channel_id=1, source_target_pairs={{0,4},{1,5},{2,6},{3,7},{4,0},{5,1},{6,2},{7,3},{8,12},{9,13},{10,... | collective-permute-start | bytes 172040 | tf_op jit(solution)/shard_map/ppermute | solution.py:366
  39.3 9.0 %collective-permute-start.17 = (bf16[32,2176]{1,0:T(8,128)(2,1)S(1)}, bf16[32,2176]{1,0:T(8,128)(2,1)S(1)}, u32[]{:S(2)}, u32[]{:S(2)}) collective-permute-start(bf16[32,2176]{1,0:T(8,128)(2,1)S(1)} %get-tuple-element.68), channel_id=1, source_target_pairs={{0,2},{1,3},{2,0},{3,1},{4,6},{5,7},{6,4},{7,5},{8,10},{9,11},{10,... | collective-permute-start | bytes 417800 | tf_op jit(solution)/shard_map/ppermute | solution.py:366
  40.5 6.5 %collective-permute-start.14 = (bf16[8,3584]{1,0:T(8,128)(2,1)S(1)}, bf16[8,3584]{1,0:T(8,128)(2,1)S(1)}, u32[]{:S(2)}, u32[]{:S(2)}) collective-permute-start(bf16[8,3584]{1,0:T(8,128)(2,1)S(1)} %get-tuple-element.63), channel_id=1, source_target_pairs={{0,12},{1,13},{2,14},{3,15},{4,8},{5,9},{6,10},{7,11},{8,4},{9,5},... | collective-permute-start | bytes 172040 | tf_op jit(solution)/shard_map/ppermute | solution.py:366
  42.6 5.6 %collective-permute-start.15 = (bf16[8,3584]{1,0:T(8,128)(2,1)S(1)}, bf16[8,3584]{1,0:T(8,128)(2,1)S(1)}, u32[]{:S(2)}, u32[]{:S(2)}) collective-permute-start(bf16[8,3584]{1,0:T(8,128)(2,1)S(1)} %get-tuple-element.64), channel_id=1, source_target_pairs={{0,8},{1,9},{2,10},{3,11},{4,12},{5,13},{6,14},{7,15},{8,0},{9,1},... | collective-permute-start | bytes 172040 | tf_op jit(solution)/shard_map/ppermute | solution.py:366
  42.7 5.6 %collective-permute-start.16 = (bf16[8,3584]{1,0:T(8,128)(2,1)S(1)}, bf16[8,3584]{1,0:T(8,128)(2,1)S(1)}, u32[]{:S(2)}, u32[]{:S(2)}) collective-permute-start(bf16[8,3584]{1,0:T(8,128)(2,1)S(1)} %get-tuple-element.65), channel_id=1, source_target_pairs={{0,4},{1,5},{2,6},{3,7},{4,0},{5,1},{6,2},{7,3},{8,12},{9,13},{10,... | collective-permute-start | bytes 172040 | tf_op jit(solution)/shard_map/ppermute | solution.py:366
  48.4 6.1 %collective-permute-start.18 = (bf16[32,3584]{1,0:T(8,128)(2,1)S(1)}, bf16[32,3584]{1,0:T(8,128)(2,1)S(1)}, u32[]{:S(2)}, u32[]{:S(2)}) collective-permute-start(bf16[32,3584]{1,0:T(8,128)(2,1)S(1)} %get-tuple-element.69.refs_1_.refs_0_), channel_id=1, source_target_pairs={{0,2},{1,3},{2,0},{3,1},{4,6},{5,7},{6,4},{7,5},{8,10},{9,11},{10,... | collective-permute-start | bytes 688136 | tf_op jit(solution)/shard_map/ppermute | solution.py:366
  56.0 5.1 %collective-permute-start.20 = (bf16[32,2176]{1,0:T(8,128)(2,1)S(1)}, bf16[32,2176]{1,0:T(8,128)(2,1)S(1)}, u32[]{:S(2)}, u32[]{:S(2)}) collective-permute-start(bf16[32,2176]{1,0:T(8,128)(2,1)S(1)} %get-tuple-element.71), channel_id=1, source_target_pairs={{0,2},{1,3},{2,0},{3,1},{4,6},{5,7},{6,4},{7,5},{8,10},{9,11},{10,... | collective-permute-start | bytes 417800 | tf_op jit(solution)/shard_map/ppermute | solution.py:366
  56.6 7.0 %collective-permute-start.24 = (bf16[8,2176]{1,0:T(8,128)(2,1)S(1)}, bf16[8,2176]{1,0:T(8,128)(2,1)S(1)}, u32[]{:S(2)}, u32[]{:S(2)}) collective-permute-start(bf16[8,2176]{1,0:T(8,128)(2,1)S(1)} %get-tuple-element.77), channel_id=1, source_target_pairs={{0,12},{1,13},{2,14},{3,15},{4,8},{5,9},{6,10},{7,11},{8,4},{9,5},... | collective-permute-start | bytes 104456 | tf_op jit(solution)/shard_map/ppermute | solution.py:366
  58.4 7.4 %collective-permute-start.25 = (bf16[8,2176]{1,0:T(8,128)(2,1)S(1)}, bf16[8,2176]{1,0:T(8,128)(2,1)S(1)}, u32[]{:S(2)}, u32[]{:S(2)}) collective-permute-start(bf16[8,2176]{1,0:T(8,128)(2,1)S(1)} %get-tuple-element.78), channel_id=1, source_target_pairs={{0,8},{1,9},{2,10},{3,11},{4,12},{5,13},{6,14},{7,15},{8,0},{9,1},... | collective-permute-start | bytes 104456 | tf_op jit(solution)/shard_map/ppermute | solution.py:366
  59.4 6.3 %collective-permute-start.26 = (bf16[8,2176]{1,0:T(8,128)(2,1)S(1)}, bf16[8,2176]{1,0:T(8,128)(2,1)S(1)}, u32[]{:S(2)}, u32[]{:S(2)}) collective-permute-start(bf16[8,2176]{1,0:T(8,128)(2,1)S(1)} %get-tuple-element.79), channel_id=1, source_target_pairs={{0,4},{1,5},{2,6},{3,7},{4,0},{5,1},{6,2},{7,3},{8,12},{9,13},{10,... | collective-permute-start | bytes 104456 | tf_op jit(solution)/shard_map/ppermute | solution.py:366
  61.3 5.8 %collective-permute-start.21 = (bf16[8,2176]{1,0:T(8,128)(2,1)S(1)}, bf16[8,2176]{1,0:T(8,128)(2,1)S(1)}, u32[]{:S(2)}, u32[]{:S(2)}) collective-permute-start(bf16[8,2176]{1,0:T(8,128)(2,1)S(1)} %get-tuple-element.73), channel_id=1, source_target_pairs={{0,12},{1,13},{2,14},{3,15},{4,8},{5,9},{6,10},{7,11},{8,4},{9,5},... | collective-permute-start | bytes 104456 | tf_op jit(solution)/shard_map/ppermute | solution.py:366
  63.2 4.9 %collective-permute-start.22 = (bf16[8,2176]{1,0:T(8,128)(2,1)S(1)}, bf16[8,2176]{1,0:T(8,128)(2,1)S(1)}, u32[]{:S(2)}, u32[]{:S(2)}) collective-permute-start(bf16[8,2176]{1,0:T(8,128)(2,1)S(1)} %get-tuple-element.74), channel_id=1, source_target_pairs={{0,8},{1,9},{2,10},{3,11},{4,12},{5,13},{6,14},{7,15},{8,0},{9,1},... | collective-permute-start | bytes 104456 | tf_op jit(solution)/shard_map/ppermute | solution.py:366
  63.6 4.5 %collective-permute-start.23 = (bf16[8,2176]{1,0:T(8,128)(2,1)S(1)}, bf16[8,2176]{1,0:T(8,128)(2,1)S(1)}, u32[]{:S(2)}, u32[]{:S(2)}) collective-permute-start(bf16[8,2176]{1,0:T(8,128)(2,1)S(1)} %get-tuple-element.75), channel_id=1, source_target_pairs={{0,4},{1,5},{2,6},{3,7},{4,0},{5,1},{6,2},{7,3},{8,12},{9,13},{10,... | collective-permute-start | bytes 104456 | tf_op jit(solution)/shard_map/ppermute | solution.py:366

commit v6 on v5

--- a/solution.py
+++ b/solution.py
@@ -173,6 +173,17 @@
         send[...] = total[at : at + rows].astype(BF16)
 
 
+def add_half_body(received, upper, keep, *refs):
+    parts, outs = refs[:received], refs[received:]
+    half = keep.shape[0] // 2
+    total = keep[half:, :] if upper else keep[:half, :]
+    total = sum((ref[...].astype(F32) for ref in parts), total)
+    rows = outs[0].shape[0]
+    for i, out in enumerate(outs):
+        at = (len(outs) - 1 - i) * rows
+        out[...] = total[at : at + rows].astype(out.dtype)
+
+
 def hidden_body(offsets, slices, passing, me, *refs):
     parts, (tokens, gain, ids, scores, *refs) = refs[: len(offsets)], refs[len(offsets) :]
     passed, outs = refs[:passing], refs[passing:]
@@ -235,7 +246,7 @@
 
 
 def late(width):
-    return width - width // 2 // BLOCK * BLOCK
+    return width - width // 8 // BLOCK * BLOCK
 
 
 def student_part(moved, moved_head, targets, start, stop):
@@ -250,7 +261,13 @@
 
 def add_student_body(parts, received, me, moved, moved_head, *refs):
     summands, refs = refs[: received + 1], refs[received + 1 + parts :]
-    add_split_body(received, *summands, *refs[:-parts])
+    total = sum((ref[...].astype(F32) for ref in summands[1:]), summands[0][...])
+    keep, *sends = refs[:-parts]
+    rows = keep.shape[0]
+    keep[...] = total[:rows]
+    for i, send in enumerate(sends):
+        at = (len(sends) // 2 - i // 2) * rows + (1 - i % 2) * rows // 2
+        send[...] = total[at : at + rows // 2].astype(BF16)
 
     @pl.when(me[0] % 2 == 0)
     def _():
@@ -456,7 +473,9 @@
     )
     outs = run(
         functools.partial(add_student_body, size_x, 1),
-        [((quarter, features), d) for d in [F32] + [BF16] * (size_x - 1)] + split_rows,
+        [((quarter, features), F32)]
+        + [((quarter // 2, features), BF16)] * (2 * (size_x - 1))
+        + split_rows,
         me,
         moved,
         moved_head,
@@ -464,11 +483,24 @@
         swap(send, 1),
         *stud_parts,
         scalars=1,
-        aliases={5 + i: size_x + i for i in range(size_x)},
-    )
-    keep, *sends = outs[:size_x]
-    stud_keep, *stud_sends = outs[size_x:]
-    summed = from_z(*take(add_x(keep, along(sends), add_split_body)))
+        aliases={5 + i: 2 * size_x - 1 + i for i in range(size_x)},
+    )
+    keep, *sends = outs[: 2 * size_x - 1]
+    stud_keep, *stud_sends = outs[2 * size_x - 1 :]
+    far, near_rows = along(sends[::2]), along(sends[1::2])
+    far = run(
+        functools.partial(add_half_body, size_x - 1, True),
+        [((tok_dev, features), BF16)] * (size_z // 2),
+        keep,
+        *far,
+    )
+    *near_rows, keep = run(
+        functools.partial(add_half_body, size_x - 1, False),
+        [((tok_dev, features), BF16)] * (size_z // 2 - 1) + [((tok_dev, features), F32)],
+        keep,
+        *near_rows,
+    )
+    summed = from_z(keep, [*far, *near_rows])
     outs = run(
         functools.partial(
             hidden_body,

time: 69.1 us -> 69.1 us (level)
  starting transfers between devices: 30.1 us -> 31.3 us
  waiting for transfers between devices: 27.9 us -> 27 us
    ppermute x27 -> x28, starting transfers between devices: 30.1 us -> 31.3 us  [swap(): lax.ppermute(values, 'expert', [(i, i ^ offset) for i in range(devices)])]
    ppermute x27 -> x28, waiting for transfers between devices: 27.9 us -> 27 us  [swap(): lax.ppermute(values, 'expert', [(i, i ^ offset) for i in range(devices)])]
    pallas_call x13 -> x14, Pallas kernels: 10.1 us -> 9.81 us  [call(): pl.pallas_call(run, out_shape=[kind(s, d) for s, d in outs], in_specs=[sm...]
  transfers between devices with their start and end apart: 27 -> 28, of which waited for: 15 -> 16; matrix products, arithmetic and copies ran while one was open for 0% -> 0% of each run, Pallas kernels for 11% -> 11%
where the time goes in v6:
time: 69.1 us; the launch traced here: 68.8 us
  starting transfers between devices  31.3 us (45%)
  waiting for transfers between devices  27 us (39%)
  Pallas kernels  9.81 us (14%)
  between operations  0.75 us (1%)
    ppermute x28, starting transfers between devices, swap(): lax.ppermute(values, 'expert', [(i, i ^ offset) for i in range(devices)])  31.3 us
    ppermute x28, waiting for transfers between devices, swap(): lax.ppermute(values, 'expert', [(i, i ^ offset) for i in range(devices)])  27 us
    pallas_call x14, Pallas kernels, call(): pl.pallas_call(run, out_shape=[kind(s, d) for s, d in outs], in_specs=[sm...  9.81 us
  transfers between devices with their start and end apart: 28, of which 16 were waited for; matrix products, arithmetic and copies ran while one was open for 0% of the time, Pallas kernels for 11%

profile of v6, /device:TPU:0, one launch (start us, length us, event | category | flops | bytes accessed | tf_op | source)
XLA Modules:
  0.0 68.8 jit_solution(4229117648234024615)
XLA Ops:
  0.6 0.5 collective-permute-start.2
  1.1 0.1 collective-permute-start.20
  1.2 5.0 %collective-permute-start.3 = (bf16[8,3584]{1,0:T(8,128)(2,1)}, bf16[8,3584]{1,0:T(8,128)(2,1)S(1)}, u32[]{:S(2)}, u32[]{:S(2)}) collective-permute-start(bf16[8,3584]{1,0:T(8,128)(2,1)} %refs_1_.1), channel_id=1, source_target_pairs={{0,12},{1,13},{2,14},{3,15},{4,8},{5,9},{6,10},{7,11},{8,4},{9,5},... | collective-permute-start | bytes 172040 | tf_op jit(solution)/shard_map/ppermute | solution.py:383
  6.3 0.0 collective-permute-start.4
  6.3 0.6 collective-permute-start.5
  6.8 2.4 %collective-permute-done.3.refs_2_.refs_1_ = bf16[8,3584]{1,0:T(8,128)(2,1)S(1)} collective-permute-done((bf16[8,3584]{1,0:T(8,128)(2,1)}, bf16[8,3584]{1,0:T(8,128)(2,1)S(1)}, u32[]{:S(2)}, u32[]{:S(2)}) %collective-permute-start.3) | collective-permute-done | bytes 57376 | tf_op jit(solution)/shard_map/ppermute | solution.py:383
  9.2 0.9 %shard_map.131 = (f32[3584]{0:T(1024)S(1)}, bf16[8,3584]{1,0:T(8,128)(2,1)S(1)}) custom-call(f32[3584]{0:T(1024)} %refs_0_.2, bf16[8,3584]{1,0:T(8,128)(2,1)} %refs_1_.1, bf16[8,3584]{1,0:T(8,128)(2,1)S(1)} %collective-permute-done.3.refs_2_.refs_1_), custom_call_target="tpu_custom_call" | custom-call | tf_op jit(solution)/shard_map/pallas_call | solution.py:83
  10.0 1.0 %collective-permute-done.4.refs_2_ = bf16[8,3584]{1,0:T(8,128)(2,1)S(1)} collective-permute-done((bf16[8,3584]{1,0:T(8,128)(2,1)}, bf16[8,3584]{1,0:T(8,128)(2,1)S(1)}, u32[]{:S(2)}, u32[]{:S(2)}) %collective-permute-start.4) | collective-permute-done | bytes 57376 | tf_op jit(solution)/shard_map/ppermute | solution.py:383
  11.0 1.2 %collective-permute-done.5.refs_3_ = bf16[8,3584]{1,0:T(8,128)(2,1)S(1)} collective-permute-done((bf16[8,3584]{1,0:T(8,128)(2,1)}, bf16[8,3584]{1,0:T(8,128)(2,1)S(1)}, u32[]{:S(2)}, u32[]{:S(2)}) %collective-permute-start.5) | collective-permute-done | bytes 57376 | tf_op jit(solution)/shard_map/ppermute | solution.py:383
  12.2 0.2 shard_map.132.refs_13_.refs_0_
  12.3 1.6 %collective-permute-start.6 = (bf16[32,3584]{1,0:T(8,128)(2,1)S(1)}, bf16[32,3584]{1,0:T(8,128)(2,1)S(1)}, u32[]{:S(2)}, u32[]{:S(2)}) collective-permute-start(bf16[32,3584]{1,0:T(8,128)(2,1)S(1)} %shard_map.132.refs_13_.refs_0_), channel_id=1, source_target_pairs={{0,2},{1,3},{2,0},{3,1},{4,6},{5,7},{6,4},{7,5},{8,10},{9,11},{10,... | collective-permute-start | bytes 688136 | tf_op jit(solution)/shard_map/ppermute | solution.py:383
  13.9 0.0 collective-permute-start.1
  13.9 0.5 collective-permute-start
  14.4 1.0 %collective-permute-done.refs_1_ = s32[1,256]{1,0:T(1,128)S(1)} collective-permute-done((s32[1,256]{1,0:T(1,128)}, s32[1,256]{1,0:T(1,128)S(1)}, u32[]{:S(2)}, u32[]{:S(2)}) %collective-permute-start) | collective-permute-done | bytes 1056 | tf_op jit(solution)/shard_map/ppermute | solution.py:383
  15.4 0.3 collective-permute-start.7
  15.7 0.0 collective-permute-done.1.refs_2_
  15.8 0.0 collective-permute-done.2.refs_3_
  15.8 3.1 %shard_map.133 = (f32[64,512]{1,0:T(8,128)S(1)}, bf16[2048,512]{1,0:T(8,128)(2,1)S(1)}, f32[32,2176]{1,0:T(8,128)S(1)}, bf16[32,2176]{1,0:T(8,128)(2,1)S(1)}, bf...) custom-call(s32[1]{0:T(128)} %bitcast.refs_0_, ...), custom_call_target="tpu_custom_call" | custom-call | flops 671088640 | bytes 5512256 | tf_op jit(solution)/shard_map/pallas_call | solution.py:83
  18.8 0.0 collective-permute-done.6.refs_0_
  18.9 0.3 collective-permute-start.8
  19.1 0.0 collective-permute-done.7.refs_2_
  19.1 1.3 %collective-permute-done.8.refs_3_ = bf16[32,3584]{1,0:T(8,128)(2,1)S(1)} collective-permute-done((bf16[32,3584]{1,0:T(8,128)(2,1)S(1)}, bf16[32,3584]{1,0:T(8,128)(2,1)S(1)}, u32[]{:S(2)}, u32[]{:S(2)}) %collective-permute-start.8) | collective-permute-done | bytes 229408 | tf_op jit(solution)/shard_map/ppermute | solution.py:383
  20.4 1.0 %shard_map.135 = (f32[64,3584]{1,0:T(8,128)S(1)}, bf16[64,3584]{1,0:T(8,128)(2,1)S(1)}) custom-call(bf16[32,3584]{1,0:T(8,128)(2,1)S(1)} %shard_map.132.refs_13_.refs_0_, bf16[32,3584]{1,0:T(8,128)(2,1)S(1)} %shard_map.134.refs_1_, bf16[32,3584]{1,0:T(8,128)(2,1)S(1)} %collective-permute-done.7.refs_2_, bf16[32,3584]{1,0:T(8,128)(2,1)S(1)} %collective-permute-done.8.refs_3_, ...), custom_call_target="tpu_custom_call" | custom-call | tf_op jit(solution)/shard_map/pallas_call | solution.py:83
  21.4 0.3 collective-permute-start.9
  21.7 1.6 %collective-permute-done.9.refs_4_ = bf16[64,3584]{1,0:T(8,128)(2,1)S(1)} collective-permute-done((bf16[64,3584]{1,0:T(8,128)(2,1)S(1)}, bf16[64,3584]{1,0:T(8,128)(2,1)S(1)}, u32[]{:S(2)}, u32[]{:S(2)}) %collective-permute-start.9) | collective-permute-done | bytes 458784 | tf_op jit(solution)/shard_map/ppermute | solution.py:383
  23.3 0.3 shard_map.136
  23.6 1.1 %collective-permute-start.11 = (bf16[16,3584]{1,0:T(8,128)(2,1)S(1)}, bf16[16,3584]{1,0:T(8,128)(2,1)S(1)}, u32[]{:S(2)}, u32[]{:S(2)}) collective-permute-start(bf16[16,3584]{1,0:T(8,128)(2,1)S(1)} %get-tuple-element.57), channel_id=1, source_target_pairs={{0,2},{1,3},{2,0},{3,1},{4,6},{5,7},{6,4},{7,5},{8,10},{9,11},{10,... | collective-permute-start | bytes 344072 | tf_op jit(solution)/shard_map/ppermute | solution.py:383
  24.8 1.0 %collective-permute-start.10 = (bf16[16,3584]{1,0:T(8,128)(2,1)S(1)}, bf16[16,3584]{1,0:T(8,128)(2,1)S(1)}, u32[]{:S(2)}, u32[]{:S(2)}) collective-permute-start(bf16[16,3584]{1,0:T(8,128)(2,1)S(1)} %get-tuple-element.55), channel_id=1, source_target_pairs={{0,2},{1,3},{2,0},{3,1},{4,6},{5,7},{6,4},{7,5},{8,10},{9,11},{10,... | collective-permute-start | bytes 344072 | tf_op jit(solution)/shard_map/ppermute | solution.py:383
  25.7 4.0 %collective-permute-done.11.refs_1_ = bf16[16,3584]{1,0:T(8,128)(2,1)S(1)} collective-permute-done((bf16[16,3584]{1,0:T(8,128)(2,1)S(1)}, bf16[16,3584]{1,0:T(8,128)(2,1)S(1)}, u32[]{:S(2)}, u32[]{:S(2)}) %collective-permute-start.11) | collective-permute-done | bytes 114720 | tf_op jit(solution)/shard_map/ppermute | solution.py:383
  29.7 2.2 %collective-permute-start.12 = (bf16[8,3584]{1,0:T(8,128)(2,1)S(1)}, bf16[8,3584]{1,0:T(8,128)(2,1)S(1)}, u32[]{:S(2)}, u32[]{:S(2)}) collective-permute-start(bf16[8,3584]{1,0:T(8,128)(2,1)S(1)} %get-tuple-element.58), channel_id=1, source_target_pairs={{0,12},{1,13},{2,14},{3,15},{4,8},{5,9},{6,10},{7,11},{8,4},{9,5},... | collective-permute-start | bytes 172040 | tf_op jit(solution)/shard_map/ppermute | solution.py:383
  31.9 0.8 %collective-permute-start.13 = (bf16[8,3584]{1,0:T(8,128)(2,1)S(1)}, bf16[8,3584]{1,0:T(8,128)(2,1)S(1)}, u32[]{:S(2)}, u32[]{:S(2)}) collective-permute-start(bf16[8,3584]{1,0:T(8,128)(2,1)S(1)} %get-tuple-element.59), channel_id=1, source_target_pairs={{0,8},{1,9},{2,10},{3,11},{4,12},{5,13},{6,14},{7,15},{8,0},{9,1},... | collective-permute-start | bytes 172040 | tf_op jit(solution)/shard_map/ppermute | solution.py:383
  32.7 0.0 collective-permute-done.10.refs_1_
  32.7 1.6 %collective-permute-start.14 = (bf16[8,3584]{1,0:T(8,128)(2,1)S(1)}, bf16[8,3584]{1,0:T(8,128)(2,1)S(1)}, u32[]{:S(2)}, u32[]{:S(2)}) collective-permute-start(bf16[8,3584]{1,0:T(8,128)(2,1)S(1)} %get-tuple-element.60), channel_id=1, source_target_pairs={{0,4},{1,5},{2,6},{3,7},{4,0},{5,1},{6,2},{7,3},{8,12},{9,13},{10,... | collective-permute-start | bytes 172040 | tf_op jit(solution)/shard_map/ppermute | solution.py:383
  34.3 1.5 %collective-permute-done.12.refs_2_ = bf16[8,3584]{1,0:T(8,128)(2,1)S(1)} collective-permute-done((bf16[8,3584]{1,0:T(8,128)(2,1)S(1)}, bf16[8,3584]{1,0:T(8,128)(2,1)S(1)}, u32[]{:S(2)}, u32[]{:S(2)}) %collective-permute-start.12) | collective-permute-done | bytes 57376 | tf_op jit(solution)/shard_map/ppermute | solution.py:383
  35.8 1.4 %collective-permute-done.13.refs_3_ = bf16[8,3584]{1,0:T(8,128)(2,1)S(1)} collective-permute-done((bf16[8,3584]{1,0:T(8,128)(2,1)S(1)}, bf16[8,3584]{1,0:T(8,128)(2,1)S(1)}, u32[]{:S(2)}, u32[]{:S(2)}) %collective-permute-start.13) | collective-permute-done | bytes 57376 | tf_op jit(solution)/shard_map/ppermute | solution.py:383
  37.2 0.4 collective-permute-done.14.refs_4_
  37.6 0.2 shard_map.139
  37.8 1.1 %collective-permute-start.18 = (bf16[32,2176]{1,0:T(8,128)(2,1)S(1)}, bf16[32,2176]{1,0:T(8,128)(2,1)S(1)}, u32[]{:S(2)}, u32[]{:S(2)}) collective-permute-start(bf16[32,2176]{1,0:T(8,128)(2,1)S(1)} %get-tuple-element.70), channel_id=1, source_target_pairs={{0,2},{1,3},{2,0},{3,1},{4,6},{5,7},{6,4},{7,5},{8,10},{9,11},{10,... | collective-permute-start | bytes 417800 | tf_op jit(solution)/shard_map/ppermute | solution.py:383
  39.0 2.0 %collective-permute-start.15 = (bf16[8,3584]{1,0:T(8,128)(2,1)S(1)}, bf16[8,3584]{1,0:T(8,128)(2,1)S(1)}, u32[]{:S(2)}, u32[]{:S(2)}) collective-permute-start(bf16[8,3584]{1,0:T(8,128)(2,1)S(1)} %get-tuple-element.65), channel_id=1, source_target_pairs={{0,12},{1,13},{2,14},{3,15},{4,8},{5,9},{6,10},{7,11},{8,4},{9,5},... | collective-permute-start | bytes 172040 | tf_op jit(solution)/shard_map/ppermute | solution.py:383
  41.0 0.3 collective-permute-start.16
  41.3 2.0 %collective-permute-start.17 = (bf16[8,3584]{1,0:T(8,128)(2,1)S(1)}, bf16[8,3584]{1,0:T(8,128)(2,1)S(1)}, u32[]{:S(2)}, u32[]{:S(2)}) collective-permute-start(bf16[8,3584]{1,0:T(8,128)(2,1)S(1)} %get-tuple-element.67), channel_id=1, source_target_pairs={{0,4},{1,5},{2,6},{3,7},{4,0},{5,1},{6,2},{7,3},{8,12},{9,13},{10,... | collective-permute-start | bytes 172040 | tf_op jit(solution)/shard_map/ppermute | solution.py:383
  43.4 1.6 %collective-permute-done.15.refs_0_ = bf16[8,3584]{1,0:T(8,128)(2,1)S(1)} collective-permute-done((bf16[8,3584]{1,0:T(8,128)(2,1)S(1)}, bf16[8,3584]{1,0:T(8,128)(2,1)S(1)}, u32[]{:S(2)}, u32[]{:S(2)}) %collective-permute-start.15) | collective-permute-done | bytes 57376 | tf_op jit(solution)/shard_map/ppermute | solution.py:383
  44.9 1.7 %collective-permute-done.16.refs_1_ = bf16[8,3584]{1,0:T(8,128)(2,1)S(1)} collective-permute-done((bf16[8,3584]{1,0:T(8,128)(2,1)S(1)}, bf16[8,3584]{1,0:T(8,128)(2,1)S(1)}, u32[]{:S(2)}, u32[]{:S(2)}) %collective-permute-start.16) | collective-permute-done | bytes 57376 | tf_op jit(solution)/shard_map/ppermute | solution.py:383
  46.6 0.0 collective-permute-done.17.refs_2_
  46.6 0.0 collective-permute-done.18.refs_5_
  46.6 0.2 shard_map.140
  46.8 0.6 collective-permute-start.19
  47.4 1.5 %shard_map.141.refs_2_ = bf16[3584,256]{1,0:T(8,128)(2,1)S(1)} custom-call(bf16[3584,256]{1,0:T(8,128)(2,1)} %refs_0_.3, bf16[32,3584]{1,0:T(8,128)(2,1)S(1)} %get-tuple-element.71.refs_1_.refs_0_), custom_call_target="tpu_custom_call" | custom-call | bytes 1835008 | tf_op jit(solution)/shard_map/pallas_call | solution.py:83
  48.9 5.4 %collective-permute-done.19.refs_1_ = bf16[32,3584]{1,0:T(8,128)(2,1)S(1)} collective-permute-done((bf16[32,3584]{1,0:T(8,128)(2,1)S(1)}, bf16[32,3584]{1,0:T(8,128)(2,1)S(1)}, u32[]{:S(2)}, u32[]{:S(2)}) %collective-permute-start.19) | collective-permute-done | bytes 229408 | tf_op jit(solution)/shard_map/ppermute | solution.py:383
  54.4 1.5 %shard_map.142 = (f32[32,2176]{1,0:T(8,128)S(1)}, bf16[32,2176]{1,0:T(8,128)(2,1)S(1)}) custom-call(bf16[32,3584]{1,0:T(8,128)(2,1)S(1)} %get-tuple-element.71.refs_1_.refs_0_, bf16[32,3584]{1,0:T(8,128)(2,1)S(1)} %collective-permute-done.19.refs_1_, bf16[3584,256]{1,0:T(8,128)(2,1)S(1)} %shard_map.141.refs_2_, ...), custom_call_target="tpu_custom_call" | custom-call | tf_op jit(solution)/shard_map/pallas_call | solution.py:83
  55.9 0.6 collective-permute-start.21
  56.5 2.0 %collective-permute-start.25 = (bf16[8,2176]{1,0:T(8,128)(2,1)S(1)}, bf16[8,2176]{1,0:T(8,128)(2,1)S(1)}, u32[]{:S(2)}, u32[]{:S(2)}) collective-permute-start(bf16[8,2176]{1,0:T(8,128)(2,1)S(1)} %get-tuple-element.79), channel_id=1, source_target_pairs={{0,12},{1,13},{2,14},{3,15},{4,8},{5,9},{6,10},{7,11},{8,4},{9,5},... | collective-permute-start | bytes 104456 | tf_op jit(solution)/shard_map/ppermute | solution.py:383
  58.5 0.8 %collective-permute-start.26 = (bf16[8,2176]{1,0:T(8,128)(2,1)S(1)}, bf16[8,2176]{1,0:T(8,128)(2,1)S(1)}, u32[]{:S(2)}, u32[]{:S(2)}) collective-permute-start(bf16[8,2176]{1,0:T(8,128)(2,1)S(1)} %get-tuple-element.80), channel_id=1, source_target_pairs={{0,8},{1,9},{2,10},{3,11},{4,12},{5,13},{6,14},{7,15},{8,0},{9,1},... | collective-permute-start | bytes 104456 | tf_op jit(solution)/shard_map/ppermute | solution.py:383
  59.3 1.6 %collective-permute-start.27 = (bf16[8,2176]{1,0:T(8,128)(2,1)S(1)}, bf16[8,2176]{1,0:T(8,128)(2,1)S(1)}, u32[]{:S(2)}, u32[]{:S(2)}) collective-permute-start(bf16[8,2176]{1,0:T(8,128)(2,1)S(1)} %get-tuple-element.81), channel_id=1, source_target_pairs={{0,4},{1,5},{2,6},{3,7},{4,0},{5,1},{6,2},{7,3},{8,12},{9,13},{10,... | collective-permute-start | bytes 104456 | tf_op jit(solution)/shard_map/ppermute | solution.py:383
  60.9 0.1 collective-permute-done.21.refs_1_
  61.0 0.1 shard_map.143
  61.1 2.1 %collective-permute-start.22 = (bf16[8,2176]{1,0:T(8,128)(2,1)S(1)}, bf16[8,2176]{1,0:T(8,128)(2,1)S(1)}, u32[]{:S(2)}, u32[]{:S(2)}) collective-permute-start(bf16[8,2176]{1,0:T(8,128)(2,1)S(1)} %get-tuple-element.75), channel_id=1, source_target_pairs={{0,12},{1,13},{2,14},{3,15},{4,8},{5,9},{6,10},{7,11},{8,4},{9,5},... | collective-permute-start | bytes 104456 | tf_op jit(solution)/shard_map/ppermute | solution.py:383
  63.2 0.4 collective-permute-start.23
  63.6 0.0 collective-permute-done.25.refs_5_
  63.6 2.0 %collective-permute-start.24 = (bf16[8,2176]{1,0:T(8,128)(2,1)S(1)}, bf16[8,2176]{1,0:T(8,128)(2,1)S(1)}, u32[]{:S(2)}, u32[]{:S(2)}) collective-permute-start(bf16[8,2176]{1,0:T(8,128)(2,1)S(1)} %get-tuple-element.77), channel_id=1, source_target_pairs={{0,4},{1,5},{2,6},{3,7},{4,0},{5,1},{6,2},{7,3},{8,12},{9,13},{10,... | collective-permute-start | bytes 104456 | tf_op jit(solution)/shard_map/ppermute | solution.py:383
  65.6 1.3 %collective-permute-done.22.refs_1_ = bf16[8,2176]{1,0:T(8,128)(2,1)S(1)} collective-permute-done((bf16[8,2176]{1,0:T(8,128)(2,1)S(1)}, bf16[8,2176]{1,0:T(8,128)(2,1)S(1)}, u32[]{:S(2)}, u32[]{:S(2)}) %collective-permute-start.22) | collective-permute-done | bytes 34848 | tf_op jit(solution)/shard_map/ppermute | solution.py:383
  66.9 1.1 %collective-permute-done.23.refs_2_ = bf16[8,2176]{1,0:T(8,128)(2,1)S(1)} collective-permute-done((bf16[8,2176]{1,0:T(8,128)(2,1)S(1)}, bf16[8,2176]{1,0:T(8,128)(2,1)S(1)}, u32[]{:S(2)}, u32[]{:S(2)}) %collective-permute-start.23) | collective-permute-done | bytes 34848 | tf_op jit(solution)/shard_map/ppermute | solution.py:383
  68.1 0.0 collective-permute-done.24.refs_3_
  68.1 0.8 %shard_map.144 = (f32[1,8]{1,0:T(1,128)}, f32[8,2048]{1,0:T(8,128)}) custom-call(f32[8,2176]{1,0:T(8,128)S(1)} %get-tuple-element.74.refs_0_, bf16[8,2176]{1,0:T(8,128)(2,1)S(1)} %collective-permute-done.22.refs_1_, bf16[8,2176]{1,0:T(8,128)(2,1)S(1)} %collective-permute-done.23.refs_2_, bf16[8,2176]{1,0:T(8,128)(2,1)S(1)} %collective-permute-done.24.refs_3_, ...), custom_call_target="tpu_custom_call" | custom-call | tf_op jit(solution)/shard_map/pallas_call | solution.py:83
  (6 shorter events, 0.1 us)
Async XLA Ops:
  0.6 15.1 %collective-permute-start.2 = (bf16[2048,256]{1,0:T(8,128)(2,1)}, bf16[2048,256]{1,0:T(8,128)(2,1)S(1)}, u32[]{:S(2)}, u32[]{:S(2)}) collective-permute-start(bf16[2048,256]{1,0:T(8,128)(2,1)} %refs_6_.1), channel_id=1, source_target_pairs={{0,1},{1,0},{2,3},{3,2},{4,5},{5,4},{6,7},{7,6},{8,9},{9,8},{10,11... | collective-permute-start | bytes 3145736 | tf_op jit(solution)/shard_map/ppermute | solution.py:383
  1.1 47.8 %collective-permute-start.20 = (bf16[3584,256]{1,0:T(8,128)(2,1)}, bf16[3584,256]{1,0:T(8,128)(2,1)S(1)}, u32[]{:S(2)}, u32[]{:S(2)}) collective-permute-start(bf16[3584,256]{1,0:T(8,128)(2,1)} %refs_0_.3), channel_id=1, source_target_pairs={{0,1},{1,0},{2,3},{3,2},{4,5},{5,4},{6,7},{7,6},{8,9},{9,8},{10,11... | collective-permute-start | bytes 5505032 | tf_op jit(solution)/shard_map/ppermute | solution.py:383
  1.2 8.0 %collective-permute-start.3 = (bf16[8,3584]{1,0:T(8,128)(2,1)}, bf16[8,3584]{1,0:T(8,128)(2,1)S(1)}, u32[]{:S(2)}, u32[]{:S(2)}) collective-permute-start(bf16[8,3584]{1,0:T(8,128)(2,1)} %refs_1_.1), channel_id=1, source_target_pairs={{0,12},{1,13},{2,14},{3,15},{4,8},{5,9},{6,10},{7,11},{8,4},{9,5},... | collective-permute-start | bytes 172040 | tf_op jit(solution)/shard_map/ppermute | solution.py:383
  6.3 4.7 %collective-permute-start.4 = (bf16[8,3584]{1,0:T(8,128)(2,1)}, bf16[8,3584]{1,0:T(8,128)(2,1)S(1)}, u32[]{:S(2)}, u32[]{:S(2)}) collective-permute-start(bf16[8,3584]{1,0:T(8,128)(2,1)} %refs_1_.1), channel_id=1, source_target_pairs={{0,4},{1,5},{2,6},{3,7},{4,0},{5,1},{6,2},{7,3},{8,12},{9,13},{10,... | collective-permute-start | bytes 172040 | tf_op jit(solution)/shard_map/ppermute | solution.py:383
  6.3 5.9 %collective-permute-start.5 = (bf16[8,3584]{1,0:T(8,128)(2,1)}, bf16[8,3584]{1,0:T(8,128)(2,1)S(1)}, u32[]{:S(2)}, u32[]{:S(2)}) collective-permute-start(bf16[8,3584]{1,0:T(8,128)(2,1)} %refs_1_.1), channel_id=1, source_target_pairs={{0,8},{1,9},{2,10},{3,11},{4,12},{5,13},{6,14},{7,15},{8,0},{9,1},... | collective-permute-start | bytes 172040 | tf_op jit(solution)/shard_map/ppermute | solution.py:383
  12.3 6.5 %collective-permute-start.6 = (bf16[32,3584]{1,0:T(8,128)(2,1)S(1)}, bf16[32,3584]{1,0:T(8,128)(2,1)S(1)}, u32[]{:S(2)}, u32[]{:S(2)}) collective-permute-start(bf16[32,3584]{1,0:T(8,128)(2,1)S(1)} %shard_map.132.refs_13_.refs_0_), channel_id=1, source_target_pairs={{0,2},{1,3},{2,0},{3,1},{4,6},{5,7},{6,4},{7,5},{8,10},{9,11},{10,... | collective-permute-start | bytes 688136 | tf_op jit(solution)/shard_map/ppermute | solution.py:383
  13.9 1.9 %collective-permute-start.1 = (bf16[128,256]{1,0:T(8,128)(2,1)}, bf16[128,256]{1,0:T(8,128)(2,1)S(1)}, u32[]{:S(2)}, u32[]{:S(2)}) collective-permute-start(bf16[128,256]{1,0:T(8,128)(2,1)} %refs_5_.1), channel_id=1, source_target_pairs={{0,1},{1,0},{2,3},{3,2},{4,5},{5,4},{6,7},{7,6},{8,9},{9,8},{10,11... | collective-permute-start | bytes 196616 | tf_op jit(solution)/shard_map/ppermute | solution.py:383
  13.9 1.5 %collective-permute-start = (s32[1,256]{1,0:T(1,128)}, s32[1,256]{1,0:T(1,128)S(1)}, u32[]{:S(2)}, u32[]{:S(2)}) collective-permute-start(s32[1,256]{1,0:T(1,128)} %bitcast.5), channel_id=1, source_target_pairs={{0,1},{1,0},{2,3},{3,2},{4,5},{5,4},{6,7},{7,6},{8,9},{9,8},{10,11... | collective-permute-start | bytes 3080 | tf_op jit(solution)/shard_map/ppermute | solution.py:383
  15.4 3.7 %collective-permute-start.7 = (bf16[32,3584]{1,0:T(8,128)(2,1)S(1)}, bf16[32,3584]{1,0:T(8,128)(2,1)S(1)}, u32[]{:S(2)}, u32[]{:S(2)}) collective-permute-start(bf16[32,3584]{1,0:T(8,128)(2,1)S(1)} %shard_map.132.refs_13_.refs_0_), channel_id=1, source_target_pairs={{0,1},{1,0},{2,3},{3,2},{4,5},{5,4},{6,7},{7,6},{8,9},{9,8},{10,11... | collective-permute-start | bytes 688136 | tf_op jit(solution)/shard_map/ppermute | solution.py:383
  18.9 1.6 %collective-permute-start.8 = (bf16[32,3584]{1,0:T(8,128)(2,1)S(1)}, bf16[32,3584]{1,0:T(8,128)(2,1)S(1)}, u32[]{:S(2)}, u32[]{:S(2)}) collective-permute-start(bf16[32,3584]{1,0:T(8,128)(2,1)S(1)} %shard_map.134.refs_1_), channel_id=1, source_target_pairs={{0,1},{1,0},{2,3},{3,2},{4,5},{5,4},{6,7},{7,6},{8,9},{9,8},{10,11... | collective-permute-start | bytes 688136 | tf_op jit(solution)/shard_map/ppermute | solution.py:383
  21.4 1.9 %collective-permute-start.9 = (bf16[64,3584]{1,0:T(8,128)(2,1)S(1)}, bf16[64,3584]{1,0:T(8,128)(2,1)S(1)}, u32[]{:S(2)}, u32[]{:S(2)}) collective-permute-start(bf16[64,3584]{1,0:T(8,128)(2,1)S(1)} %get-tuple-element.51), channel_id=1, source_target_pairs={{0,1},{1,0},{2,3},{3,2},{4,5},{5,4},{6,7},{7,6},{8,9},{9,8},{10,11... | collective-permute-start | bytes 1376264 | tf_op jit(solution)/shard_map/ppermute | solution.py:383
  23.6 6.1 %collective-permute-start.11 = (bf16[16,3584]{1,0:T(8,128)(2,1)S(1)}, bf16[16,3584]{1,0:T(8,128)(2,1)S(1)}, u32[]{:S(2)}, u32[]{:S(2)}) collective-permute-start(bf16[16,3584]{1,0:T(8,128)(2,1)S(1)} %get-tuple-element.57), channel_id=1, source_target_pairs={{0,2},{1,3},{2,0},{3,1},{4,6},{5,7},{6,4},{7,5},{8,10},{9,11},{10,... | collective-permute-start | bytes 344072 | tf_op jit(solution)/shard_map/ppermute | solution.py:383
  24.8 7.9 %collective-permute-start.10 = (bf16[16,3584]{1,0:T(8,128)(2,1)S(1)}, bf16[16,3584]{1,0:T(8,128)(2,1)S(1)}, u32[]{:S(2)}, u32[]{:S(2)}) collective-permute-start(bf16[16,3584]{1,0:T(8,128)(2,1)S(1)} %get-tuple-element.55), channel_id=1, source_target_pairs={{0,2},{1,3},{2,0},{3,1},{4,6},{5,7},{6,4},{7,5},{8,10},{9,11},{10,... | collective-permute-start | bytes 344072 | tf_op jit(solution)/shard_map/ppermute | solution.py:383
  29.7 6.0 %collective-permute-start.12 = (bf16[8,3584]{1,0:T(8,128)(2,1)S(1)}, bf16[8,3584]{1,0:T(8,128)(2,1)S(1)}, u32[]{:S(2)}, u32[]{:S(2)}) collective-permute-start(bf16[8,3584]{1,0:T(8,128)(2,1)S(1)} %get-tuple-element.58), channel_id=1, source_target_pairs={{0,12},{1,13},{2,14},{3,15},{4,8},{5,9},{6,10},{7,11},{8,4},{9,5},... | collective-permute-start | bytes 172040 | tf_op jit(solution)/shard_map/ppermute | solution.py:383
  31.9 5.3 %collective-permute-start.13 = (bf16[8,3584]{1,0:T(8,128)(2,1)S(1)}, bf16[8,3584]{1,0:T(8,128)(2,1)S(1)}, u32[]{:S(2)}, u32[]{:S(2)}) collective-permute-start(bf16[8,3584]{1,0:T(8,128)(2,1)S(1)} %get-tuple-element.59), channel_id=1, source_target_pairs={{0,8},{1,9},{2,10},{3,11},{4,12},{5,13},{6,14},{7,15},{8,0},{9,1},... | collective-permute-start | bytes 172040 | tf_op jit(solution)/shard_map/ppermute | solution.py:383
  32.7 4.9 %collective-permute-start.14 = (bf16[8,3584]{1,0:T(8,128)(2,1)S(1)}, bf16[8,3584]{1,0:T(8,128)(2,1)S(1)}, u32[]{:S(2)}, u32[]{:S(2)}) collective-permute-start(bf16[8,3584]{1,0:T(8,128)(2,1)S(1)} %get-tuple-element.60), channel_id=1, source_target_pairs={{0,4},{1,5},{2,6},{3,7},{4,0},{5,1},{6,2},{7,3},{8,12},{9,13},{10,... | collective-permute-start | bytes 172040 | tf_op jit(solution)/shard_map/ppermute | solution.py:383
  37.8 8.8 %collective-permute-start.18 = (bf16[32,2176]{1,0:T(8,128)(2,1)S(1)}, bf16[32,2176]{1,0:T(8,128)(2,1)S(1)}, u32[]{:S(2)}, u32[]{:S(2)}) collective-permute-start(bf16[32,2176]{1,0:T(8,128)(2,1)S(1)} %get-tuple-element.70), channel_id=1, source_target_pairs={{0,2},{1,3},{2,0},{3,1},{4,6},{5,7},{6,4},{7,5},{8,10},{9,11},{10,... | collective-permute-start | bytes 417800 | tf_op jit(solution)/shard_map/ppermute | solution.py:383
  39.0 6.0 %collective-permute-start.15 = (bf16[8,3584]{1,0:T(8,128)(2,1)S(1)}, bf16[8,3584]{1,0:T(8,128)(2,1)S(1)}, u32[]{:S(2)}, u32[]{:S(2)}) collective-permute-start(bf16[8,3584]{1,0:T(8,128)(2,1)S(1)} %get-tuple-element.65), channel_id=1, source_target_pairs={{0,12},{1,13},{2,14},{3,15},{4,8},{5,9},{6,10},{7,11},{8,4},{9,5},... | collective-permute-start | bytes 172040 | tf_op jit(solution)/shard_map/ppermute | solution.py:383
  41.0 5.6 %collective-permute-start.16 = (bf16[8,3584]{1,0:T(8,128)(2,1)S(1)}, bf16[8,3584]{1,0:T(8,128)(2,1)S(1)}, u32[]{:S(2)}, u32[]{:S(2)}) collective-permute-start(bf16[8,3584]{1,0:T(8,128)(2,1)S(1)} %get-tuple-element.66), channel_id=1, source_target_pairs={{0,8},{1,9},{2,10},{3,11},{4,12},{5,13},{6,14},{7,15},{8,0},{9,1},... | collective-permute-start | bytes 172040 | tf_op jit(solution)/shard_map/ppermute | solution.py:383
  41.3 5.3 %collective-permute-start.17 = (bf16[8,3584]{1,0:T(8,128)(2,1)S(1)}, bf16[8,3584]{1,0:T(8,128)(2,1)S(1)}, u32[]{:S(2)}, u32[]{:S(2)}) collective-permute-start(bf16[8,3584]{1,0:T(8,128)(2,1)S(1)} %get-tuple-element.67), channel_id=1, source_target_pairs={{0,4},{1,5},{2,6},{3,7},{4,0},{5,1},{6,2},{7,3},{8,12},{9,13},{10,... | collective-permute-start | bytes 172040 | tf_op jit(solution)/shard_map/ppermute | solution.py:383
  46.8 7.6 %collective-permute-start.19 = (bf16[32,3584]{1,0:T(8,128)(2,1)S(1)}, bf16[32,3584]{1,0:T(8,128)(2,1)S(1)}, u32[]{:S(2)}, u32[]{:S(2)}) collective-permute-start(bf16[32,3584]{1,0:T(8,128)(2,1)S(1)} %get-tuple-element.71.refs_1_.refs_0_), channel_id=1, source_target_pairs={{0,2},{1,3},{2,0},{3,1},{4,6},{5,7},{6,4},{7,5},{8,10},{9,11},{10,... | collective-permute-start | bytes 688136 | tf_op jit(solution)/shard_map/ppermute | solution.py:383
  55.9 5.1 %collective-permute-start.21 = (bf16[32,2176]{1,0:T(8,128)(2,1)S(1)}, bf16[32,2176]{1,0:T(8,128)(2,1)S(1)}, u32[]{:S(2)}, u32[]{:S(2)}) collective-permute-start(bf16[32,2176]{1,0:T(8,128)(2,1)S(1)} %get-tuple-element.73), channel_id=1, source_target_pairs={{0,2},{1,3},{2,0},{3,1},{4,6},{5,7},{6,4},{7,5},{8,10},{9,11},{10,... | collective-permute-start | bytes 417800 | tf_op jit(solution)/shard_map/ppermute | solution.py:383
  56.5 7.1 %collective-permute-start.25 = (bf16[8,2176]{1,0:T(8,128)(2,1)S(1)}, bf16[8,2176]{1,0:T(8,128)(2,1)S(1)}, u32[]{:S(2)}, u32[]{:S(2)}) collective-permute-start(bf16[8,2176]{1,0:T(8,128)(2,1)S(1)} %get-tuple-element.79), channel_id=1, source_target_pairs={{0,12},{1,13},{2,14},{3,15},{4,8},{5,9},{6,10},{7,11},{8,4},{9,5},... | collective-permute-start | bytes 104456 | tf_op jit(solution)/shard_map/ppermute | solution.py:383
  58.5 7.1 %collective-permute-start.26 = (bf16[8,2176]{1,0:T(8,128)(2,1)S(1)}, bf16[8,2176]{1,0:T(8,128)(2,1)S(1)}, u32[]{:S(2)}, u32[]{:S(2)}) collective-permute-start(bf16[8,2176]{1,0:T(8,128)(2,1)S(1)} %get-tuple-element.80), channel_id=1, source_target_pairs={{0,8},{1,9},{2,10},{3,11},{4,12},{5,13},{6,14},{7,15},{8,0},{9,1},... | collective-permute-start | bytes 104456 | tf_op jit(solution)/shard_map/ppermute | solution.py:383
  59.3 6.3 %collective-permute-start.27 = (bf16[8,2176]{1,0:T(8,128)(2,1)S(1)}, bf16[8,2176]{1,0:T(8,128)(2,1)S(1)}, u32[]{:S(2)}, u32[]{:S(2)}) collective-permute-start(bf16[8,2176]{1,0:T(8,128)(2,1)S(1)} %get-tuple-element.81), channel_id=1, source_target_pairs={{0,4},{1,5},{2,6},{3,7},{4,0},{5,1},{6,2},{7,3},{8,12},{9,13},{10,... | collective-permute-start | bytes 104456 | tf_op jit(solution)/shard_map/ppermute | solution.py:383
  61.1 5.8 %collective-permute-start.22 = (bf16[8,2176]{1,0:T(8,128)(2,1)S(1)}, bf16[8,2176]{1,0:T(8,128)(2,1)S(1)}, u32[]{:S(2)}, u32[]{:S(2)}) collective-permute-start(bf16[8,2176]{1,0:T(8,128)(2,1)S(1)} %get-tuple-element.75), channel_id=1, source_target_pairs={{0,12},{1,13},{2,14},{3,15},{4,8},{5,9},{6,10},{7,11},{8,4},{9,5},... | collective-permute-start | bytes 104456 | tf_op jit(solution)/shard_map/ppermute | solution.py:383
  63.2 4.8 %collective-permute-start.23 = (bf16[8,2176]{1,0:T(8,128)(2,1)S(1)}, bf16[8,2176]{1,0:T(8,128)(2,1)S(1)}, u32[]{:S(2)}, u32[]{:S(2)}) collective-permute-start(bf16[8,2176]{1,0:T(8,128)(2,1)S(1)} %get-tuple-element.76), channel_id=1, source_target_pairs={{0,8},{1,9},{2,10},{3,11},{4,12},{5,13},{6,14},{7,15},{8,0},{9,1},... | collective-permute-start | bytes 104456 | tf_op jit(solution)/shard_map/ppermute | solution.py:383
  63.6 4.5 %collective-permute-start.24 = (bf16[8,2176]{1,0:T(8,128)(2,1)S(1)}, bf16[8,2176]{1,0:T(8,128)(2,1)S(1)}, u32[]{:S(2)}, u32[]{:S(2)}) collective-permute-start(bf16[8,2176]{1,0:T(8,128)(2,1)S(1)} %get-tuple-element.77), channel_id=1, source_target_pairs={{0,4},{1,5},{2,6},{3,7},{4,0},{5,1},{6,2},{7,3},{8,12},{9,13},{10,... | collective-permute-start | bytes 104456 | tf_op jit(solution)/shard_map/ppermute | solution.py:383

commit v7 on v4

--- a/solution.py
+++ b/solution.py
@@ -112,6 +112,20 @@
     return values * lax.rsqrt(jnp.mean(values * values, axis=-1, keepdims=True) + EPSILON) * gain[None, :]
 
 
+def early_body(gain_far, tokens_far, map_far, logits_far, gain, tokens, entries, vocab_map, semaphores):
+    count = logits_far.shape[0]
+    copies = fetch(
+        (map_far, logits_far, gain_far, tokens_far),
+        (vocab_map, entries.at[:count], gain, tokens),
+        semaphores,
+    )
+    copies[0].wait()
+    places = vocab_map[...].astype(F32)[None, :]
+    entries[count:, :] = jnp.broadcast_to(places, (16, places.shape[1])).astype(BF16)
+    for copy in copies[1:]:
+        copy.wait()
+
+
 def paired(out):
     return [slice(at, at + 16) for at in range(0, out.shape[0], 16)]
 
@@ -199,25 +213,22 @@
         target[...] = source[...]
 
 
-def student_body(devices, order, prefetched, me, their_map, their_logits, their_head, *refs):
-    (map_far, logits_far, head_far, *refs) = refs
+def student_body(devices, order, prefetched, me, ours, theirs, their_head, head_far, *refs):
     sources, (moved, moved_head, *refs) = refs[:prefetched], refs[prefetched:]
-    parts = refs[: len(refs) - prefetched - 5]
+    parts = refs[: len(refs) - prefetched - 3]
     refs = refs[len(parts) :]
-    targets, (own_map, logits, head, scratch, semaphores) = refs[:prefetched], refs[prefetched:]
-    copies = fetch(
-        (map_far, logits_far, head_far, *sources), (own_map, logits, head, *targets), semaphores
-    )
-    for copy in copies[:3]:
-        copy.wait()
+    targets, (head, scratch, semaphores) = refs[:prefetched], refs[prefetched:]
+    copies = fetch((head_far, *sources), (head, *targets), semaphores)
+    copies[0].wait()
+    count = scratch.shape[0]
     entries = head.shape[1]
-    tok_dev = logits.shape[0] // devices
-    own, other = (own_map, logits, head), (their_map, their_logits, their_head)
-    for i, (places, rows, weights) in enumerate((own, other)):
+    tok_dev = count // devices
+    for i, (rows, weights) in enumerate(((ours, head), (theirs, their_head))):
         cols = slice(i * entries, (i + 1) * entries)
-        place = lax.broadcasted_iota(jnp.int32, (entries, entries), 0) == places[...]
+        index = lax.broadcasted_iota(jnp.int32, (entries, entries), 0).astype(F32)
+        place = index == rows[count:, :].astype(F32)[:1, :]
         place = jnp.where(place, 1.0, 0.0).astype(BF16)
-        scratch[:, cols] = dot_t(rows[...], place)
+        scratch[:, cols] = dot_t(rows[:count, :], place)
         moved_head[:, cols] = dot_t(weights[...], place).astype(BF16)
     for slot, offset in enumerate(order):
         source = pl.multiple_of((me[0] ^ offset) * tok_dev, tok_dev)
@@ -230,7 +241,7 @@
     def _():
         student_part(moved, moved_head, parts, late(width), width)
 
-    for copy in copies[3:]:
+    for copy in copies[1:]:
         copy.wait()
 
 
@@ -390,22 +401,28 @@
     turn = list(range(size_z - 1, 0, -1))
     first_turn = [size_z - 1, *range(1, size_z - 1)]
     parts = along_z([tokens] * size_z, first_turn)
-    if near:
-        moe_gain, tokens = run(
-            fetch_body,
-            [(moe_gain.shape, F32), (tokens.shape, BF16)],
-            moe_gain,
-            tokens,
-            scratch=[pltpu.SemaphoreType.DMA((2,))],
-            far=2,
-            after=parts[:1],
-        )
-        parts[-1] = tokens
+    moe_gain, tokens, ours = run(
+        early_body,
+        [(moe_gain.shape, F32), (tokens.shape, BF16), ((all_rows + 16, entries), BF16)],
+        moe_gain,
+        tokens,
+        vocab_map,
+        student_logits,
+        scratch=[pltpu.VMEM((entries,), jnp.int32), pltpu.SemaphoreType.DMA((4,))],
+        far=4,
+        after=parts[:1],
+    )
+    parts[-1] = tokens
+    theirs = swap(ours, 1)
     (column_rows,) = run(
-        functools.partial(join_normed_body, places(first_turn)), [((quarter, features), BF16)], moe_gain, *parts)
+        functools.partial(join_normed_body, places(first_turn)),
+        [((quarter, features), BF16)],
+        moe_gain,
+        *parts,
+
+    )
     plane = along_x(column_rows)
-    own_map = vocab_map.reshape(1, -1)
-    theirs = [swap(a, 1) for a in (own_map, student_logits, student_head)]
+    their_head = swap(student_head, 1)
     their_teacher = swap(teacher_head, 1)
     prefetched = [w_gate, w_up, w_down, teacher_head, final_gain, expert_ids.T, gate_scores.T]
     fetched = prefetched if near else []
@@ -420,20 +437,18 @@
             *[(a.shape, a.dtype) for a in fetched],
         ],
         me,
-        *theirs,
-        own_map,
-        student_logits,
+        ours,
+        theirs,
+        their_head,
         student_head,
         *fetched,
         scratch=[
-            pltpu.VMEM((1, entries), jnp.int32),
-            pltpu.VMEM((all_rows, entries), BF16),
             pltpu.VMEM((width, entries), BF16),
             pltpu.VMEM((all_rows, 2 * entries), F32),
-            pltpu.SemaphoreType.DMA((3 + len(fetched),)),
+            pltpu.SemaphoreType.DMA((1 + len(fetched),)),
         ],
         scalars=1,
-        far=3 + len(fetched),
+        far=1 + len(fetched),
         cost=(4 * entries * width * (half + entries), 2 * sum(a.size for a in prefetched)),
         after=[column_rows],
     )

time: 69.7 us -> 69 us (0.990)
  waiting for transfers between devices: 29.9 us -> 28.7 us
    ppermute x27 -> x26, waiting for transfers between devices: 29.9 us -> 28.7 us  [swap(): lax.ppermute(values, 'expert', [(i, i ^ offset) for i in range(devices)])]
    ppermute x27 -> x26, starting transfers between devices: 29.7 us -> 30.3 us  [swap(): lax.ppermute(values, 'expert', [(i, i ^ offset) for i in range(devices)])]
  transfers between devices with their start and end apart: 27 -> 26, of which waited for: 14 -> 14; matrix products, arithmetic and copies ran while one was open for 0% -> 0% of each run, Pallas kernels for 10% -> 10%
where the time goes in v7:
time: 69 us; the launch traced here: 68.9 us
  starting transfers between devices  30.3 us (44%)
  waiting for transfers between devices  28.7 us (42%)
  Pallas kernels  9.1 us (13%)
  between operations  0.73 us (1%)
    ppermute x26, starting transfers between devices, swap(): lax.ppermute(values, 'expert', [(i, i ^ offset) for i in range(devices)])  30.3 us
    ppermute x26, waiting for transfers between devices, swap(): lax.ppermute(values, 'expert', [(i, i ^ offset) for i in range(devices)])  28.7 us
    pallas_call x12, Pallas kernels, call(): pl.pallas_call(run, out_shape=[kind(s, d) for s, d in outs], in_specs=[sm...  9.1 us
  transfers between devices with their start and end apart: 26, of which 14 were waited for; matrix products, arithmetic and copies ran while one was open for 0% of the time, Pallas kernels for 10%

profile of v7, /device:TPU:0, one launch (start us, length us, event | category | flops | bytes accessed | tf_op | source)
XLA Modules:
  0.0 68.9 jit_solution(13165863472215223367)
XLA Ops:
  0.6 0.5 collective-permute-start.2
  1.1 0.1 collective-permute-start.18
  1.2 5.0 %collective-permute-start = (bf16[8,3584]{1,0:T(8,128)(2,1)}, bf16[8,3584]{1,0:T(8,128)(2,1)S(1)}, u32[]{:S(2)}, u32[]{:S(2)}) collective-permute-start(bf16[8,3584]{1,0:T(8,128)(2,1)} %refs_1_.1), channel_id=1, source_target_pairs={{0,12},{1,13},{2,14},{3,15},{4,8},{5,9},{6,10},{7,11},{8,4},{9,5},... | collective-permute-start | bytes 172040 | tf_op jit(solution)/shard_map/ppermute | solution.py:377
  6.3 0.0 collective-permute-start.3
  6.3 0.6 collective-permute-start.4
  6.8 2.4 %collective-permute-done.refs_4_.refs_1_ = bf16[8,3584]{1,0:T(8,128)(2,1)S(1)} collective-permute-done((bf16[8,3584]{1,0:T(8,128)(2,1)}, bf16[8,3584]{1,0:T(8,128)(2,1)S(1)}, u32[]{:S(2)}, u32[]{:S(2)}) %collective-permute-start) | collective-permute-done | bytes 57376 | tf_op jit(solution)/shard_map/ppermute | solution.py:377
  9.2 0.9 %shard_map.131 = (f32[3584]{0:T(1024)S(1)}, bf16[8,3584]{1,0:T(8,128)(2,1)S(1)}, bf16[144,256]{1,0:T(8,128)(2,1)S(1)}) custom-call(f32[3584]{0:T(1024)} %refs_0_.1, bf16[8,3584]{1,0:T(8,128)(2,1)} %refs_1_.1, s32[256]{0:T(256)} %refs_2_.1, bf16[128,256]{1,0:T(8,128)(2,1)} %refs_3_.1, bf16[8,3584]{1,0:T(8,128)(2,1)S(1)} %collective-permute-done.refs_4_.refs_1_), custom_call_target="tpu_custom_call" | custom-call | tf_op jit(solution)/shard_map/pallas_call | solution.py:83
  10.1 0.9 %collective-permute-done.3.refs_2_ = bf16[8,3584]{1,0:T(8,128)(2,1)S(1)} collective-permute-done((bf16[8,3584]{1,0:T(8,128)(2,1)}, bf16[8,3584]{1,0:T(8,128)(2,1)S(1)}, u32[]{:S(2)}, u32[]{:S(2)}) %collective-permute-start.3) | collective-permute-done | bytes 57376 | tf_op jit(solution)/shard_map/ppermute | solution.py:377
  11.0 1.2 %collective-permute-done.4.refs_3_ = bf16[8,3584]{1,0:T(8,128)(2,1)S(1)} collective-permute-done((bf16[8,3584]{1,0:T(8,128)(2,1)}, bf16[8,3584]{1,0:T(8,128)(2,1)S(1)}, u32[]{:S(2)}, u32[]{:S(2)}) %collective-permute-start.4) | collective-permute-done | bytes 57376 | tf_op jit(solution)/shard_map/ppermute | solution.py:377
  12.2 0.2 shard_map.132.refs_12_.refs_0_
  12.3 1.6 %collective-permute-start.5 = (bf16[32,3584]{1,0:T(8,128)(2,1)S(1)}, bf16[32,3584]{1,0:T(8,128)(2,1)S(1)}, u32[]{:S(2)}, u32[]{:S(2)}) collective-permute-start(bf16[32,3584]{1,0:T(8,128)(2,1)S(1)} %shard_map.132.refs_12_.refs_0_), channel_id=1, source_target_pairs={{0,2},{1,3},{2,0},{3,1},{4,6},{5,7},{6,4},{7,5},{8,10},{9,11},{10,... | collective-permute-start | bytes 688136 | tf_op jit(solution)/shard_map/ppermute | solution.py:377
  13.9 0.0 collective-permute-start.1
  13.9 0.5 collective-permute-start.6
  14.4 0.8 %collective-permute-done.1.refs_2_ = bf16[144,256]{1,0:T(8,128)(2,1)S(1)} collective-permute-done((bf16[144,256]{1,0:T(8,128)(2,1)S(1)}, bf16[144,256]{1,0:T(8,128)(2,1)S(1)}, u32[]{:S(2)}, u32[]{:S(2)}) %collective-permute-start.1) | collective-permute-done | bytes 73760 | tf_op jit(solution)/shard_map/ppermute | solution.py:377
  15.2 0.0 collective-permute-done.2.refs_3_
  15.2 3.5 %shard_map.133 = (f32[64,512]{1,0:T(8,128)S(1)}, bf16[2048,512]{1,0:T(8,128)(2,1)S(1)}, f32[32,2176]{1,0:T(8,128)S(1)}, bf16[32,2176]{1,0:T(8,128)(2,1)S(1)}, bf...) custom-call(s32[1]{0:T(128)} %bitcast.refs_0_, ...), custom_call_target="tpu_custom_call" | custom-call | flops 671088640 | bytes 7347264 | tf_op jit(solution)/shard_map/pallas_call | solution.py:83
  18.7 0.0 collective-permute-done.5.refs_0_
  18.7 0.2 collective-permute-start.7
  19.0 0.0 collective-permute-done.6.refs_2_
  19.0 1.3 %collective-permute-done.7.refs_3_ = bf16[32,3584]{1,0:T(8,128)(2,1)S(1)} collective-permute-done((bf16[32,3584]{1,0:T(8,128)(2,1)S(1)}, bf16[32,3584]{1,0:T(8,128)(2,1)S(1)}, u32[]{:S(2)}, u32[]{:S(2)}) %collective-permute-start.7) | collective-permute-done | bytes 229408 | tf_op jit(solution)/shard_map/ppermute | solution.py:377
  20.3 1.0 %shard_map.135 = (f32[64,3584]{1,0:T(8,128)S(1)}, bf16[64,3584]{1,0:T(8,128)(2,1)S(1)}) custom-call(bf16[32,3584]{1,0:T(8,128)(2,1)S(1)} %shard_map.132.refs_12_.refs_0_, bf16[32,3584]{1,0:T(8,128)(2,1)S(1)} %shard_map.134.refs_1_, bf16[32,3584]{1,0:T(8,128)(2,1)S(1)} %collective-permute-done.6.refs_2_, bf16[32,3584]{1,0:T(8,128)(2,1)S(1)} %collective-permute-done.7.refs_3_, ...), custom_call_target="tpu_custom_call" | custom-call | tf_op jit(solution)/shard_map/pallas_call | solution.py:83
  21.3 0.2 collective-permute-start.8
  21.5 1.7 %collective-permute-done.8.refs_4_ = bf16[64,3584]{1,0:T(8,128)(2,1)S(1)} collective-permute-done((bf16[64,3584]{1,0:T(8,128)(2,1)S(1)}, bf16[64,3584]{1,0:T(8,128)(2,1)S(1)}, u32[]{:S(2)}, u32[]{:S(2)}) %collective-permute-start.8) | collective-permute-done | bytes 458784 | tf_op jit(solution)/shard_map/ppermute | solution.py:377
  23.2 0.6 shard_map.136
  23.8 1.3 %collective-permute-start.9 = (bf16[32,3584]{1,0:T(8,128)(2,1)S(1)}, bf16[32,3584]{1,0:T(8,128)(2,1)S(1)}, u32[]{:S(2)}, u32[]{:S(2)}) collective-permute-start(bf16[32,3584]{1,0:T(8,128)(2,1)S(1)} %get-tuple-element.57), channel_id=1, source_target_pairs={{0,2},{1,3},{2,0},{3,1},{4,6},{5,7},{6,4},{7,5},{8,10},{9,11},{10,... | collective-permute-start | bytes 688136 | tf_op jit(solution)/shard_map/ppermute | solution.py:377
  25.0 6.0 %collective-permute-done.9.refs_1_ = bf16[32,3584]{1,0:T(8,128)(2,1)S(1)} collective-permute-done((bf16[32,3584]{1,0:T(8,128)(2,1)S(1)}, bf16[32,3584]{1,0:T(8,128)(2,1)S(1)}, u32[]{:S(2)}, u32[]{:S(2)}) %collective-permute-start.9) | collective-permute-done | bytes 229408 | tf_op jit(solution)/shard_map/ppermute | solution.py:377
  31.0 0.1 shard_map.137
  31.1 2.3 %collective-permute-start.10 = (bf16[8,3584]{1,0:T(8,128)(2,1)S(1)}, bf16[8,3584]{1,0:T(8,128)(2,1)S(1)}, u32[]{:S(2)}, u32[]{:S(2)}) collective-permute-start(bf16[8,3584]{1,0:T(8,128)(2,1)S(1)} %get-tuple-element.59), channel_id=1, source_target_pairs={{0,12},{1,13},{2,14},{3,15},{4,8},{5,9},{6,10},{7,11},{8,4},{9,5},... | collective-permute-start | bytes 172040 | tf_op jit(solution)/shard_map/ppermute | solution.py:377
  33.4 0.7 collective-permute-start.11
  34.0 1.5 %collective-permute-start.12 = (bf16[8,3584]{1,0:T(8,128)(2,1)S(1)}, bf16[8,3584]{1,0:T(8,128)(2,1)S(1)}, u32[]{:S(2)}, u32[]{:S(2)}) collective-permute-start(bf16[8,3584]{1,0:T(8,128)(2,1)S(1)} %get-tuple-element.61), channel_id=1, source_target_pairs={{0,4},{1,5},{2,6},{3,7},{4,0},{5,1},{6,2},{7,3},{8,12},{9,13},{10,... | collective-permute-start | bytes 172040 | tf_op jit(solution)/shard_map/ppermute | solution.py:377
  35.5 2.2 %collective-permute-done.10.refs_2_ = bf16[8,3584]{1,0:T(8,128)(2,1)S(1)} collective-permute-done((bf16[8,3584]{1,0:T(8,128)(2,1)S(1)}, bf16[8,3584]{1,0:T(8,128)(2,1)S(1)}, u32[]{:S(2)}, u32[]{:S(2)}) %collective-permute-start.10) | collective-permute-done | bytes 57376 | tf_op jit(solution)/shard_map/ppermute | solution.py:377
  37.7 1.2 %collective-permute-done.11.refs_3_ = bf16[8,3584]{1,0:T(8,128)(2,1)S(1)} collective-permute-done((bf16[8,3584]{1,0:T(8,128)(2,1)S(1)}, bf16[8,3584]{1,0:T(8,128)(2,1)S(1)}, u32[]{:S(2)}, u32[]{:S(2)}) %collective-permute-start.11) | collective-permute-done | bytes 57376 | tf_op jit(solution)/shard_map/ppermute | solution.py:377
  39.0 0.0 collective-permute-done.12.refs_4_
  39.0 0.2 shard_map.138
  39.2 1.2 %collective-permute-start.16 = (bf16[32,2176]{1,0:T(8,128)(2,1)S(1)}, bf16[32,2176]{1,0:T(8,128)(2,1)S(1)}, u32[]{:S(2)}, u32[]{:S(2)}) collective-permute-start(bf16[32,2176]{1,0:T(8,128)(2,1)S(1)} %get-tuple-element.71), channel_id=1, source_target_pairs={{0,2},{1,3},{2,0},{3,1},{4,6},{5,7},{6,4},{7,5},{8,10},{9,11},{10,... | collective-permute-start | bytes 417800 | tf_op jit(solution)/shard_map/ppermute | solution.py:377
  40.5 2.2 %collective-permute-start.13 = (bf16[8,3584]{1,0:T(8,128)(2,1)S(1)}, bf16[8,3584]{1,0:T(8,128)(2,1)S(1)}, u32[]{:S(2)}, u32[]{:S(2)}) collective-permute-start(bf16[8,3584]{1,0:T(8,128)(2,1)S(1)} %get-tuple-element.66), channel_id=1, source_target_pairs={{0,12},{1,13},{2,14},{3,15},{4,8},{5,9},{6,10},{7,11},{8,4},{9,5},... | collective-permute-start | bytes 172040 | tf_op jit(solution)/shard_map/ppermute | solution.py:377
  42.7 0.0 collective-permute-start.14
  42.7 2.2 %collective-permute-start.15 = (bf16[8,3584]{1,0:T(8,128)(2,1)S(1)}, bf16[8,3584]{1,0:T(8,128)(2,1)S(1)}, u32[]{:S(2)}, u32[]{:S(2)}) collective-permute-start(bf16[8,3584]{1,0:T(8,128)(2,1)S(1)} %get-tuple-element.68), channel_id=1, source_target_pairs={{0,4},{1,5},{2,6},{3,7},{4,0},{5,1},{6,2},{7,3},{8,12},{9,13},{10,... | collective-permute-start | bytes 172040 | tf_op jit(solution)/shard_map/ppermute | solution.py:377
  44.9 2.1 %collective-permute-done.13.refs_0_ = bf16[8,3584]{1,0:T(8,128)(2,1)S(1)} collective-permute-done((bf16[8,3584]{1,0:T(8,128)(2,1)S(1)}, bf16[8,3584]{1,0:T(8,128)(2,1)S(1)}, u32[]{:S(2)}, u32[]{:S(2)}) %collective-permute-start.13) | collective-permute-done | bytes 57376 | tf_op jit(solution)/shard_map/ppermute | solution.py:377
  47.0 1.3 %collective-permute-done.14.refs_1_ = bf16[8,3584]{1,0:T(8,128)(2,1)S(1)} collective-permute-done((bf16[8,3584]{1,0:T(8,128)(2,1)S(1)}, bf16[8,3584]{1,0:T(8,128)(2,1)S(1)}, u32[]{:S(2)}, u32[]{:S(2)}) %collective-permute-start.14) | collective-permute-done | bytes 57376 | tf_op jit(solution)/shard_map/ppermute | solution.py:377
  48.3 0.0 collective-permute-done.15.refs_2_
  48.3 0.0 collective-permute-done.16.refs_5_
  48.3 0.2 shard_map.139
  48.4 0.7 %collective-permute-start.17 = (bf16[32,3584]{1,0:T(8,128)(2,1)S(1)}, bf16[32,3584]{1,0:T(8,128)(2,1)S(1)}, u32[]{:S(2)}, u32[]{:S(2)}) collective-permute-start(bf16[32,3584]{1,0:T(8,128)(2,1)S(1)} %get-tuple-element.72.refs_0_), channel_id=1, source_target_pairs={{0,2},{1,3},{2,0},{3,1},{4,6},{5,7},{6,4},{7,5},{8,10},{9,11},{10,... | collective-permute-start | bytes 688136 | tf_op jit(solution)/shard_map/ppermute | solution.py:377
  49.2 0.0 collective-permute-done.18.refs_3_
  49.2 5.4 %collective-permute-done.17.refs_1_ = bf16[32,3584]{1,0:T(8,128)(2,1)S(1)} collective-permute-done((bf16[32,3584]{1,0:T(8,128)(2,1)S(1)}, bf16[32,3584]{1,0:T(8,128)(2,1)S(1)}, u32[]{:S(2)}, u32[]{:S(2)}) %collective-permute-start.17) | collective-permute-done | bytes 229408 | tf_op jit(solution)/shard_map/ppermute | solution.py:377
  54.5 1.5 %shard_map.140 = (f32[32,2176]{1,0:T(8,128)S(1)}, bf16[32,2176]{1,0:T(8,128)(2,1)S(1)}) custom-call(bf16[32,3584]{1,0:T(8,128)(2,1)S(1)} %get-tuple-element.72.refs_0_, bf16[32,3584]{1,0:T(8,128)(2,1)S(1)} %collective-permute-done.17.refs_1_, bf16[3584,256]{1,0:T(8,128)(2,1)S(1)} %get-tuple-element.73.refs_2_, ...), custom_call_target="tpu_custom_call" | custom-call | tf_op jit(solution)/shard_map/pallas_call | solution.py:83
  56.0 0.7 %collective-permute-start.19 = (bf16[32,2176]{1,0:T(8,128)(2,1)S(1)}, bf16[32,2176]{1,0:T(8,128)(2,1)S(1)}, u32[]{:S(2)}, u32[]{:S(2)}) collective-permute-start(bf16[32,2176]{1,0:T(8,128)(2,1)S(1)} %get-tuple-element.75), channel_id=1, source_target_pairs={{0,2},{1,3},{2,0},{3,1},{4,6},{5,7},{6,4},{7,5},{8,10},{9,11},{10,... | collective-permute-start | bytes 417800 | tf_op jit(solution)/shard_map/ppermute | solution.py:377
  56.8 1.7 %collective-permute-start.23 = (bf16[8,2176]{1,0:T(8,128)(2,1)S(1)}, bf16[8,2176]{1,0:T(8,128)(2,1)S(1)}, u32[]{:S(2)}, u32[]{:S(2)}) collective-permute-start(bf16[8,2176]{1,0:T(8,128)(2,1)S(1)} %get-tuple-element.81), channel_id=1, source_target_pairs={{0,12},{1,13},{2,14},{3,15},{4,8},{5,9},{6,10},{7,11},{8,4},{9,5},... | collective-permute-start | bytes 104456 | tf_op jit(solution)/shard_map/ppermute | solution.py:377
  58.4 0.9 %collective-permute-start.24 = (bf16[8,2176]{1,0:T(8,128)(2,1)S(1)}, bf16[8,2176]{1,0:T(8,128)(2,1)S(1)}, u32[]{:S(2)}, u32[]{:S(2)}) collective-permute-start(bf16[8,2176]{1,0:T(8,128)(2,1)S(1)} %get-tuple-element.82), channel_id=1, source_target_pairs={{0,8},{1,9},{2,10},{3,11},{4,12},{5,13},{6,14},{7,15},{8,0},{9,1},... | collective-permute-start | bytes 104456 | tf_op jit(solution)/shard_map/ppermute | solution.py:377
  59.3 1.9 %collective-permute-start.25 = (bf16[8,2176]{1,0:T(8,128)(2,1)S(1)}, bf16[8,2176]{1,0:T(8,128)(2,1)S(1)}, u32[]{:S(2)}, u32[]{:S(2)}) collective-permute-start(bf16[8,2176]{1,0:T(8,128)(2,1)S(1)} %get-tuple-element.83), channel_id=1, source_target_pairs={{0,4},{1,5},{2,6},{3,7},{4,0},{5,1},{6,2},{7,3},{8,12},{9,13},{10,... | collective-permute-start | bytes 104456 | tf_op jit(solution)/shard_map/ppermute | solution.py:377
  61.2 0.0 collective-permute-done.19.refs_1_
  61.2 0.1 shard_map.141
  61.3 1.9 %collective-permute-start.20 = (bf16[8,2176]{1,0:T(8,128)(2,1)S(1)}, bf16[8,2176]{1,0:T(8,128)(2,1)S(1)}, u32[]{:S(2)}, u32[]{:S(2)}) collective-permute-start(bf16[8,2176]{1,0:T(8,128)(2,1)S(1)} %get-tuple-element.77), channel_id=1, source_target_pairs={{0,12},{1,13},{2,14},{3,15},{4,8},{5,9},{6,10},{7,11},{8,4},{9,5},... | collective-permute-start | bytes 104456 | tf_op jit(solution)/shard_map/ppermute | solution.py:377
  63.2 0.4 collective-permute-start.21
  63.6 0.0 collective-permute-done.23.refs_5_
  63.6 2.2 %collective-permute-start.22 = (bf16[8,2176]{1,0:T(8,128)(2,1)S(1)}, bf16[8,2176]{1,0:T(8,128)(2,1)S(1)}, u32[]{:S(2)}, u32[]{:S(2)}) collective-permute-start(bf16[8,2176]{1,0:T(8,128)(2,1)S(1)} %get-tuple-element.79), channel_id=1, source_target_pairs={{0,4},{1,5},{2,6},{3,7},{4,0},{5,1},{6,2},{7,3},{8,12},{9,13},{10,... | collective-permute-start | bytes 104456 | tf_op jit(solution)/shard_map/ppermute | solution.py:377
  65.8 0.0 collective-permute-done.24.refs_6_
  65.8 0.0 collective-permute-done.25.refs_7_
  65.8 1.3 %collective-permute-done.20.refs_1_ = bf16[8,2176]{1,0:T(8,128)(2,1)S(1)} collective-permute-done((bf16[8,2176]{1,0:T(8,128)(2,1)S(1)}, bf16[8,2176]{1,0:T(8,128)(2,1)S(1)}, u32[]{:S(2)}, u32[]{:S(2)}) %collective-permute-start.20) | collective-permute-done | bytes 34848 | tf_op jit(solution)/shard_map/ppermute | solution.py:377
  67.1 0.9 %collective-permute-done.21.refs_2_ = bf16[8,2176]{1,0:T(8,128)(2,1)S(1)} collective-permute-done((bf16[8,2176]{1,0:T(8,128)(2,1)S(1)}, bf16[8,2176]{1,0:T(8,128)(2,1)S(1)}, u32[]{:S(2)}, u32[]{:S(2)}) %collective-permute-start.21) | collective-permute-done | bytes 34848 | tf_op jit(solution)/shard_map/ppermute | solution.py:377
  68.1 0.0 collective-permute-done.22.refs_3_
  68.1 0.8 %shard_map.142 = (f32[1,8]{1,0:T(1,128)}, f32[8,2048]{1,0:T(8,128)}) custom-call(f32[8,2176]{1,0:T(8,128)S(1)} %get-tuple-element.76.refs_0_, bf16[8,2176]{1,0:T(8,128)(2,1)S(1)} %collective-permute-done.20.refs_1_, bf16[8,2176]{1,0:T(8,128)(2,1)S(1)} %collective-permute-done.21.refs_2_, bf16[8,2176]{1,0:T(8,128)(2,1)S(1)} %collective-permute-done.22.refs_3_, ...), custom_call_target="tpu_custom_call" | custom-call | tf_op jit(solution)/shard_map/pallas_call | solution.py:83
  (1 shorter events, 0.0 us)
Async XLA Ops:
  0.6 14.5 %collective-permute-start.2 = (bf16[2048,256]{1,0:T(8,128)(2,1)}, bf16[2048,256]{1,0:T(8,128)(2,1)S(1)}, u32[]{:S(2)}, u32[]{:S(2)}) collective-permute-start(bf16[2048,256]{1,0:T(8,128)(2,1)} %refs_4_.1), channel_id=1, source_target_pairs={{0,1},{1,0},{2,3},{3,2},{4,5},{5,4},{6,7},{7,6},{8,9},{9,8},{10,11... | collective-permute-start | bytes 3145736 | tf_op jit(solution)/shard_map/ppermute | solution.py:377
  1.1 48.0 %collective-permute-start.18 = (bf16[3584,256]{1,0:T(8,128)(2,1)}, bf16[3584,256]{1,0:T(8,128)(2,1)S(1)}, u32[]{:S(2)}, u32[]{:S(2)}) collective-permute-start(bf16[3584,256]{1,0:T(8,128)(2,1)} %refs_8_.1), channel_id=1, source_target_pairs={{0,1},{1,0},{2,3},{3,2},{4,5},{5,4},{6,7},{7,6},{8,9},{9,8},{10,11... | collective-permute-start | bytes 5505032 | tf_op jit(solution)/shard_map/ppermute | solution.py:377
  1.2 8.0 %collective-permute-start = (bf16[8,3584]{1,0:T(8,128)(2,1)}, bf16[8,3584]{1,0:T(8,128)(2,1)S(1)}, u32[]{:S(2)}, u32[]{:S(2)}) collective-permute-start(bf16[8,3584]{1,0:T(8,128)(2,1)} %refs_1_.1), channel_id=1, source_target_pairs={{0,12},{1,13},{2,14},{3,15},{4,8},{5,9},{6,10},{7,11},{8,4},{9,5},... | collective-permute-start | bytes 172040 | tf_op jit(solution)/shard_map/ppermute | solution.py:377
  6.3 4.7 %collective-permute-start.3 = (bf16[8,3584]{1,0:T(8,128)(2,1)}, bf16[8,3584]{1,0:T(8,128)(2,1)S(1)}, u32[]{:S(2)}, u32[]{:S(2)}) collective-permute-start(bf16[8,3584]{1,0:T(8,128)(2,1)} %refs_1_.1), channel_id=1, source_target_pairs={{0,4},{1,5},{2,6},{3,7},{4,0},{5,1},{6,2},{7,3},{8,12},{9,13},{10,... | collective-permute-start | bytes 172040 | tf_op jit(solution)/shard_map/ppermute | solution.py:377
  6.3 5.9 %collective-permute-start.4 = (bf16[8,3584]{1,0:T(8,128)(2,1)}, bf16[8,3584]{1,0:T(8,128)(2,1)S(1)}, u32[]{:S(2)}, u32[]{:S(2)}) collective-permute-start(bf16[8,3584]{1,0:T(8,128)(2,1)} %refs_1_.1), channel_id=1, source_target_pairs={{0,8},{1,9},{2,10},{3,11},{4,12},{5,13},{6,14},{7,15},{8,0},{9,1},... | collective-permute-start | bytes 172040 | tf_op jit(solution)/shard_map/ppermute | solution.py:377
  12.3 6.4 %collective-permute-start.5 = (bf16[32,3584]{1,0:T(8,128)(2,1)S(1)}, bf16[32,3584]{1,0:T(8,128)(2,1)S(1)}, u32[]{:S(2)}, u32[]{:S(2)}) collective-permute-start(bf16[32,3584]{1,0:T(8,128)(2,1)S(1)} %shard_map.132.refs_12_.refs_0_), channel_id=1, source_target_pairs={{0,2},{1,3},{2,0},{3,1},{4,6},{5,7},{6,4},{7,5},{8,10},{9,11},{10,... | collective-permute-start | bytes 688136 | tf_op jit(solution)/shard_map/ppermute | solution.py:377
  13.9 1.3 %collective-permute-start.1 = (bf16[144,256]{1,0:T(8,128)(2,1)S(1)}, bf16[144,256]{1,0:T(8,128)(2,1)S(1)}, u32[]{:S(2)}, u32[]{:S(2)}) collective-permute-start(bf16[144,256]{1,0:T(8,128)(2,1)S(1)} %get-tuple-element.44.refs_1_), channel_id=1, source_target_pairs={{0,1},{1,0},{2,3},{3,2},{4,5},{5,4},{6,7},{7,6},{8,9},{9,8},{10,11... | collective-permute-start | bytes 221192 | tf_op jit(solution)/shard_map/ppermute | solution.py:377
  13.9 5.1 %collective-permute-start.6 = (bf16[32,3584]{1,0:T(8,128)(2,1)S(1)}, bf16[32,3584]{1,0:T(8,128)(2,1)S(1)}, u32[]{:S(2)}, u32[]{:S(2)}) collective-permute-start(bf16[32,3584]{1,0:T(8,128)(2,1)S(1)} %shard_map.132.refs_12_.refs_0_), channel_id=1, source_target_pairs={{0,1},{1,0},{2,3},{3,2},{4,5},{5,4},{6,7},{7,6},{8,9},{9,8},{10,11... | collective-permute-start | bytes 688136 | tf_op jit(solution)/shard_map/ppermute | solution.py:377
  18.7 1.6 %collective-permute-start.7 = (bf16[32,3584]{1,0:T(8,128)(2,1)S(1)}, bf16[32,3584]{1,0:T(8,128)(2,1)S(1)}, u32[]{:S(2)}, u32[]{:S(2)}) collective-permute-start(bf16[32,3584]{1,0:T(8,128)(2,1)S(1)} %shard_map.134.refs_1_), channel_id=1, source_target_pairs={{0,1},{1,0},{2,3},{3,2},{4,5},{5,4},{6,7},{7,6},{8,9},{9,8},{10,11... | collective-permute-start | bytes 688136 | tf_op jit(solution)/shard_map/ppermute | solution.py:377
  21.3 1.9 %collective-permute-start.8 = (bf16[64,3584]{1,0:T(8,128)(2,1)S(1)}, bf16[64,3584]{1,0:T(8,128)(2,1)S(1)}, u32[]{:S(2)}, u32[]{:S(2)}) collective-permute-start(bf16[64,3584]{1,0:T(8,128)(2,1)S(1)} %get-tuple-element.53), channel_id=1, source_target_pairs={{0,1},{1,0},{2,3},{3,2},{4,5},{5,4},{6,7},{7,6},{8,9},{9,8},{10,11... | collective-permute-start | bytes 1376264 | tf_op jit(solution)/shard_map/ppermute | solution.py:377
  23.8 7.3 %collective-permute-start.9 = (bf16[32,3584]{1,0:T(8,128)(2,1)S(1)}, bf16[32,3584]{1,0:T(8,128)(2,1)S(1)}, u32[]{:S(2)}, u32[]{:S(2)}) collective-permute-start(bf16[32,3584]{1,0:T(8,128)(2,1)S(1)} %get-tuple-element.57), channel_id=1, source_target_pairs={{0,2},{1,3},{2,0},{3,1},{4,6},{5,7},{6,4},{7,5},{8,10},{9,11},{10,... | collective-permute-start | bytes 688136 | tf_op jit(solution)/shard_map/ppermute | solution.py:377
  31.1 6.6 %collective-permute-start.10 = (bf16[8,3584]{1,0:T(8,128)(2,1)S(1)}, bf16[8,3584]{1,0:T(8,128)(2,1)S(1)}, u32[]{:S(2)}, u32[]{:S(2)}) collective-permute-start(bf16[8,3584]{1,0:T(8,128)(2,1)S(1)} %get-tuple-element.59), channel_id=1, source_target_pairs={{0,12},{1,13},{2,14},{3,15},{4,8},{5,9},{6,10},{7,11},{8,4},{9,5},... | collective-permute-start | bytes 172040 | tf_op jit(solution)/shard_map/ppermute | solution.py:377
  33.4 5.6 %collective-permute-start.11 = (bf16[8,3584]{1,0:T(8,128)(2,1)S(1)}, bf16[8,3584]{1,0:T(8,128)(2,1)S(1)}, u32[]{:S(2)}, u32[]{:S(2)}) collective-permute-start(bf16[8,3584]{1,0:T(8,128)(2,1)S(1)} %get-tuple-element.60), channel_id=1, source_target_pairs={{0,8},{1,9},{2,10},{3,11},{4,12},{5,13},{6,14},{7,15},{8,0},{9,1},... | collective-permute-start | bytes 172040 | tf_op jit(solution)/shard_map/ppermute | solution.py:377
  34.0 5.0 %collective-permute-start.12 = (bf16[8,3584]{1,0:T(8,128)(2,1)S(1)}, bf16[8,3584]{1,0:T(8,128)(2,1)S(1)}, u32[]{:S(2)}, u32[]{:S(2)}) collective-permute-start(bf16[8,3584]{1,0:T(8,128)(2,1)S(1)} %get-tuple-element.61), channel_id=1, source_target_pairs={{0,4},{1,5},{2,6},{3,7},{4,0},{5,1},{6,2},{7,3},{8,12},{9,13},{10,... | collective-permute-start | bytes 172040 | tf_op jit(solution)/shard_map/ppermute | solution.py:377
  39.2 9.1 %collective-permute-start.16 = (bf16[32,2176]{1,0:T(8,128)(2,1)S(1)}, bf16[32,2176]{1,0:T(8,128)(2,1)S(1)}, u32[]{:S(2)}, u32[]{:S(2)}) collective-permute-start(bf16[32,2176]{1,0:T(8,128)(2,1)S(1)} %get-tuple-element.71), channel_id=1, source_target_pairs={{0,2},{1,3},{2,0},{3,1},{4,6},{5,7},{6,4},{7,5},{8,10},{9,11},{10,... | collective-permute-start | bytes 417800 | tf_op jit(solution)/shard_map/ppermute | solution.py:377
  40.5 6.5 %collective-permute-start.13 = (bf16[8,3584]{1,0:T(8,128)(2,1)S(1)}, bf16[8,3584]{1,0:T(8,128)(2,1)S(1)}, u32[]{:S(2)}, u32[]{:S(2)}) collective-permute-start(bf16[8,3584]{1,0:T(8,128)(2,1)S(1)} %get-tuple-element.66), channel_id=1, source_target_pairs={{0,12},{1,13},{2,14},{3,15},{4,8},{5,9},{6,10},{7,11},{8,4},{9,5},... | collective-permute-start | bytes 172040 | tf_op jit(solution)/shard_map/ppermute | solution.py:377
  42.7 5.6 %collective-permute-start.14 = (bf16[8,3584]{1,0:T(8,128)(2,1)S(1)}, bf16[8,3584]{1,0:T(8,128)(2,1)S(1)}, u32[]{:S(2)}, u32[]{:S(2)}) collective-permute-start(bf16[8,3584]{1,0:T(8,128)(2,1)S(1)} %get-tuple-element.67), channel_id=1, source_target_pairs={{0,8},{1,9},{2,10},{3,11},{4,12},{5,13},{6,14},{7,15},{8,0},{9,1},... | collective-permute-start | bytes 172040 | tf_op jit(solution)/shard_map/ppermute | solution.py:377
  42.7 5.6 %collective-permute-start.15 = (bf16[8,3584]{1,0:T(8,128)(2,1)S(1)}, bf16[8,3584]{1,0:T(8,128)(2,1)S(1)}, u32[]{:S(2)}, u32[]{:S(2)}) collective-permute-start(bf16[8,3584]{1,0:T(8,128)(2,1)S(1)} %get-tuple-element.68), channel_id=1, source_target_pairs={{0,4},{1,5},{2,6},{3,7},{4,0},{5,1},{6,2},{7,3},{8,12},{9,13},{10,... | collective-permute-start | bytes 172040 | tf_op jit(solution)/shard_map/ppermute | solution.py:377
  48.4 6.1 %collective-permute-start.17 = (bf16[32,3584]{1,0:T(8,128)(2,1)S(1)}, bf16[32,3584]{1,0:T(8,128)(2,1)S(1)}, u32[]{:S(2)}, u32[]{:S(2)}) collective-permute-start(bf16[32,3584]{1,0:T(8,128)(2,1)S(1)} %get-tuple-element.72.refs_0_), channel_id=1, source_target_pairs={{0,2},{1,3},{2,0},{3,1},{4,6},{5,7},{6,4},{7,5},{8,10},{9,11},{10,... | collective-permute-start | bytes 688136 | tf_op jit(solution)/shard_map/ppermute | solution.py:377
  56.0 5.1 %collective-permute-start.19 = (bf16[32,2176]{1,0:T(8,128)(2,1)S(1)}, bf16[32,2176]{1,0:T(8,128)(2,1)S(1)}, u32[]{:S(2)}, u32[]{:S(2)}) collective-permute-start(bf16[32,2176]{1,0:T(8,128)(2,1)S(1)} %get-tuple-element.75), channel_id=1, source_target_pairs={{0,2},{1,3},{2,0},{3,1},{4,6},{5,7},{6,4},{7,5},{8,10},{9,11},{10,... | collective-permute-start | bytes 417800 | tf_op jit(solution)/shard_map/ppermute | solution.py:377
  56.8 6.8 %collective-permute-start.23 = (bf16[8,2176]{1,0:T(8,128)(2,1)S(1)}, bf16[8,2176]{1,0:T(8,128)(2,1)S(1)}, u32[]{:S(2)}, u32[]{:S(2)}) collective-permute-start(bf16[8,2176]{1,0:T(8,128)(2,1)S(1)} %get-tuple-element.81), channel_id=1, source_target_pairs={{0,12},{1,13},{2,14},{3,15},{4,8},{5,9},{6,10},{7,11},{8,4},{9,5},... | collective-permute-start | bytes 104456 | tf_op jit(solution)/shard_map/ppermute | solution.py:377
  58.4 7.3 %collective-permute-start.24 = (bf16[8,2176]{1,0:T(8,128)(2,1)S(1)}, bf16[8,2176]{1,0:T(8,128)(2,1)S(1)}, u32[]{:S(2)}, u32[]{:S(2)}) collective-permute-start(bf16[8,2176]{1,0:T(8,128)(2,1)S(1)} %get-tuple-element.82), channel_id=1, source_target_pairs={{0,8},{1,9},{2,10},{3,11},{4,12},{5,13},{6,14},{7,15},{8,0},{9,1},... | collective-permute-start | bytes 104456 | tf_op jit(solution)/shard_map/ppermute | solution.py:377
  59.3 6.5 %collective-permute-start.25 = (bf16[8,2176]{1,0:T(8,128)(2,1)S(1)}, bf16[8,2176]{1,0:T(8,128)(2,1)S(1)}, u32[]{:S(2)}, u32[]{:S(2)}) collective-permute-start(bf16[8,2176]{1,0:T(8,128)(2,1)S(1)} %get-tuple-element.83), channel_id=1, source_target_pairs={{0,4},{1,5},{2,6},{3,7},{4,0},{5,1},{6,2},{7,3},{8,12},{9,13},{10,... | collective-permute-start | bytes 104456 | tf_op jit(solution)/shard_map/ppermute | solution.py:377
  61.3 5.8 %collective-permute-start.20 = (bf16[8,2176]{1,0:T(8,128)(2,1)S(1)}, bf16[8,2176]{1,0:T(8,128)(2,1)S(1)}, u32[]{:S(2)}, u32[]{:S(2)}) collective-permute-start(bf16[8,2176]{1,0:T(8,128)(2,1)S(1)} %get-tuple-element.77), channel_id=1, source_target_pairs={{0,12},{1,13},{2,14},{3,15},{4,8},{5,9},{6,10},{7,11},{8,4},{9,5},... | collective-permute-start | bytes 104456 | tf_op jit(solution)/shard_map/ppermute | solution.py:377
  63.2 4.9 %collective-permute-start.21 = (bf16[8,2176]{1,0:T(8,128)(2,1)S(1)}, bf16[8,2176]{1,0:T(8,128)(2,1)S(1)}, u32[]{:S(2)}, u32[]{:S(2)}) collective-permute-start(bf16[8,2176]{1,0:T(8,128)(2,1)S(1)} %get-tuple-element.78), channel_id=1, source_target_pairs={{0,8},{1,9},{2,10},{3,11},{4,12},{5,13},{6,14},{7,15},{8,0},{9,1},... | collective-permute-start | bytes 104456 | tf_op jit(solution)/shard_map/ppermute | solution.py:377
  63.6 4.5 %collective-permute-start.22 = (bf16[8,2176]{1,0:T(8,128)(2,1)S(1)}, bf16[8,2176]{1,0:T(8,128)(2,1)S(1)}, u32[]{:S(2)}, u32[]{:S(2)}) collective-permute-start(bf16[8,2176]{1,0:T(8,128)(2,1)S(1)} %get-tuple-element.79), channel_id=1, source_target_pairs={{0,4},{1,5},{2,6},{3,7},{4,0},{5,1},{6,2},{7,3},{8,12},{9,13},{10,... | collective-permute-start | bytes 104456 | tf_op jit(solution)/shard_map/ppermute | solution.py:377
